TPU v7x, 32 devices: a whole 2x2x4 slice. The times are simulated.
32 devices in a mesh: groups: 2 (over x), tensor: 16 (over z, y, core).
Axes of the slice: x: 2, y: 2, z: 4, core: 2. Of those that a mesh axis runs over, the one named last changes fastest.
Arguments:
- input_queries: bfloat16 [4096, 3072], P(('groups', 'tensor')), parts along dimension 0, may hold values from -110 to 110
- input_keys: bfloat16 [4096, 3072], P(('groups', 'tensor')), parts along dimension 0, may hold values from -4.5 to 4.5, as said below
- input_values: bfloat16 [4096, 3072], P(('groups', 'tensor')), parts along dimension 0, may hold values from -12 to 12
- output_matrix: bfloat16 [3072, 3072], P('tensor'), may hold values from -0.109375 to 0.109375
- adapter_down_weight: bfloat16 [3072, 64], replicated, may hold values from -0.109375 to 0.109375
- adapter_up_weight: bfloat16 [64, 3072], replicated, may hold values from -0.75 to 0.75
- upstream: bfloat16 [4096, 3072], P(('groups', 'tensor')), parts along dimension 0, may hold values from -6 to 6
- window_frame_reach: int32 [24], replicated, may hold values from 0 to 1, as said below
- window_row_reach: int32 [24], replicated, may hold values from 0 to 1, as said below
Outputs:
- projected_output: bfloat16 [4096, 3072], P(('groups', 'tensor')), parts along dimension 0
- grad_query: bfloat16 [4096, 3072], P(('groups', 'tensor')), parts along dimension 0
- grad_key: bfloat16 [4096, 3072], P(('groups', 'tensor')), parts along dimension 0
- grad_value: bfloat16 [4096, 3072], P(('groups', 'tensor')), parts along dimension 0
- grad_down: float32 [6144, 64], P('groups'), parts along dimension 0
- up_weight_gradient: float32 [128, 3072], P('groups'), parts along dimension 0
There are 2 independent parts, one for each index of `groups`. A program takes and returns all parts, laid end to end along the dimension named above; an argument that names none is the same for every part. Nothing has to cross between parts.
Inputs may be any that keep to these rules, and one draw needn't show every extreme that they name: `input_keys`: keys are standard normal draws cut at 4.5. `window_frame_reach`: some head has reach 0 and some head reach 1. `window_row_reach`: some head has reach 0 and some head reach 1.
All inputs are finite; a program needn't handle non-finite values.
Results may differ from a plain program's by a relative error of at most 0.015.
Values may be sent and summed in bfloat16 or wider, within the bound.
No kernel may reach another device: no remote copies, remote signals or barrier semaphores. Data moves between devices by JAX's collectives and lax.ppermute only.
A program may use at most 128 MiB of HBM per device.

v0:
```python
import jax
import jax.numpy as jnp
from jax import lax
from jax.sharding import PartitionSpec as P

ROWS = 8
CTILES = 4
BANDS = 2
RIM = 1
CRIM = 1
TCOLS = 16
KEYS = 540


adapter_scale = 0.5


def from_behind(block, axis, distance):
    devices = range(lax.axis_size(axis))
    route = [(i - distance, i) for i in devices if i - distance in devices]
    return lax.ppermute(block, axis, route)


def window_table(frame_idx, band_idx, col_idx, frames, window_frame_reach, window_row_reach):
    extent = ROWS + 2 * RIM
    span = TCOLS + 2 * CRIM
    shifts = jnp.arange(3, dtype=jnp.int32) - 1
    frame_ok = (frame_idx + shifts >= 0) & (frame_idx + shifts < frames)
    key_height = band_idx * ROWS - RIM + jnp.arange(extent, dtype=jnp.int32)
    height_ok = (key_height >= 0) & (key_height < BANDS * ROWS)
    query_height = band_idx * ROWS + jnp.arange(ROWS, dtype=jnp.int32)
    height_gap = jnp.abs(key_height[None, :] - query_height[:, None])
    key_column = col_idx * TCOLS - CRIM + jnp.arange(span, dtype=jnp.int32)
    column_ok = (key_column >= 0) & (key_column < CTILES * TCOLS)
    query_column = col_idx * TCOLS + jnp.arange(TCOLS, dtype=jnp.int32)
    column_gap = jnp.abs(key_column[None, :] - query_column[:, None])
    width_fit = (column_gap <= CRIM) & column_ok[None, :]
    time_fit = (jnp.abs(shifts)[None, :] <= window_frame_reach[:, None]) & frame_ok[None, :]
    height_fit = (height_gap[None] <= window_row_reach[:, None, None]) & height_ok[None, None, :]
    allowed = (
        time_fit[:, None, None, :, None, None]
        & height_fit[:, :, None, None, :, None]
        & width_fit[None, None, :, None, None, :]
    )
    return allowed.reshape(window_frame_reach.shape[0], ROWS * TCOLS, 3 * extent * span)


def split_heads(block, heads):
    return block.reshape(block.shape[0], heads, -1)


def tile_scores(query_heads, key_heads, allowed):
    scale = query_heads.shape[2] ** (-0.5)
    scores = (
        jnp.einsum("qhd,khd->hqk", query_heads, key_heads, preferred_element_type=jnp.float32)
        * scale
    )
    return jnp.where(allowed, scores, -1e30)


def attend_tile(query_tile, key_block, value_block, allowed):
    heads = allowed.shape[0]
    query_heads = split_heads(query_tile, heads)
    scores = tile_scores(query_heads, split_heads(key_block, heads), allowed)
    row_max = jnp.max(scores, axis=2, keepdims=True)
    weights = jnp.exp(scores - row_max)
    totals = jnp.sum(weights, axis=2)
    mixed = jnp.einsum(
        "hqk,khd->qhd",
        weights.astype(jnp.bfloat16),
        split_heads(value_block, heads),
        preferred_element_type=jnp.float32,
    )
    attention_result = (mixed / totals.T[:, :, None]).astype(jnp.bfloat16).reshape(query_tile.shape)
    return (attention_result, row_max[:, :, 0] + jnp.log(totals))


def attend_back(
    query_tile, key_block, value_block, allowed, attention_result, attention_gradient, log_total
):
    heads = allowed.shape[0]
    query_heads = split_heads(query_tile, heads)
    key_heads = split_heads(key_block, heads)
    value_heads = split_heads(value_block, heads)
    grad_heads = split_heads(attention_gradient, heads)
    attended_heads = split_heads(attention_result, heads)
    scale = query_heads.shape[2] ** (-0.5)
    scores = tile_scores(query_heads, key_heads, allowed)
    probs = jnp.exp(scores - log_total[:, :, None])
    value_terms = jnp.einsum(
        "hqk,qhd->khd", probs.astype(jnp.bfloat16), grad_heads, preferred_element_type=jnp.float32
    ).astype(jnp.bfloat16)
    grad_probs = jnp.einsum(
        "qhd,khd->hqk", grad_heads, value_heads, preferred_element_type=jnp.float32
    )
    inner = jnp.sum(grad_heads.astype(jnp.float32) * attended_heads.astype(jnp.float32), axis=2).T
    grad_scores = (probs * (grad_probs - inner[:, :, None])).astype(jnp.bfloat16)
    grad_query = (
        jnp.einsum("hqk,khd->qhd", grad_scores, key_heads, preferred_element_type=jnp.float32)
        * scale
    ).astype(jnp.bfloat16)
    key_terms = (
        jnp.einsum("hqk,qhd->khd", grad_scores, query_heads, preferred_element_type=jnp.float32)
        * scale
    ).astype(jnp.bfloat16)
    return (grad_query.reshape(query_tile.shape), key_terms, value_terms)


def on_device(
    input_queries,
    input_keys,
    input_values,
    output_matrix,
    adapter_down_weight,
    adapter_up_weight,
    upstream,
    window_frame_reach,
    window_row_reach,
):
    width = input_keys.shape[1]
    extent = ROWS + 2 * RIM
    span = TCOLS + 2 * CRIM
    per_frame = BANDS * CTILES
    devices = lax.axis_size("tensor")
    frames = devices // per_frame
    position = lax.axis_index("tensor")
    frame_idx = position % frames
    col_idx = position // frames % CTILES
    band_idx = position // (frames * CTILES)
    band_step = CTILES * frames
    allowed = window_table(
        frame_idx, band_idx, col_idx, frames, window_frame_reach, window_row_reach
    )
    key_tile = input_keys.reshape(ROWS, TCOLS, width)
    value_tile = input_values.reshape(ROWS, TCOLS, width)
    sideways = {}
    for offset, first_col in ((frames, TCOLS - CRIM), (-frames, 0)):
        sideways[offset] = from_behind(
            (
                key_tile[:, first_col : first_col + CRIM],
                value_tile[:, first_col : first_col + CRIM],
            ),
            "tensor",
            offset,
        )
    key_row = jnp.concatenate([sideways[frames][0], key_tile, sideways[-frames][0]], axis=1)
    value_row = jnp.concatenate([sideways[frames][1], value_tile, sideways[-frames][1]], axis=1)
    vertical = {}
    for offset, first_row in ((band_step, ROWS - RIM), (-band_step, 0)):
        vertical[offset] = from_behind(
            (key_row[first_row : first_row + RIM], value_row[first_row : first_row + RIM]),
            "tensor",
            offset,
        )
    key_ext = jnp.concatenate([vertical[band_step][0], key_row, vertical[-band_step][0]], axis=0)
    value_ext = jnp.concatenate(
        [vertical[band_step][1], value_row, vertical[-band_step][1]], axis=0
    )
    frame_keys = {}
    for offset in (1, -1):
        frame_keys[offset] = from_behind((key_ext, value_ext), "tensor", offset)
    key_block = jnp.stack([frame_keys[1][0], key_ext, frame_keys[-1][0]]).reshape(KEYS, width)
    value_block = jnp.stack([frame_keys[1][1], value_ext, frame_keys[-1][1]]).reshape(KEYS, width)
    attention_result, log_total = attend_tile(input_queries, key_block, value_block, allowed)
    reduced_rows = jnp.dot(
        attention_result, adapter_down_weight, preferred_element_type=jnp.float32
    ).astype(jnp.bfloat16)
    whole_weight = lax.all_gather(output_matrix, "tensor", axis=0, tiled=True)
    frozen_path_output = jnp.dot(attention_result, whole_weight, preferred_element_type=jnp.float32)
    projected_output = (
        frozen_path_output
        + adapter_scale
        * jnp.dot(reduced_rows, adapter_up_weight, preferred_element_type=jnp.float32)
    ).astype(jnp.bfloat16)
    reduced_gradient = (
        adapter_scale * jnp.dot(upstream, adapter_up_weight.T, preferred_element_type=jnp.float32)
    ).astype(jnp.bfloat16)
    sharded_up_weight = adapter_scale * jnp.dot(
        reduced_rows.T, upstream, preferred_element_type=jnp.float32
    )
    local_down = jnp.dot(attention_result.T, reduced_gradient, preferred_element_type=jnp.float32)
    grad_down, up_weight_gradient = lax.psum((local_down, sharded_up_weight), "tensor")
    frozen_path_gradient = jnp.dot(upstream, whole_weight.T, preferred_element_type=jnp.float32)
    attention_gradient = (
        frozen_path_gradient
        + jnp.dot(reduced_gradient, adapter_down_weight.T, preferred_element_type=jnp.float32)
    ).astype(jnp.bfloat16)
    grad_query, key_terms, value_terms = attend_back(
        input_queries,
        key_block,
        value_block,
        allowed,
        attention_result,
        attention_gradient,
        log_total,
    )
    key_terms = key_terms.reshape(3, extent, span, width)
    value_terms = value_terms.reshape(3, extent, span, width)
    returned = {}
    for offset, slot_idx in ((1, 0), (-1, 2)):
        returned[slot_idx] = from_behind(
            (key_terms[slot_idx], value_terms[slot_idx]), "tensor", -offset
        )
    key_full = (
        key_terms[1].astype(jnp.float32)
        + returned[0][0].astype(jnp.float32)
        + returned[2][0].astype(jnp.float32)
    )
    value_full = (
        value_terms[1].astype(jnp.float32)
        + returned[0][1].astype(jnp.float32)
        + returned[2][1].astype(jnp.float32)
    )
    for offset, first_row, target in ((-band_step, 0, ROWS), (band_step, RIM + ROWS, RIM)):
        got_keys, got_values = (
            from_behind(
                key_full[first_row : first_row + RIM].astype(jnp.bfloat16), "tensor", offset
            ).astype(jnp.float32),
            from_behind(
                value_full[first_row : first_row + RIM].astype(jnp.bfloat16), "tensor", offset
            ).astype(jnp.float32),
        )
        key_full = key_full.at[target : target + RIM].add(got_keys)
        value_full = value_full.at[target : target + RIM].add(got_values)
    key_core = key_full[RIM : RIM + ROWS]
    value_core = value_full[RIM : RIM + ROWS]
    for offset, first_col, target in ((-frames, 0, TCOLS), (frames, CRIM + TCOLS, CRIM)):
        got_keys, got_values = from_behind(
            (
                key_core[:, first_col : first_col + CRIM],
                value_core[:, first_col : first_col + CRIM],
            ),
            "tensor",
            offset,
        )
        key_core = key_core.at[:, target : target + CRIM].add(got_keys)
        value_core = value_core.at[:, target : target + CRIM].add(got_values)
    grad_key = key_core[:, CRIM : CRIM + TCOLS].reshape(input_queries.shape).astype(jnp.bfloat16)
    grad_value = (
        value_core[:, CRIM : CRIM + TCOLS].reshape(input_queries.shape).astype(jnp.bfloat16)
    )
    return (projected_output, grad_query, grad_key, grad_value, grad_down, up_weight_gradient)


def solution(mesh):
    placed = (
        P(("groups", "tensor"), None),
        P(("groups", "tensor"), None),
        P(("groups", "tensor"), None),
        P("tensor", None),
        P(),
        P(),
        P(("groups", "tensor"), None),
        P(),
        P(),
    )
    return jax.shard_map(
        on_device,
        mesh=mesh,
        in_specs=placed,
        out_specs=(
            P(("groups", "tensor"), None),
            P(("groups", "tensor"), None),
            P(("groups", "tensor"), None),
            P(("groups", "tensor"), None),
            P("groups", None),
            P("groups", None),
        ),
        check_vma=False,
    )
```

profile of v0, /device:TPU:0, one launch (start us, length us, event | category | flops | bytes accessed | tf_op | source)
XLA Modules:
  0.0 410.7 jit_solution(16443283099671239720)
XLA Ops:
  10.6 5.5 %collective-permute-start.6 = (bf16[8,1,3072]{2,1,0:T(2,128)(2,1)S(1)}, bf16[8,1,3072]{2,1,0:T(2,128)(2,1)S(1)}, u32[]{:S(2)}, u32[]{:S(2)}) collective-permute-start(bf16[8,1,3072]{2,1,0:T(2,128)(2,1)S(1)} %get-tuple-element.142), channel_id=1, source_target_pairs={{0,2},{1,3},{2,4},{3,5},{4,6},{5,7},{6,8},{7,9},{8,10},{9,11},{10,... | collective-permute-start | bytes 147464 | tf_op jit(solution)/shard_map/ppermute | solution.py:21
  18.7 5.4 %collective-permute-start = (bf16[8,1,3072]{2,1,0:T(2,128)(2,1)S(1)}, bf16[8,1,3072]{2,1,0:T(2,128)(2,1)S(1)}, u32[]{:S(2)}, u32[]{:S(2)}) collective-permute-start(bf16[8,1,3072]{2,1,0:T(2,128)(2,1)S(1)} %get-tuple-element.140), channel_id=1, source_target_pairs={{0,2},{1,3},{2,4},{3,5},{4,6},{5,7},{6,8},{7,9},{8,10},{9,11},{10,... | collective-permute-start | bytes 147464 | tf_op jit(solution)/shard_map/ppermute | solution.py:21
  28.3 5.5 %collective-permute-start.8 = (bf16[1,18,3072]{2,1,0:T(8,128)(2,1)S(1)}, bf16[1,18,3072]{2,1,0:T(8,128)(2,1)S(1)}, u32[]{:S(2)}, u32[]{:S(2)}) collective-permute-start(bf16[1,18,3072]{2,1,0:T(8,128)(2,1)S(1)} %get-tuple-element.138), channel_id=1, source_target_pairs={{0,8},{1,9},{2,10},{3,11},{4,12},{5,13},{6,14},{7,15},{16,24},{17,... | collective-permute-start | bytes 331784 | tf_op jit(solution)/shard_map/ppermute | solution.py:21
  35.9 6.7 %collective-permute-start.2 = (bf16[1,18,3072]{2,1,0:T(8,128)(2,1)}, bf16[1,18,3072]{2,1,0:T(8,128)(2,1)}, u32[]{:S(2)}, u32[]{:S(2)}) collective-permute-start(bf16[1,18,3072]{2,1,0:T(8,128)(2,1)} %get-tuple-element.136), channel_id=1, source_target_pairs={{0,8},{1,9},{2,10},{3,11},{4,12},{5,13},{6,14},{7,15},{16,24},{17,... | collective-permute-start | bytes 331784 | tf_op jit(solution)/shard_map/ppermute | solution.py:21
  44.4 2.2 fusion.45
  47.8 4.2 %collective-permute-start.10 = (bf16[10,18,3072]{2,1,0:T(8,128)(2,1)}, bf16[10,18,3072]{2,1,0:T(8,128)(2,1)}, u32[]{:S(2)}, u32[]{:S(2)}) collective-permute-start(bf16[10,18,3072]{2,1,0:T(8,128)(2,1)} %get-tuple-element.135), channel_id=1, source_target_pairs={{0,1},{1,2},{2,3},{3,4},{4,5},{5,6},{6,7},{7,8},{8,9},{9,10},{10,1... | collective-permute-start | bytes 3317768 | tf_op jit(solution)/shard_map/ppermute | solution.py:21
  52.0 5.5 %and.149 = pred[24,8,16,3,10,18]{2,1,0,5,4,3:T(8,128)(4,1)} broadcast(pred[24,8,3,10]{1,0,3,2:T(8,128)(4,1)S(1)} %broadcast_and_fusion), dimensions={0,1,3,4} | broadcast | bytes 1664640 | tf_op jit(solution)/shard_map/and | solution.py:41
  57.6 25.2 %and.150 = pred[24,128,540]{1,0,2:T(8,128)(4,1)S(1)} reshape(pred[24,8,16,3,10,18]{2,1,0,5,4,3:T(8,128)(4,1)} %and.149) | data formatting | bytes 3317760 | tf_op jit(solution)/shard_map/and | solution.py:41
  82.8 3.6 fusion.46
  87.7 5.3 %collective-permute-start.4 = (bf16[10,18,3072]{2,1,0:T(8,128)(2,1)}, bf16[10,18,3072]{2,1,0:T(8,128)(2,1)}, u32[]{:S(2)}, u32[]{:S(2)}) collective-permute-start(bf16[10,18,3072]{2,1,0:T(8,128)(2,1)} %get-tuple-element.133), channel_id=1, source_target_pairs={{0,1},{1,2},{2,3},{3,4},{4,5},{5,6},{6,7},{7,8},{8,9},{9,10},{10,1... | collective-permute-start | bytes 3317768 | tf_op jit(solution)/shard_map/ppermute | solution.py:21
  94.0 1.9 and.157
  97.4 4.0 pad_maximum_fusion.1
  101.3 6.4 %reshape_reshape.9 = bf16[540,24,128]{2,1,0:T(8,128)(2,1)} reshape(bf16[3,10,18,3072]{3,2,1,0:T(8,128)(2,1)} %pad_maximum_fusion.1) | data formatting | bytes 6635520 | tf_op jit(solution)/shard_map/reshape;reshape | solution.py:49
  107.7 4.0 pad_maximum_fusion
  111.7 6.4 %reshape_reshape.8 = bf16[540,24,128]{2,1,0:T(8,128)(2,1)} reshape(bf16[3,10,18,3072]{3,2,1,0:T(8,128)(2,1)} %pad_maximum_fusion) | data formatting | bytes 6635520 | tf_op jit(solution)/shard_map/reshape;reshape | solution.py:49
  118.1 3.1 fusion.23
  121.2 5.1 %fusion.47 = f32[24,128]{1,0:T(8,128)S(1)} fusion(f32[24,540,128]{2,1,0:T(8,128)S(1)} %fusion.23, pred[24,128,540]{1,0,2:T(8,128)(4,1)S(1)} %and.150, pred[128,540]{0,1:T(8,128)(4,1)S(1)} %and.157), kind=kLoop, calls=%fused_computation.96 | loop fusion | flops 6632448 | bytes 8375808 | tf_op jit(solution)/shard_map/reduce_max | solution.py:65
  126.3 12.0 %fusion.3 = (f32[24,128]{1,0:T(8,128)S(1)}, bf16[24,128,540]{1,0,2:T(8,128)(2,1)}) fusion(f32[24,128]{1,0:T(8,128)S(1)} %fusion.47, f32[24,540,128]{2,1,0:T(8,128)S(1)} %fusion.23, pred[24,128,540]{1,0,2:T(8,128)(4,1)S(1)} %and.150, pred[128,540]{0,1:T(8,128)(4,1)S(1)} %and.157), kind=kLoop, calls=%fused_computation.10 | loop fusion | flops 9950208 | bytes 11705856 | tf_op jit(solution)/shard_map/reduce_sum | solution.py:67
  138.4 34.8 %all-gather.2.cloned.1.call-done = bf16[3072,3072]{1,0:T(8,128)(2,1)} async-done(((bf16[192,3072]{1,0:T(8,128)(2,1)}), bf16[3072,3072]{1,0:T(8,128)(2,1)}) %all-gather.2.cloned.1.call-update) | async-done | bytes 18874384 | tf_op jit(solution)/shard_map/all_gather | solution.py:168
  173.2 13.9 %fusion.53 = f32[128,3072]{1,0:T(8,128)} fusion(bf16[128,3072]{1,0:T(8,128)(2,1)S(1)} %copy-done.10, bf16[3072,3072]{1,0:T(8,128)(2,1)} %all-gather.2.cloned.1.call-done), kind=kOutput, calls=%fused_computation.102 | convolution fusion | flops 2415919104 | bytes 21233664 | tf_op jit(solution)/shard_map/dot_general | solution.py:183
  187.1 2.8 fusion.8
  191.5 3.3 fusion.19
  195.7 2.2 multiply_reduce_fusion
  197.9 17.1 %fusion.5 = (bf16[24,128,540]{1,0,2:T(8,128)(2,1)}, bf16[24,128,540]{1,0,2:T(8,128)(2,1)S(1)}) fusion(f32[24,128]{1,0:T(8,128)S(1)} %log_add_fusion, f32[24,540,128]{2,1,0:T(8,128)S(1)} %bitcast.79, pred[24,128,540]{1,0,2:T(8,128)(4,1)S(1)} %and.150, pred[128,540]{0,1:T(8,128)(4,1)S(1)} %and.157, f32[24,128]{1,0:T(8,128)S(1)} %bitcast.97, ...), kind=kLoop, calls=%fused_computation.12 | loop fusion | flops 13271040 | bytes 21659136 | tf_op jit(solution)/shard_map/convert_element_type | solution.py:91
  215.0 2.0 multiply_convert_fusion
  217.0 3.9 fusion.15
  223.6 7.2 %fusion.13 = bf16[540,24,128]{2,1,0:T(8,128)(2,1)S(1)} fusion(f32[24,540,128]{2,1,0:T(8,128)} %fusion.15), kind=kLoop, calls=%fused_computation.25 | loop fusion | flops 3317760 | bytes 9953280 | tf_op jit(solution)/shard_map/convert_element_type | solution.py:105
  232.6 2.5 squeeze.15
  235.1 35.7 %collective-permute-start.13 = (bf16[10,18,3072]{2,1,0:T(8,128)(2,1)}, bf16[10,18,3072]{2,1,0:T(8,128)(2,1)}, u32[]{:S(2)}, u32[]{:S(2)}) collective-permute-start(bf16[10,18,3072]{2,1,0:T(8,128)(2,1)} %squeeze.15), channel_id=1, source_target_pairs={{0,1},{1,2},{2,3},{3,4},{4,5},{5,6},{6,7},{7,8},{8,9},{9,10},{10,1... | collective-permute-start | bytes 3317768 | tf_op jit(solution)/shard_map/ppermute | solution.py:21
  272.6 2.5 squeeze.14
  276.5 3.0 fusion.9
  282.6 2.5 squeeze.17
  285.1 5.0 %collective-permute-start.19 = (bf16[10,18,3072]{2,1,0:T(8,128)(2,1)}, bf16[10,18,3072]{2,1,0:T(8,128)(2,1)}, u32[]{:S(2)}, u32[]{:S(2)}) collective-permute-start(bf16[10,18,3072]{2,1,0:T(8,128)(2,1)} %squeeze.17), channel_id=1, source_target_pairs={{0,1},{1,2},{2,3},{3,4},{4,5},{5,6},{6,7},{7,8},{8,9},{9,10},{10,1... | collective-permute-start | bytes 3317768 | tf_op jit(solution)/shard_map/ppermute | solution.py:21
  296.2 8.0 %fusion.52 = f32[128,3072]{1,0:T(8,128)S(1)} fusion(bf16[128,3072]{0,1:T(8,128)(2,1)S(1)} %bitcast.83, bf16[3072,3072]{1,0:T(8,128)(2,1)} %all-gather.2.cloned.1.call-done), kind=kOutput, calls=%fused_computation.101 | convolution fusion | flops 2415919104 | bytes 21233664 | tf_op jit(solution)/shard_map/dot_general | solution.py:169
  305.5 2.6 convert_add_fusion.1
  309.5 2.4 convert_add_fusion
  313.3 5.5 %collective-permute-done.14 = bf16[1,18,3072]{2,1,0:T(8,128)(2,1)S(1)} collective-permute-done((bf16[1,18,3072]{2,1,0:T(8,128)(2,1)S(1)}, bf16[1,18,3072]{2,1,0:T(8,128)(2,1)S(1)}, u32[]{:S(2)}, u32[]{:S(2)}) %collective-permute-start.14) | collective-permute-done | bytes 110624 | tf_op jit(solution)/shard_map/ppermute | solution.py:21
  320.3 2.5 collective-permute-done.20
  325.7 2.7 collective-permute-done.21
  332.2 14.9 %collective-permute-done.16 = f32[8,1,3072]{2,1,0:T(1,128)S(1)} collective-permute-done((f32[8,1,3072]{2,1,0:T(1,128)S(1)}, f32[8,1,3072]{2,1,0:T(1,128)S(1)}, u32[]{:S(2)}, u32[]{:S(2)}) %collective-permute-start.16) | collective-permute-done | bytes 98336 | tf_op jit(solution)/shard_map/ppermute | solution.py:21
  347.2 3.0 scatter-add.30
  351.5 5.1 %collective-permute-start.17 = (f32[8,1,3072]{2,1,0:T(1,128)S(1)}, f32[8,1,3072]{2,1,0:T(1,128)S(1)}, u32[]{:S(2)}, u32[]{:S(2)}) collective-permute-start(f32[8,1,3072]{2,1,0:T(1,128)S(1)} %slice.335), channel_id=1, source_target_pairs={{0,2},{1,3},{2,4},{3,5},{4,6},{5,7},{6,8},{7,9},{8,10},{9,11},{10,... | collective-permute-start | bytes 294920 | tf_op jit(solution)/shard_map/ppermute | solution.py:21
  358.7 6.0 %collective-permute-start.23 = (f32[8,1,3072]{2,1,0:T(1,128)S(1)}, f32[8,1,3072]{2,1,0:T(1,128)S(1)}, u32[]{:S(2)}, u32[]{:S(2)}) collective-permute-start(f32[8,1,3072]{2,1,0:T(1,128)S(1)} %slice.348), channel_id=1, source_target_pairs={{0,2},{1,3},{2,4},{3,5},{4,6},{5,7},{6,8},{7,9},{8,10},{9,11},{10,... | collective-permute-start | bytes 294920 | tf_op jit(solution)/shard_map/ppermute | solution.py:21
  365.9 3.0 scatter-add.31
  368.9 2.8 slice.375
  373.6 25.9 %all-reduce.3.cloned.1.call-done = (f32[3072,64]{0,1:T(8,128)}, f32[64,3072]{1,0:T(8,128)}) async-done(((f32[3072,64]{0,1:T(8,128)}, f32[64,3072]{1,0:T(8,128)}), (f32[3072,64]{0,1:T(8,128)}, f32[64,3072]{1,0:T(8,128)})) %all-reduce.3.cloned.1.call-update) | async-done | bytes 1572880 | tf_op jit(solution)/shard_map/psum | solution.py:182
  399.6 2.1 copy.132
  401.6 2.1 copy.133
  (134 shorter events, 56.9 us)
Async XLA Ops:
  7.2 110.9 %copy-start = (bf16[128,3072]{1,0:T(8,128)(2,1)S(1)}, bf16[128,3072]{1,0:T(8,128)(2,1)}, u32[]{:S(2)}) copy-start(bf16[128,3072]{1,0:T(8,128)(2,1)} %param.25) | copy-start | bytes 2359300
  7.2 37.2 %copy-start.14 = (bf16[128,3072]{1,0:T(8,128)(2,1)S(1)}, bf16[128,3072]{1,0:T(8,128)(2,1)}, u32[]{:S(2)}) copy-start(bf16[128,3072]{1,0:T(8,128)(2,1)} %param.26) | copy-start | bytes 2359300
  7.2 26.6 %copy-start.15 = (bf16[128,3072]{1,0:T(8,128)(2,1)S(1)}, bf16[128,3072]{1,0:T(8,128)(2,1)}, u32[]{:S(2)}) copy-start(bf16[128,3072]{1,0:T(8,128)(2,1)} %param.27) | copy-start | bytes 2359300
  7.2 165.9 %all-gather.2.cloned.1.call-start = ((), (), s32[]{:S(2)}) async-start(), calls=%async_computation | async-start | bytes 20054016 | tf_op jit(solution)/shard_map/all_gather | solution.py:168
  7.9 391.6 %all-reduce.3.cloned.1.call-start = ((), (), s32[]{:S(2)}) async-start(), calls=%async_computation.1 | async-start | bytes 3145728 | tf_op jit(solution)/shard_map/psum | solution.py:182
  9.3 16.6 %collective-permute-start.7 = (bf16[8,1,3072]{2,1,0:T(2,128)(2,1)S(1)}, bf16[8,1,3072]{2,1,0:T(2,128)(2,1)S(1)}, u32[]{:S(2)}, u32[]{:S(2)}) collective-permute-start(bf16[8,1,3072]{2,1,0:T(2,128)(2,1)S(1)} %get-tuple-element.143), channel_id=1, source_target_pairs={{2,0},{3,1},{4,2},{5,3},{6,4},{7,5},{8,6},{9,7},{10,8},{11,9},{12,... | collective-permute-start | bytes 147464 | tf_op jit(solution)/shard_map/ppermute | solution.py:21
  10.6 15.3 %collective-permute-start.6 = (bf16[8,1,3072]{2,1,0:T(2,128)(2,1)S(1)}, bf16[8,1,3072]{2,1,0:T(2,128)(2,1)S(1)}, u32[]{:S(2)}, u32[]{:S(2)}) collective-permute-start(bf16[8,1,3072]{2,1,0:T(2,128)(2,1)S(1)} %get-tuple-element.142), channel_id=1, source_target_pairs={{0,2},{1,3},{2,4},{3,5},{4,6},{5,7},{6,8},{7,9},{8,10},{9,11},{10,... | collective-permute-start | bytes 147464 | tf_op jit(solution)/shard_map/ppermute | solution.py:21
  17.4 16.4 %collective-permute-start.1 = (bf16[8,1,3072]{2,1,0:T(2,128)(2,1)S(1)}, bf16[8,1,3072]{2,1,0:T(2,128)(2,1)S(1)}, u32[]{:S(2)}, u32[]{:S(2)}) collective-permute-start(bf16[8,1,3072]{2,1,0:T(2,128)(2,1)S(1)} %get-tuple-element.141), channel_id=1, source_target_pairs={{2,0},{3,1},{4,2},{5,3},{6,4},{7,5},{8,6},{9,7},{10,8},{11,9},{12,... | collective-permute-start | bytes 147464 | tf_op jit(solution)/shard_map/ppermute | solution.py:21
  18.7 15.1 %collective-permute-start = (bf16[8,1,3072]{2,1,0:T(2,128)(2,1)S(1)}, bf16[8,1,3072]{2,1,0:T(2,128)(2,1)S(1)}, u32[]{:S(2)}, u32[]{:S(2)}) collective-permute-start(bf16[8,1,3072]{2,1,0:T(2,128)(2,1)S(1)} %get-tuple-element.140), channel_id=1, source_target_pairs={{0,2},{1,3},{2,4},{3,5},{4,6},{5,7},{6,8},{7,9},{8,10},{9,11},{10,... | collective-permute-start | bytes 147464 | tf_op jit(solution)/shard_map/ppermute | solution.py:21
  27.0 17.4 %collective-permute-start.9 = (bf16[1,18,3072]{2,1,0:T(8,128)(2,1)S(1)}, bf16[1,18,3072]{2,1,0:T(8,128)(2,1)S(1)}, u32[]{:S(2)}, u32[]{:S(2)}) collective-permute-start(bf16[1,18,3072]{2,1,0:T(8,128)(2,1)S(1)} %get-tuple-element.139), channel_id=1, source_target_pairs={{8,0},{9,1},{10,2},{11,3},{12,4},{13,5},{14,6},{15,7},{24,16},{25,... | collective-permute-start | bytes 331784 | tf_op jit(solution)/shard_map/ppermute | solution.py:21
  28.3 16.1 %collective-permute-start.8 = (bf16[1,18,3072]{2,1,0:T(8,128)(2,1)S(1)}, bf16[1,18,3072]{2,1,0:T(8,128)(2,1)S(1)}, u32[]{:S(2)}, u32[]{:S(2)}) collective-permute-start(bf16[1,18,3072]{2,1,0:T(8,128)(2,1)S(1)} %get-tuple-element.138), channel_id=1, source_target_pairs={{0,8},{1,9},{2,10},{3,11},{4,12},{5,13},{6,14},{7,15},{16,24},{17,... | collective-permute-start | bytes 331784 | tf_op jit(solution)/shard_map/ppermute | solution.py:21
  34.6 48.2 %collective-permute-start.3 = (bf16[1,18,3072]{2,1,0:T(8,128)(2,1)}, bf16[1,18,3072]{2,1,0:T(8,128)(2,1)}, u32[]{:S(2)}, u32[]{:S(2)}) collective-permute-start(bf16[1,18,3072]{2,1,0:T(8,128)(2,1)} %get-tuple-element.137), channel_id=1, source_target_pairs={{8,0},{9,1},{10,2},{11,3},{12,4},{13,5},{14,6},{15,7},{24,16},{25,... | collective-permute-start | bytes 331784 | tf_op jit(solution)/shard_map/ppermute | solution.py:21
  35.9 46.9 %collective-permute-start.2 = (bf16[1,18,3072]{2,1,0:T(8,128)(2,1)}, bf16[1,18,3072]{2,1,0:T(8,128)(2,1)}, u32[]{:S(2)}, u32[]{:S(2)}) collective-permute-start(bf16[1,18,3072]{2,1,0:T(8,128)(2,1)} %get-tuple-element.136), channel_id=1, source_target_pairs={{0,8},{1,9},{2,10},{3,11},{4,12},{5,13},{6,14},{7,15},{16,24},{17,... | collective-permute-start | bytes 331784 | tf_op jit(solution)/shard_map/ppermute | solution.py:21
  46.5 50.8 %collective-permute-start.11 = (bf16[10,18,3072]{2,1,0:T(8,128)(2,1)}, bf16[10,18,3072]{2,1,0:T(8,128)(2,1)}, u32[]{:S(2)}, u32[]{:S(2)}) collective-permute-start(bf16[10,18,3072]{2,1,0:T(8,128)(2,1)} %get-tuple-element.135), channel_id=1, source_target_pairs={{1,0},{2,1},{3,2},{4,3},{5,4},{6,5},{7,6},{8,7},{9,8},{10,9},{11,1... | collective-permute-start | bytes 3317768 | tf_op jit(solution)/shard_map/ppermute | solution.py:21
  47.8 49.6 %collective-permute-start.10 = (bf16[10,18,3072]{2,1,0:T(8,128)(2,1)}, bf16[10,18,3072]{2,1,0:T(8,128)(2,1)}, u32[]{:S(2)}, u32[]{:S(2)}) collective-permute-start(bf16[10,18,3072]{2,1,0:T(8,128)(2,1)} %get-tuple-element.135), channel_id=1, source_target_pairs={{0,1},{1,2},{2,3},{3,4},{4,5},{5,6},{6,7},{7,8},{8,9},{9,10},{10,1... | collective-permute-start | bytes 3317768 | tf_op jit(solution)/shard_map/ppermute | solution.py:21
  82.8 13.1 %copy-start.10 = (bf16[128,3072]{1,0:T(8,128)(2,1)S(1)}, bf16[128,3072]{1,0:T(8,128)(2,1)}, u32[]{:S(2)}) copy-start(bf16[128,3072]{1,0:T(8,128)(2,1)} %param.31) | copy-start | bytes 2359300
  86.4 21.3 %collective-permute-start.5 = (bf16[10,18,3072]{2,1,0:T(8,128)(2,1)}, bf16[10,18,3072]{2,1,0:T(8,128)(2,1)}, u32[]{:S(2)}, u32[]{:S(2)}) collective-permute-start(bf16[10,18,3072]{2,1,0:T(8,128)(2,1)} %get-tuple-element.133), channel_id=1, source_target_pairs={{1,0},{2,1},{3,2},{4,3},{5,4},{6,5},{7,6},{8,7},{9,8},{10,9},{11,1... | collective-permute-start | bytes 3317768 | tf_op jit(solution)/shard_map/ppermute | solution.py:21
  87.7 20.0 %collective-permute-start.4 = (bf16[10,18,3072]{2,1,0:T(8,128)(2,1)}, bf16[10,18,3072]{2,1,0:T(8,128)(2,1)}, u32[]{:S(2)}, u32[]{:S(2)}) collective-permute-start(bf16[10,18,3072]{2,1,0:T(8,128)(2,1)} %get-tuple-element.133), channel_id=1, source_target_pairs={{0,1},{1,2},{2,3},{3,4},{4,5},{5,6},{6,7},{7,8},{8,9},{9,10},{10,1... | collective-permute-start | bytes 3317768 | tf_op jit(solution)/shard_map/ppermute | solution.py:21
  121.2 5.1 %copy-start.2 = (f32[24,540,128]{2,1,0:T(8,128)}, f32[24,540,128]{2,1,0:T(8,128)S(1)}, u32[]{:S(2)}) copy-start(f32[24,540,128]{2,1,0:T(8,128)S(1)} %fusion.23) | copy-start | bytes 19906564
  191.5 3.3 copy-start.12
  191.5 3.3 copy-start.5
  191.5 4.2 %copy-start.16 = (bf16[24,128,540]{1,0,2:T(8,128)(2,1)S(1)}, bf16[24,128,540]{1,0,2:T(8,128)(2,1)}, u32[]{:S(2)}) copy-start(bf16[24,128,540]{1,0,2:T(8,128)(2,1)} %get-tuple-element.125) | copy-start | bytes 9953284
  194.8 3.1 slice-start
  195.7 2.2 slice-start.1
  197.8 23.3 %copy-start.8 = (bf16[128,24,128]{0,2,1:T(8,128)(2,1)}, bf16[128,24,128]{0,2,1:T(8,128)(2,1)S(1)}, u32[]{:S(2)}) copy-start(bf16[128,24,128]{0,2,1:T(8,128)(2,1)S(1)} %get-tuple-element.145) | copy-start | bytes 2359300
  197.9 17.1 %copy-start.4 = (bf16[540,24,128]{2,1,0:T(8,128)(2,1)S(1)}, bf16[540,24,128]{2,1,0:T(8,128)(2,1)}, u32[]{:S(2)}) copy-start(bf16[540,24,128]{2,1,0:T(8,128)(2,1)} %reshape_reshape.9) | copy-start | bytes 9953284
  217.0 3.9 copy-start.17
  235.1 70.4 %collective-permute-start.13 = (bf16[10,18,3072]{2,1,0:T(8,128)(2,1)}, bf16[10,18,3072]{2,1,0:T(8,128)(2,1)}, u32[]{:S(2)}, u32[]{:S(2)}) collective-permute-start(bf16[10,18,3072]{2,1,0:T(8,128)(2,1)} %squeeze.15), channel_id=1, source_target_pairs={{0,1},{1,2},{2,3},{3,4},{4,5},{5,6},{6,7},{7,8},{8,9},{9,10},{10,1... | collective-permute-start | bytes 3317768 | tf_op jit(solution)/shard_map/ppermute | solution.py:21
  270.8 5.8 %copy-start.13 = (bf16[128,3072]{0,1:T(8,128)(2,1)S(1)}, bf16[128,3072]{0,1:T(8,128)(2,1)}, u32[]{:S(2)}) copy-start(bf16[128,3072]{0,1:T(8,128)(2,1)} %copy-done.12) | copy-start | bytes 2359300
  275.1 30.4 %collective-permute-start.12 = (bf16[10,18,3072]{2,1,0:T(8,128)(2,1)}, bf16[10,18,3072]{2,1,0:T(8,128)(2,1)}, u32[]{:S(2)}, u32[]{:S(2)}) collective-permute-start(bf16[10,18,3072]{2,1,0:T(8,128)(2,1)} %squeeze.14), channel_id=1, source_target_pairs={{1,0},{2,1},{3,2},{4,3},{5,4},{6,5},{7,6},{8,7},{9,8},{10,9},{11,1... | collective-permute-start | bytes 3317768 | tf_op jit(solution)/shard_map/ppermute | solution.py:21
  285.1 24.3 %collective-permute-start.19 = (bf16[10,18,3072]{2,1,0:T(8,128)(2,1)}, bf16[10,18,3072]{2,1,0:T(8,128)(2,1)}, u32[]{:S(2)}, u32[]{:S(2)}) collective-permute-start(bf16[10,18,3072]{2,1,0:T(8,128)(2,1)} %squeeze.17), channel_id=1, source_target_pairs={{0,1},{1,2},{2,3},{3,4},{4,5},{5,6},{6,7},{7,8},{8,9},{9,10},{10,1... | collective-permute-start | bytes 3317768 | tf_op jit(solution)/shard_map/ppermute | solution.py:21
  292.0 3.1 copy-start.11
  292.0 4.2 %copy-start.9 = (bf16[128,24,128]{0,2,1:T(8,128)(2,1)S(1)}, bf16[128,24,128]{0,2,1:T(8,128)(2,1)}, u32[]{:S(2)}) copy-start(bf16[128,24,128]{0,2,1:T(8,128)(2,1)} %copy-done.8) | copy-start | bytes 2359300
  293.7 15.7 %collective-permute-start.18 = (bf16[10,18,3072]{2,1,0:T(8,128)(2,1)S(1)}, bf16[10,18,3072]{2,1,0:T(8,128)(2,1)}, u32[]{:S(2)}, u32[]{:S(2)}) collective-permute-start(bf16[10,18,3072]{2,1,0:T(8,128)(2,1)S(1)} %squeeze.16), channel_id=1, source_target_pairs={{1,0},{2,1},{3,2},{4,3},{5,4},{6,5},{7,6},{8,7},{9,8},{10,9},{11,1... | collective-permute-start | bytes 3317768 | tf_op jit(solution)/shard_map/ppermute | solution.py:21
  296.2 8.0 %copy-start.18 = (bf16[64,3072]{1,0:T(8,128)(2,1)S(1)}, bf16[64,3072]{1,0:T(8,128)(2,1)}, u32[]{:S(2)}) copy-start(bf16[64,3072]{1,0:T(8,128)(2,1)} %param.30) | copy-start | bytes 1179652
  296.2 9.3 %copy-start.6 = (f32[10,18,3072]{2,1,0:T(8,128)S(1)}, f32[10,18,3072]{2,1,0:T(8,128)}, u32[]{:S(2)}) copy-start(f32[10,18,3072]{2,1,0:T(8,128)} %reshape.455) | copy-start | bytes 6635524
  305.5 4.0 copy-start.7
  308.2 10.6 %collective-permute-start.14 = (bf16[1,18,3072]{2,1,0:T(8,128)(2,1)S(1)}, bf16[1,18,3072]{2,1,0:T(8,128)(2,1)S(1)}, u32[]{:S(2)}, u32[]{:S(2)}) collective-permute-start(bf16[1,18,3072]{2,1,0:T(8,128)(2,1)S(1)} %slice.379), channel_id=1, source_target_pairs={{8,0},{9,1},{10,2},{11,3},{12,4},{13,5},{14,6},{15,7},{24,16},{25,... | collective-permute-start | bytes 331784 | tf_op jit(solution)/shard_map/ppermute | solution.py:21
  312.0 10.8 %collective-permute-start.20 = (bf16[1,18,3072]{2,1,0:T(8,128)(2,1)S(1)}, bf16[1,18,3072]{2,1,0:T(8,128)(2,1)S(1)}, u32[]{:S(2)}, u32[]{:S(2)}) collective-permute-start(bf16[1,18,3072]{2,1,0:T(8,128)(2,1)S(1)} %slice.377), channel_id=1, source_target_pairs={{8,0},{9,1},{10,2},{11,3},{12,4},{13,5},{14,6},{15,7},{24,16},{25,... | collective-permute-start | bytes 331784 | tf_op jit(solution)/shard_map/ppermute | solution.py:21
  318.8 5.5 %collective-permute-start.15 = (bf16[1,18,3072]{2,1,0:T(8,128)(2,1)S(1)}, bf16[1,18,3072]{2,1,0:T(8,128)(2,1)S(1)}, u32[]{:S(2)}, u32[]{:S(2)}) collective-permute-start(bf16[1,18,3072]{2,1,0:T(8,128)(2,1)S(1)} %slice.378), channel_id=1, source_target_pairs={{0,8},{1,9},{2,10},{3,11},{4,12},{5,13},{6,14},{7,15},{16,24},{17,... | collective-permute-start | bytes 331784 | tf_op jit(solution)/shard_map/ppermute | solution.py:21
  322.9 5.5 %collective-permute-start.21 = (bf16[1,18,3072]{2,1,0:T(8,128)(2,1)S(1)}, bf16[1,18,3072]{2,1,0:T(8,128)(2,1)S(1)}, u32[]{:S(2)}, u32[]{:S(2)}) collective-permute-start(bf16[1,18,3072]{2,1,0:T(8,128)(2,1)S(1)} %slice.376), channel_id=1, source_target_pairs={{0,8},{1,9},{2,10},{3,11},{4,12},{5,13},{6,14},{7,15},{16,24},{17,... | collective-permute-start | bytes 331784 | tf_op jit(solution)/shard_map/ppermute | solution.py:21
  324.4 22.7 %collective-permute-start.16 = (f32[8,1,3072]{2,1,0:T(1,128)S(1)}, f32[8,1,3072]{2,1,0:T(1,128)S(1)}, u32[]{:S(2)}, u32[]{:S(2)}) collective-permute-start(f32[8,1,3072]{2,1,0:T(1,128)S(1)} %slice.333), channel_id=1, source_target_pairs={{2,0},{3,1},{4,2},{5,3},{6,4},{7,5},{8,6},{9,7},{10,8},{11,9},{12,... | collective-permute-start | bytes 294920 | tf_op jit(solution)/shard_map/ppermute | solution.py:21
  328.5 2.4 copy-start.3
  330.9 25.7 %collective-permute-start.22 = (f32[8,1,3072]{2,1,0:T(1,128)S(1)}, f32[8,1,3072]{2,1,0:T(1,128)S(1)}, u32[]{:S(2)}, u32[]{:S(2)}) collective-permute-start(f32[8,1,3072]{2,1,0:T(1,128)S(1)} %slice.346), channel_id=1, source_target_pairs={{2,0},{3,1},{4,2},{5,3},{6,4},{7,5},{8,6},{9,7},{10,8},{11,9},{12,... | collective-permute-start | bytes 294920 | tf_op jit(solution)/shard_map/ppermute | solution.py:21
  351.5 13.1 %collective-permute-start.17 = (f32[8,1,3072]{2,1,0:T(1,128)S(1)}, f32[8,1,3072]{2,1,0:T(1,128)S(1)}, u32[]{:S(2)}, u32[]{:S(2)}) collective-permute-start(f32[8,1,3072]{2,1,0:T(1,128)S(1)} %slice.335), channel_id=1, source_target_pairs={{0,2},{1,3},{2,4},{3,5},{4,6},{5,7},{6,8},{7,9},{8,10},{9,11},{10,... | collective-permute-start | bytes 294920 | tf_op jit(solution)/shard_map/ppermute | solution.py:21
  358.7 13.1 %collective-permute-start.23 = (f32[8,1,3072]{2,1,0:T(1,128)S(1)}, f32[8,1,3072]{2,1,0:T(1,128)S(1)}, u32[]{:S(2)}, u32[]{:S(2)}) collective-permute-start(f32[8,1,3072]{2,1,0:T(1,128)S(1)} %slice.348), channel_id=1, source_target_pairs={{0,2},{1,3},{2,4},{3,5},{4,6},{5,7},{6,8},{7,9},{8,10},{9,11},{10,... | collective-permute-start | bytes 294920 | tf_op jit(solution)/shard_map/ppermute | solution.py:21
  368.9 34.8 %copy-start.1 = (bf16[128,3072]{1,0:T(8,128)(2,1)S(1)}, bf16[128,3072]{1,0:T(8,128)(2,1)}, u32[]{:S(2)}) copy-start(bf16[128,3072]{1,0:T(8,128)(2,1)} %param.25) | copy-start | bytes 2359300
Sparse Core Ops, SparseCore 0:
  9.6 163.4 all-gather.1
  296.3 103.1 all-reduce.2
where the time goes:
time: 417 us; the launch traced here: 411 us
  starting transfers between devices  103 us (25%)
  waiting for transfers between devices  88.8 us (21%)
  local copies, waits for them, and re-layouts  86.1 us (21%)
  other arithmetic  70.4 us (17%)
  matrix products  47.4 us (11%)
  between operations  15.1 us (4%)
    ppermute x24, starting transfers between devices, from_behind(): return lax.ppermute(block, axis, route)  103 us
    all_gather x1, waiting for transfers between devices, on_device(): whole_weight = lax.all_gather(output_matrix, 'tensor', axis=0, tiled=True)  34.8 us
    and x4, local copies, waits for them, and re-layouts, window_table(): time_fit[:, None, None, :, None, None]  33.6 us
    ppermute x24, waiting for transfers between devices, from_behind(): return lax.ppermute(block, axis, route)  27.4 us
    psum x1, waiting for transfers between devices, on_device(): lax.psum((local_down, sharded_up_weight), 'tensor')  25.9 us
    convert_element_type x1, other arithmetic, attend_back(): probs.astype(jnp.bfloat16)  17.1 us
    dot_general x1, matrix products, on_device(): jnp.dot(upstream, whole_weight.T, preferred_element_type=jnp.float32)  13.9 us
    another operation x2, local copies, waits for them, and re-layouts, split_heads(): return block.reshape(block.shape[0], heads, -1)  12.7 us
  transfers between devices with their start and end apart: 26, of which 7 were waited for; matrix products, arithmetic and copies ran while one was open for 33% of the time, Pallas kernels for 0%

commit v1 on v0

v1 whole, which is shorter than its diff:
```python
import functools

import jax
import jax.numpy as jnp
from jax import lax
from jax.experimental import pallas as pl
from jax.experimental.pallas import tpu as pltpu
from jax.sharding import PartitionSpec as P

ROWS = 8
CTILES = 4
BANDS = 2
TCOLS = 16
TILE = ROWS * TCOLS
RIM = 48
SLOT = TILE + RIM
HEAD = 128
STEP = 4

SCALE = HEAD**-0.5
ADAPTER = 0.5
F32 = jnp.float32
BF16 = jnp.bfloat16


def nn(a, b):
    return jnp.dot(a, b, preferred_element_type=F32)


def nt(a, b):
    return lax.dot_general(a, b, (((1,), (1,)), ((), ())), preferred_element_type=F32)


def tn(a, b):
    return lax.dot_general(a, b, (((0,), (0,)), ((), ())), preferred_element_type=F32)


def slot_keys(slots, cols):
    keys, values = [], []
    for core_keys, core_values, rim in slots:
        keys += [core_keys[:, cols], rim[:RIM, cols]]
        values += [core_values[:, cols], rim[RIM:, cols]]
    return jnp.concatenate(keys, axis=0), jnp.concatenate(values, axis=0)


def forward_kernel(n_slots, combo, query, *refs):
    slots = [refs[3 * i : 3 * i + 3] for i in range(n_slots)]
    bias, down, grad_low, upstream, att_ref, log_ref, grads_ref, low_ref, low_acc = refs[
        3 * n_slots :
    ]
    step = pl.program_id(0)
    rank = down.shape[0]

    @pl.when(step == 0)
    def _():
        low_acc[...] = jnp.zeros_like(low_acc)

    for i in range(STEP):
        cols = slice(i * HEAD, (i + 1) * HEAD)
        keys, values = slot_keys(slots, cols)
        scores = nt(keys, query[:, cols]) * SCALE + bias[combo[step * STEP + i]]
        top = jnp.max(scores, axis=0, keepdims=True)
        weights = jnp.exp(scores - top)
        totals = jnp.sum(weights, axis=0, keepdims=True)
        att = (tn(values, weights.astype(BF16)) / totals).astype(BF16)
        att_ref[cols, :] = att
        log_ref[0, i : i + 1, :] = top + jnp.log(totals)
        low_acc[...] += nn(down[:, cols], att)
        grads_ref[:rank, pl.ds(pl.multiple_of((step * STEP + i) * HEAD, HEAD), HEAD)] = nt(
            grad_low[...], att
        )

    @pl.when(step == pl.num_programs(0) - 1)
    def _():
        low = low_acc[...].astype(BF16)
        low_ref[...] = low
        grads_ref[rank:, :] = ADAPTER * nn(low, upstream[...])


def backward_kernel(n_slots, combo, query, *refs):
    slots = [refs[3 * i : 3 * i + 3] for i in range(n_slots)]
    bias, att, grad, log_total, grad_query = refs[3 * n_slots : 3 * n_slots + 5]
    terms = refs[3 * n_slots + 5 :]
    step = pl.program_id(0)
    for i in range(STEP):
        cols = slice(i * HEAD, (i + 1) * HEAD)
        keys, values = slot_keys(slots, cols)
        here = query[:, cols]
        scores = nt(keys, here) * SCALE + bias[combo[step * STEP + i]]
        probs = jnp.exp(scores - log_total[0, i : i + 1, :])
        grad_att = grad[cols, :]
        inner = jnp.sum(
            grad_att.astype(F32) * att[cols, :].astype(F32), axis=0, keepdims=True
        )
        value_terms = nt(probs.astype(BF16), grad_att).astype(BF16)
        grad_scores = (probs * (nn(values, grad_att) - inner)).astype(BF16)
        key_terms = (nn(grad_scores, here) * SCALE).astype(BF16)
        grad_query[:, cols] = (tn(grad_scores, keys) * SCALE).astype(BF16)
        for s in range(n_slots):
            core, rim = terms[2 * s : 2 * s + 2]
            at = s * SLOT
            core[:TILE, cols] = key_terms[at : at + TILE]
            core[TILE:, cols] = value_terms[at : at + TILE]
            rim[:RIM, cols] = key_terms[at + TILE : at + SLOT]
            rim[RIM:, cols] = value_terms[at + TILE : at + SLOT]


def column_block(rows):
    return pl.BlockSpec((rows, STEP * HEAD), lambda step, *_: (0, step))


def row_block():
    return pl.BlockSpec((STEP * HEAD, TILE), lambda step, *_: (step, 0))


def whole(shape):
    return pl.BlockSpec(shape, lambda *_: (0,) * len(shape))


def head_call(kernel, steps, in_specs, out_specs, out_shape, scratch, flops):
    return pl.pallas_call(
        kernel,
        grid_spec=pltpu.PrefetchScalarGridSpec(
            num_scalar_prefetch=1,
            grid=(steps,),
            in_specs=in_specs,
            out_specs=out_specs,
            scratch_shapes=scratch,
        ),
        out_shape=out_shape,
        compiler_params=pltpu.CompilerParams(
            dimension_semantics=("arbitrary",), vmem_limit_bytes=40 * 1024 * 1024
        ),
        cost_estimate=pl.CostEstimate(
            flops=flops, bytes_accessed=6_000_000, transcendentals=0
        ),
    )


def slot_specs(n_slots):
    return [column_block(TILE), column_block(TILE), column_block(2 * RIM)] * n_slots


def attend(combo, query, slots, bias, down, grad_low, upstream):
    tokens, width = query.shape
    heads = width // HEAD
    rank = down.shape[0]
    n_slots = len(slots)
    keys = n_slots * SLOT
    return head_call(
        functools.partial(forward_kernel, n_slots),
        heads // STEP,
        [column_block(tokens)]
        + slot_specs(n_slots)
        + [
            whole(bias.shape),
            column_block(rank),
            whole(grad_low.shape),
            whole(upstream.shape),
        ],
        [
            row_block(),
            pl.BlockSpec((1, STEP, tokens), lambda step, *_: (step, 0, 0)),
            whole((2 * rank, width)),
            whole((rank, tokens)),
        ],
        [
            jax.ShapeDtypeStruct((width, tokens), BF16),
            jax.ShapeDtypeStruct((heads // STEP, STEP, tokens), F32),
            jax.ShapeDtypeStruct((2 * rank, width), F32),
            jax.ShapeDtypeStruct((rank, tokens), BF16),
        ],
        [pltpu.VMEM((rank, tokens), F32)],
        4 * keys * tokens * width,
    )(combo, query, *[part for slot in slots for part in slot], bias, down, grad_low, upstream)


def attend_back(combo, query, slots, bias, att, grad, log_total):
    tokens, width = query.shape
    heads = width // HEAD
    n_slots = len(slots)
    keys = n_slots * SLOT
    out = head_call(
        functools.partial(backward_kernel, n_slots),
        heads // STEP,
        [column_block(tokens)]
        + slot_specs(n_slots)
        + [
            whole(bias.shape),
            row_block(),
            row_block(),
            pl.BlockSpec((1, STEP, tokens), lambda step, *_: (step, 0, 0)),
        ],
        [column_block(tokens)] + [column_block(2 * TILE), column_block(2 * RIM)] * n_slots,
        [jax.ShapeDtypeStruct((tokens, width), BF16)]
        + [
            jax.ShapeDtypeStruct((2 * TILE, width), BF16),
            jax.ShapeDtypeStruct((2 * RIM, width), BF16),
        ]
        * n_slots,
        [],
        10 * keys * tokens * width,
    )(combo, query, *[part for slot in slots for part in slot], bias, att, grad, log_total)
    return out[0], [out[1 + 2 * s : 3 + 2 * s] for s in range(n_slots)]


def window_bias(shifts, frame_idx, band_idx, col_idx, frames):
    at = jnp.arange(SLOT, dtype=jnp.int32)
    rim = at - TILE
    outer = jnp.where(band_idx == 0, ROWS, -1)
    row = jnp.where(at < TILE, at // TCOLS, jnp.where(rim < 16, rim % ROWS, outer))
    col = jnp.where(
        at < TILE,
        at % TCOLS,
        jnp.where(
            rim < 8,
            -1,
            jnp.where(
                rim < 16, TCOLS, jnp.where(rim < 32, rim - 16, jnp.where(rim == 32, -1, TCOLS))
            ),
        ),
    )
    height = band_idx * ROWS + row
    across = col_idx * TCOLS + col
    there = (height >= 0) & (height < BANDS * ROWS) & (across >= 0) & (across < CTILES * TCOLS)
    there &= rim < 34
    query = jnp.arange(TILE, dtype=jnp.int32)
    row_gap = jnp.abs(row[:, None] - (query // TCOLS)[None, :])
    col_gap = jnp.abs(col[:, None] - (query % TCOLS)[None, :])
    near = there[:, None] & (col_gap <= 1)
    reach = jnp.arange(2, dtype=jnp.int32)
    space = near[None] & (row_gap[None] <= reach[:, None, None])
    shift = jnp.array(shifts, dtype=jnp.int32)
    time = (jnp.abs(shift)[None, :] <= reach[:, None]) & (
        (frame_idx + shift >= 0) & (frame_idx + shift < frames) | (frames == 2)
    )
    allowed = time[:, None, :, None, None] & space[None, :, None, :, :]
    return jnp.where(allowed, 0.0, -1e30).astype(F32).reshape(4, len(shifts) * SLOT, TILE)


def permute(block, route):
    return lax.ppermute(block, "tensor", route)


def on_device(
    input_queries,
    input_keys,
    input_values,
    output_matrix,
    adapter_down_weight,
    adapter_up_weight,
    upstream,
    window_frame_reach,
    window_row_reach,
):
    devices = lax.axis_size("tensor")
    frames = devices // (BANDS * CTILES)
    position = lax.axis_index("tensor")
    frame_idx = position % frames
    col_idx = position // frames % CTILES
    band_idx = position // (frames * CTILES)
    everyone = range(devices)
    to_right = [(i, i + frames) for i in everyone if i // frames % CTILES < CTILES - 1]
    to_left = [(j, i) for i, j in to_right]
    to_band = [(i, (i + devices // BANDS) % devices) for i in everyone]
    if frames == 1:
        shifts, to_frame = [0], []
    elif frames == 2:
        shifts, to_frame = [0, 1], [[(i, i ^ 1) for i in everyone]]
    else:
        later = [(i, i + 1) for i in everyone if i % frames < frames - 1]
        shifts, to_frame = [0, -1, 1], [later, [(j, i) for i, j in later]]
    edge_row = jnp.where(band_idx == 0, ROWS - 1, 0)
    combo = 2 * window_frame_reach + window_row_reach

    cell = jnp.arange(TILE, dtype=jnp.int32)
    mark = jnp.arange(32, dtype=jnp.int32)
    source = jnp.where(
        mark < 8,
        mark * TCOLS,
        jnp.where(mark < 16, (mark - 8) * TCOLS + TCOLS - 1, edge_row * TCOLS + mark - 16),
    )
    pick = (source[:, None] == cell[None, :]).astype(BF16)
    edge_keys = nn(pick, input_keys).astype(BF16)
    edge_values = nn(pick, input_values).astype(BF16)
    right = permute(jnp.concatenate([edge_keys[:8], edge_values[:8]]), to_left)
    left = permute(jnp.concatenate([edge_keys[8:16], edge_values[8:16]]), to_right)
    core_slots = [
        (permute(input_keys, route), permute(input_values, route)) for route in to_frame
    ]

    def corner(block, at):
        return lax.dynamic_slice_in_dim(block, at + edge_row, 1)

    outer = permute(
        jnp.concatenate(
            [
                edge_keys[16:],
                edge_values[16:],
                corner(left, 0),
                corner(right, 0),
                corner(left, 8),
                corner(right, 8),
            ]
        ),
        to_band,
    )
    blank = jnp.zeros((14, input_keys.shape[1]), BF16)
    rim = jnp.concatenate(
        [
            left[:8], right[:8], outer[:16], outer[32:34], blank,
            left[8:], right[8:], outer[16:32], outer[34:], blank,
        ]
    )
    slots = [(input_keys, input_values, rim)] + [
        (*core, permute(rim, route)) for core, route in zip(core_slots, to_frame)
    ]
    bias = window_bias(shifts, frame_idx, band_idx, col_idx, frames)

    whole_weight = lax.all_gather(output_matrix, "tensor", axis=0, tiled=True)
    down = adapter_down_weight.T
    grad_low = (ADAPTER * nt(adapter_up_weight, upstream)).astype(BF16)
    att, log_total, grads, low = attend(
        combo, input_queries, slots, bias, down, grad_low, upstream
    )

    def rounded(block):
        return block.astype(BF16).astype(F32)

    rank = down.shape[0]
    second = position % 2
    mine = lax.dynamic_slice_in_dim(grads, second * rank, rank)
    theirs = lax.dynamic_slice_in_dim(grads, (1 - second) * rank, rank).astype(BF16)
    part = mine + permute(theirs, [(i, i ^ 1) for i in everyone]).astype(F32)
    bit = 2
    while bit < devices:
        part = part.astype(BF16)
        part = part.astype(F32) + permute(part, [(i, i ^ bit) for i in everyone]).astype(F32)
        bit *= 2
    part = part.astype(BF16)
    other = permute(part, [(i, i ^ 1) for i in everyone])
    grad_down = jnp.where(second == 0, part, other).astype(F32).T
    grad_up = jnp.where(second == 0, other, part).astype(F32)

    grad_att = (nt(whole_weight, upstream) + tn(down, grad_low)).astype(BF16)
    grad_query, terms = attend_back(
        combo, input_queries, slots, bias, att, grad_att, log_total
    )
    projected = (
        tn(att, whole_weight) + ADAPTER * tn(low, adapter_up_weight)
    ).astype(BF16)

    core, rim_terms = terms[0]
    rim_terms = rim_terms.astype(F32)
    back = [[(j, i) for i, j in route] for route in to_frame]
    for (_, sent), route in zip(terms[1:], back):
        rim_terms += permute(sent, route).astype(F32)
    core_terms = [core] + [permute(sent, route) for (sent, _), route in zip(terms[1:], back)]
    keys_out, values_out = rim_terms[:RIM], rim_terms[RIM:]
    outer = permute(
        jnp.concatenate(
            [keys_out[16:32], values_out[16:32], keys_out[32:34], values_out[32:34]]
        ).astype(BF16),
        to_band,
    )
    at_edge = (jnp.arange(ROWS)[:, None] == edge_row).astype(F32)
    outer_corners = outer[32:].astype(F32)

    def side(number):
        at = 8 * number
        return jnp.concatenate(
            [
                keys_out[at : at + 8] + at_edge * outer_corners[number],
                values_out[at : at + 8] + at_edge * outer_corners[2 + number],
            ]
        ).astype(BF16)

    from_right = permute(side(0), to_left)
    from_left = permute(side(1), to_right)
    gathered = [
        jnp.concatenate([from_left[at : at + 8], from_right[at : at + 8], outer[row : row + 16]])
        for at, row in ((0, 0), (8, 16))
    ]
    grad_key, grad_value = (
        (
            sum(block[rows].astype(F32) for block in core_terms) + tn(pick, got)
        ).astype(BF16)
        for rows, got in ((slice(0, TILE), gathered[0]), (slice(TILE, None), gathered[1]))
    )
    return (projected, grad_query, grad_key, grad_value, grad_down, grad_up)


def solution(mesh):
    tokens = P(("groups", "tensor"), None)
    return jax.shard_map(
        on_device,
        mesh=mesh,
        in_specs=(tokens, tokens, tokens, P("tensor", None), P(), P(), tokens, P(), P()),
        out_specs=(tokens, tokens, tokens, tokens, P("groups", None), P("groups", None)),
        check_vma=False,
    )
```

time: 417 us -> 197 us (0.47); the launches traced: 411 us -> 196 us
  starting transfers between devices: 103 us -> 19.6 us
  local copies, waits for them, and re-layouts: 86.1 us -> 8.25 us
  other arithmetic: 70.4 us -> 7.49 us
  Pallas kernels: 0 us -> 22.1 us
  matrix products: 47.4 us -> 27.2 us
  waiting for transfers between devices: 88.8 us -> 96.5 us
    ppermute x24 -> x16, starting transfers between devices: 103 us -> 19.6 us  [permute(): return lax.ppermute(block, 'tensor', route)]
    ppermute x24 -> x16, waiting for transfers between devices: 27.4 us -> 95.8 us  [permute(): return lax.ppermute(block, 'tensor', route)]
    all_gather x1, waiting for transfers between devices: 34.8 us -> 0.01 us  [on_device(): whole_weight = lax.all_gather(output_matrix, 'tensor', axis=0, tiled=True)]
    and x4 -> x3, local copies, waits for them, and re-layouts: 33.6 us -> 0.21 us  [window_bias(): allowed = time[:, None, :, None, None] & space[None, :, None, :, :]]
    psum x1 -> x0, waiting for transfers between devices: 25.9 us -> none  [on_device(): lax.psum((local_down, sharded_up_weight), 'tensor')]
    pallas_call x0 -> x2, Pallas kernels: none -> 22.1 us  [the longest x1 11.6 us: attend(): head_call(functools.partial(forward_kernel, n_slots), heads // STEP, [col...]
    dot_general x14 -> x9, matrix products: 47.4 us -> 27.2 us  [the longest x5 14.6 us: tn(): lax.dot_general(a, b, (((0,), (0,)), ((), ())), preferred_element_type=F32)]
    convert_element_type x2 -> x7, other arithmetic: 24.3 us -> 6.59 us  [the longest x4 4.22 us: on_device(): part = part.astype(BF16)]
  transfers between devices with their start and end apart: 26 -> 17, of which waited for: 7 -> 11; matrix products, arithmetic and copies ran while one was open for 33% -> 17% of each run, Pallas kernels for 0% -> 11%
where the time goes in v1:
time: 197 us; the launch traced here: 196 us
  waiting for transfers between devices  96.5 us (49%)
  matrix products  27.2 us (14%)
  Pallas kernels  22.1 us (11%)
  starting transfers between devices  19.6 us (10%)
  between operations  14.5 us (7%)
  local copies, waits for them, and re-layouts  8.25 us (4%)
  other arithmetic  7.49 us (4%)
    ppermute x16, waiting for transfers between devices, permute(): return lax.ppermute(block, 'tensor', route)  95.8 us
    ppermute x16, starting transfers between devices, permute(): return lax.ppermute(block, 'tensor', route)  19.6 us
    dot_general x5, matrix products, tn(): lax.dot_general(a, b, (((0,), (0,)), ((), ())), preferred_element_type=F32)  14.6 us
    pallas_call x1, Pallas kernels, attend(): head_call(functools.partial(forward_kernel, n_slots), heads // STEP, [col...  11.6 us
    dot_general x2, matrix products, nt(): lax.dot_general(a, b, (((1,), (1,)), ((), ())), preferred_element_type=F32)  10.9 us
    pallas_call x1, Pallas kernels, attend_back(): head_call(functools.partial(backward_kernel, n_slots), heads // STEP, [co...  10.5 us
    unnamed x28, local copies, waits for them, and re-layouts  6.29 us
    convert_element_type x4, other arithmetic, on_device(): part = part.astype(BF16)  4.22 us
  transfers between devices with their start and end apart: 17, of which 11 were waited for; matrix products, arithmetic and copies ran while one was open for 17% of the time, Pallas kernels for 11%

profile of v1, /device:TPU:0, one launch (start us, length us, event | category | flops | bytes accessed | tf_op | source)
XLA Modules:
  0.0 195.6 jit_solution(12297005934436359725)
XLA Ops:
  7.2 0.7 all-gather.2.cloned.1.call-update
  7.9 0.5 collective-permute-start.3
  8.6 1.4 convolution_convert_fusion
  10.0 0.3 convolution_convert_fusion.1
  10.3 4.9 %collective-permute-start = (bf16[16,3072]{1,0:T(8,128)(2,1)S(1)}, bf16[16,3072]{1,0:T(8,128)(2,1)S(1)}, u32[]{:S(2)}, u32[]{:S(2)}) collective-permute-start(bf16[16,3072]{1,0:T(8,128)(2,1)S(1)} %pad_maximum_fusion.1), channel_id=1, source_target_pairs={{0,2},{1,3},{2,4},{3,5},{4,6},{5,7},{8,10},{9,11},{10,12},{11,13},... | collective-permute-start | bytes 294920 | tf_op jit(solution)/shard_map/ppermute | solution.py:242
  15.2 1.3 collective-permute-start.1
  16.9 0.5 collective-permute-done
  17.5 5.8 %collective-permute-done.1 = bf16[16,3072]{1,0:T(8,128)(2,1)S(1)} collective-permute-done((bf16[16,3072]{1,0:T(8,128)(2,1)S(1)}, bf16[16,3072]{1,0:T(8,128)(2,1)S(1)}, u32[]{:S(2)}, u32[]{:S(2)}) %collective-permute-start.1) | collective-permute-done | bytes 98336 | tf_op jit(solution)/shard_map/ppermute | solution.py:242
  23.4 1.1 collective-permute-start.2
  24.5 17.7 %collective-permute-done.2 = bf16[36,3072]{1,0:T(8,128)(2,1)S(1)} collective-permute-done((bf16[36,3072]{1,0:T(8,128)(2,1)S(1)}, bf16[36,3072]{1,0:T(8,128)(2,1)S(1)}, u32[]{:S(2)}, u32[]{:S(2)}) %collective-permute-start.2) | collective-permute-done | bytes 221216 | tf_op jit(solution)/shard_map/ppermute | solution.py:242
  42.3 0.6 concatenate.33.refs_2_
  43.2 0.3 and_select_fusion.refs_6_
  43.5 1.5 fusion.3.refs_8_
  45.1 1.1 copy-done.5
  46.3 1.1 copy-done.6
  47.4 1.0 copy-done.8
  48.4 11.6 %shard_map.145 = (bf16[3072,128]{1,0:T(8,128)(2,1)S(1)}, f32[6,4,128]{2,1,0:T(4,128)S(1)}, f32[128,3072]{1,0:T(8,128)S(1)}, bf16[64,128]{1,0:T(8,128)(2,1)S(1)}) custom-call(s32[24]{0:T(128)S(1)} %multiply_add_fusion.combo, bf16[128,3072]{1,0:T(8,128)(2,1)S(1)} %copy-done.6, bf16[128,3072]{1,0:T(8,128)(2,1)S(1)} %copy-done.1, ...), custom_call_target="tpu_custom_call" | custom-call | flops 553648128 | bytes 6000000 | tf_op jit(solution)/shard_map/pallas_call | solution.py:150
  60.0 0.9 copy-done.3
  60.9 1.1 copy-done.10
  62.1 0.8 dynamic-slice_convert_fusion
  62.8 0.5 collective-permute-start.11
  63.3 1.8 collective-permute-done.11
  65.2 1.3 add_convert_fusion.5
  66.5 1.5 collective-permute-start.12
  68.0 18.7 %collective-permute-done.12 = bf16[64,3072]{1,0:T(8,128)(2,1)S(1)} collective-permute-done((bf16[64,3072]{1,0:T(8,128)(2,1)S(1)}, bf16[64,3072]{1,0:T(8,128)(2,1)S(1)}, u32[]{:S(2)}, u32[]{:S(2)}) %collective-permute-start.12) | collective-permute-done | bytes 393248 | tf_op jit(solution)/shard_map/ppermute | solution.py:242
  86.9 19.9 %collective-permute-done.13 = bf16[64,3072]{1,0:T(8,128)(2,1)S(1)} collective-permute-done((bf16[64,3072]{1,0:T(8,128)(2,1)S(1)}, bf16[64,3072]{1,0:T(8,128)(2,1)S(1)}, u32[]{:S(2)}, u32[]{:S(2)}) %collective-permute-start.13) | collective-permute-done | bytes 393248 | tf_op jit(solution)/shard_map/ppermute | solution.py:242
  106.9 0.8 add_convert_fusion.3
  107.7 1.7 collective-permute-start.14
  109.4 1.5 convolution_multiply_fusion
  110.9 25.7 %collective-permute-done.14 = bf16[64,3072]{1,0:T(8,128)(2,1)} collective-permute-done((bf16[64,3072]{1,0:T(8,128)(2,1)}, bf16[64,3072]{1,0:T(8,128)(2,1)}, u32[]{:S(2)}, u32[]{:S(2)}) %collective-permute-start.14) | collective-permute-done | bytes 393248 | tf_op jit(solution)/shard_map/ppermute | solution.py:242
  136.6 2.0 add_convert_fusion.2
  138.6 9.4 %fusion.53 = f32[3072,128]{1,0:T(8,128)S(1)} fusion(bf16[3072,3072]{1,0:T(8,128)(2,1)} %all-gather.2.cloned.1.call-done, bf16[128,3072]{1,0:T(8,128)(2,1)} %refs_9_.1), kind=kOutput, calls=%fused_computation.108 | convolution fusion | flops 2415919104 | bytes 21233664 | tf_op jit(solution)/shard_map/dot_general | solution.py:31
  148.0 0.4 fusion.2.refs_8_
  148.4 0.7 copy-done.4
  149.1 0.2 copy-done.7
  149.3 10.5 %shard_map.146 = (bf16[128,3072]{1,0:T(8,128)(2,1)}, bf16[256,3072]{1,0:T(8,128)(2,1)S(1)}, bf16[96,3072]{1,0:T(8,128)(2,1)S(1)}, bf16[256,3072]{1,0:T(8,128)(2,1)S(1)}, bf16[96,3072]{1,0:T(8,128)(2,1)S(1)}) custom-call(s32[24]{0:T(128)S(1)} %multiply_add_fusion.combo, bf16[128,3072]{1,0:T(8,128)(2,1)S(1)} %copy-done.7, bf16[128,3072]{1,0:T(8,128)(2,1)S(1)} %copy-done.1, ...), custom_call_target="tpu_custom_call" | custom-call | flops 1384120320 | bytes 6000000 | tf_op jit(solution)/shard_map/pallas_call | solution.py:183
  159.8 0.5 collective-permute-start.7
  160.3 2.4 %select_convert_fusion = (f32[64,3072]{1,0:T(8,128)}, f32[3072,64]{0,1:T(8,128)}) fusion(bf16[64,3072]{1,0:T(8,128)(2,1)} %collective-permute-done.15, bf16[64,3072]{1,0:T(8,128)(2,1)} %add_convert_fusion.2, pred[]{:T(512)S(6)} %eq.59), kind=kLoop, calls=%fused_computation.20 | loop fusion | flops 786432 | bytes 2359297 | tf_op jit(solution)/shard_map/convert_element_type | solution.py:343
  162.7 0.2 convert_add_fusion
  163.0 1.5 collective-permute-start.8
  164.5 9.9 %fusion.1 = bf16[128,3072]{1,0:T(8,128)(2,1)} fusion(f32[128,3072]{1,0:T(8,128)S(1)} %copy-done.11, bf16[3072,128]{1,0:T(8,128)(2,1)S(1)} %copy-done.4, bf16[3072,3072]{1,0:T(8,128)(2,1)} %all-gather.2.cloned.1.call-done), kind=kOutput, calls=%fused_computation.4 | convolution fusion | flops 2416705536 | bytes 22020096 | tf_op jit(solution)/shard_map/dot_general | solution.py:35
  174.4 3.2 %collective-permute-done.8 = bf16[36,3072]{1,0:T(8,128)(2,1)S(1)} collective-permute-done((bf16[36,3072]{1,0:T(8,128)(2,1)S(1)}, bf16[36,3072]{1,0:T(8,128)(2,1)S(1)}, u32[]{:S(2)}, u32[]{:S(2)}) %collective-permute-start.8) | collective-permute-done | bytes 221216 | tf_op jit(solution)/shard_map/ppermute | solution.py:242
  177.7 1.3 collective-permute-start.10
  179.1 4.6 %collective-permute-start.9 = (bf16[16,3072]{1,0:T(8,128)(2,1)S(1)}, bf16[16,3072]{1,0:T(8,128)(2,1)S(1)}, u32[]{:S(2)}, u32[]{:S(2)}) collective-permute-start(bf16[16,3072]{1,0:T(8,128)(2,1)S(1)} %pad_maximum_fusion.3), channel_id=1, source_target_pairs={{0,2},{1,3},{2,4},{3,5},{4,6},{5,7},{8,10},{9,11},{10,12},{11,13},... | collective-permute-start | bytes 294920 | tf_op jit(solution)/shard_map/ppermute | solution.py:242
  183.6 0.6 collective-permute-done.10
  184.3 1.7 collective-permute-done.9
  186.0 1.4 add_convert_fusion.1
  187.4 1.4 add_convert_fusion
  (73 shorter events, 1.6 us)
Async XLA Ops:
  7.2 36.3 %copy-start = (bf16[64,3072]{1,0:T(8,128)(2,1)S(1)}, bf16[64,3072]{1,0:T(8,128)(2,1)}, u32[]{:S(2)}) copy-start(bf16[64,3072]{1,0:T(8,128)(2,1)} %param.15) | copy-start | bytes 1179652
  7.2 2.8 %copy-start.1 = (bf16[128,3072]{1,0:T(8,128)(2,1)S(1)}, bf16[128,3072]{1,0:T(8,128)(2,1)}, u32[]{:S(2)}) copy-start(bf16[128,3072]{1,0:T(8,128)(2,1)} %refs_0_.3) | copy-start | bytes 2359300
  7.2 131.4 %all-gather.2.cloned.1.call-start = ((), (), s32[]{:S(2)}) async-start(), calls=%async_computation | async-start | bytes 20054016 | tf_op jit(solution)/shard_map/all_gather | solution.py:320
  7.9 8.9 %copy-start.12 = (s32[24]{0:T(128)S(1)}, s32[24]{0:T(128)}, u32[]{:S(2)}) copy-start(s32[24]{0:T(128)} %param.18) | copy-start | bytes 292
  7.9 8.9 %copy-start.13 = (s32[24]{0:T(128)S(1)}, s32[24]{0:T(128)}, u32[]{:S(2)}) copy-start(s32[24]{0:T(128)} %param.17) | copy-start | bytes 292
  7.9 37.1 %collective-permute-start.3 = (bf16[128,3072]{1,0:T(8,128)(2,1)}, bf16[128,3072]{1,0:T(8,128)(2,1)}, u32[]{:S(2)}, u32[]{:S(2)}) collective-permute-start(bf16[128,3072]{1,0:T(8,128)(2,1)} %refs_0_.3), channel_id=1, source_target_pairs={{0,1},{1,0},{2,3},{3,2},{4,5},{5,4},{6,7},{7,6},{8,9},{9,8},{10,11... | collective-permute-start | bytes 2359304 | tf_op jit(solution)/shard_map/ppermute | solution.py:242
  8.5 36.6 %collective-permute-start.4 = (bf16[128,3072]{1,0:T(8,128)(2,1)}, bf16[128,3072]{1,0:T(8,128)(2,1)}, u32[]{:S(2)}, u32[]{:S(2)}) collective-permute-start(bf16[128,3072]{1,0:T(8,128)(2,1)} %refs_1_.3), channel_id=1, source_target_pairs={{0,1},{1,0},{2,3},{3,2},{4,5},{5,4},{6,7},{7,6},{8,9},{9,8},{10,11... | collective-permute-start | bytes 2359304 | tf_op jit(solution)/shard_map/ppermute | solution.py:242
  10.3 7.1 %collective-permute-start = (bf16[16,3072]{1,0:T(8,128)(2,1)S(1)}, bf16[16,3072]{1,0:T(8,128)(2,1)S(1)}, u32[]{:S(2)}, u32[]{:S(2)}) collective-permute-start(bf16[16,3072]{1,0:T(8,128)(2,1)S(1)} %pad_maximum_fusion.1), channel_id=1, source_target_pairs={{0,2},{1,3},{2,4},{3,5},{4,6},{5,7},{8,10},{9,11},{10,12},{11,13},... | collective-permute-start | bytes 294920 | tf_op jit(solution)/shard_map/ppermute | solution.py:242
  15.2 8.1 %collective-permute-start.1 = (bf16[16,3072]{1,0:T(8,128)(2,1)S(1)}, bf16[16,3072]{1,0:T(8,128)(2,1)S(1)}, u32[]{:S(2)}, u32[]{:S(2)}) collective-permute-start(bf16[16,3072]{1,0:T(8,128)(2,1)S(1)} %pad_maximum_fusion.2), channel_id=1, source_target_pairs={{2,0},{3,1},{4,2},{5,3},{6,4},{7,5},{10,8},{11,9},{12,10},{13,11},... | collective-permute-start | bytes 294920 | tf_op jit(solution)/shard_map/ppermute | solution.py:242
  23.4 18.8 %collective-permute-start.2 = (bf16[36,3072]{1,0:T(8,128)(2,1)S(1)}, bf16[36,3072]{1,0:T(8,128)(2,1)S(1)}, u32[]{:S(2)}, u32[]{:S(2)}) collective-permute-start(bf16[36,3072]{1,0:T(8,128)(2,1)S(1)} %concatenate.32), channel_id=1, source_target_pairs={{0,8},{1,9},{2,10},{3,11},{4,12},{5,13},{6,14},{7,15},{8,0},{9,1},... | collective-permute-start | bytes 663560 | tf_op jit(solution)/shard_map/ppermute | solution.py:242
  42.3 2.8 %copy-start.2 = (bf16[128,3072]{1,0:T(8,128)(2,1)S(1)}, bf16[128,3072]{1,0:T(8,128)(2,1)}, u32[]{:S(2)}) copy-start(bf16[128,3072]{1,0:T(8,128)(2,1)} %refs_1_.3) | copy-start | bytes 2359300
  42.9 2.2 %collective-permute-start.5 = (bf16[96,3072]{1,0:T(8,128)(2,1)S(1)}, bf16[96,3072]{1,0:T(8,128)(2,1)}, u32[]{:S(2)}, u32[]{:S(2)}) collective-permute-start(bf16[96,3072]{1,0:T(8,128)(2,1)S(1)} %concatenate.33.refs_2_), channel_id=1, source_target_pairs={{0,1},{1,0},{2,3},{3,2},{4,5},{5,4},{6,7},{7,6},{8,9},{9,8},{10,11... | collective-permute-start | bytes 1769480 | tf_op jit(solution)/shard_map/ppermute | solution.py:242
  45.1 1.1 copy-start.5
  46.3 1.1 copy-start.6
  47.4 1.0 copy-start.8
  60.0 0.9 copy-start.3
  60.9 1.1 copy-start.10
  62.8 2.3 %collective-permute-start.11 = (bf16[64,3072]{1,0:T(8,128)(2,1)}, bf16[64,3072]{1,0:T(8,128)(2,1)}, u32[]{:S(2)}, u32[]{:S(2)}) collective-permute-start(bf16[64,3072]{1,0:T(8,128)(2,1)} %dynamic-slice_convert_fusion), channel_id=1, source_target_pairs={{0,1},{1,0},{2,3},{3,2},{4,5},{5,4},{6,7},{7,6},{8,9},{9,8},{10,11... | collective-permute-start | bytes 1179656 | tf_op jit(solution)/shard_map/ppermute | solution.py:242
  66.5 20.3 %collective-permute-start.12 = (bf16[64,3072]{1,0:T(8,128)(2,1)S(1)}, bf16[64,3072]{1,0:T(8,128)(2,1)S(1)}, u32[]{:S(2)}, u32[]{:S(2)}) collective-permute-start(bf16[64,3072]{1,0:T(8,128)(2,1)S(1)} %add_convert_fusion.5), channel_id=1, source_target_pairs={{0,2},{1,3},{2,0},{3,1},{4,6},{5,7},{6,4},{7,5},{8,10},{9,11},{10,... | collective-permute-start | bytes 1179656 | tf_op jit(solution)/shard_map/ppermute | solution.py:242
  86.9 20.0 %collective-permute-start.13 = (bf16[64,3072]{1,0:T(8,128)(2,1)S(1)}, bf16[64,3072]{1,0:T(8,128)(2,1)S(1)}, u32[]{:S(2)}, u32[]{:S(2)}) collective-permute-start(bf16[64,3072]{1,0:T(8,128)(2,1)S(1)} %add_convert_fusion.4), channel_id=1, source_target_pairs={{0,4},{1,5},{2,6},{3,7},{4,0},{5,1},{6,2},{7,3},{8,12},{9,13},{10,... | collective-permute-start | bytes 1179656 | tf_op jit(solution)/shard_map/ppermute | solution.py:242
  107.7 28.9 %collective-permute-start.14 = (bf16[64,3072]{1,0:T(8,128)(2,1)}, bf16[64,3072]{1,0:T(8,128)(2,1)}, u32[]{:S(2)}, u32[]{:S(2)}) collective-permute-start(bf16[64,3072]{1,0:T(8,128)(2,1)} %add_convert_fusion.3), channel_id=1, source_target_pairs={{0,8},{1,9},{2,10},{3,11},{4,12},{5,13},{6,14},{7,15},{8,0},{9,1},... | collective-permute-start | bytes 1179656 | tf_op jit(solution)/shard_map/ppermute | solution.py:242
  138.6 21.7 %collective-permute-start.15 = (bf16[64,3072]{1,0:T(8,128)(2,1)}, bf16[64,3072]{1,0:T(8,128)(2,1)}, u32[]{:S(2)}, u32[]{:S(2)}) collective-permute-start(bf16[64,3072]{1,0:T(8,128)(2,1)} %add_convert_fusion.2), channel_id=1, source_target_pairs={{0,1},{1,0},{2,3},{3,2},{4,5},{5,4},{6,7},{7,6},{8,9},{9,8},{10,11... | collective-permute-start | bytes 1179656 | tf_op jit(solution)/shard_map/ppermute | solution.py:242
  138.6 9.4 %copy-start.9 = (bf16[3072,64]{0,1:T(8,128)(2,1)S(1)}, bf16[3072,64]{0,1:T(8,128)(2,1)}, u32[]{:S(2)}) copy-start(bf16[3072,64]{0,1:T(8,128)(2,1)} %param.14) | copy-start | bytes 1179652
  148.0 1.1 copy-start.4
  148.0 1.4 copy-start.7
  159.8 2.9 %collective-permute-start.7 = (bf16[96,3072]{1,0:T(8,128)(2,1)S(1)}, bf16[96,3072]{1,0:T(8,128)(2,1)S(1)}, u32[]{:S(2)}, u32[]{:S(2)}) collective-permute-start(bf16[96,3072]{1,0:T(8,128)(2,1)S(1)} %get-tuple-element.22), channel_id=1, source_target_pairs={{1,0},{0,1},{3,2},{2,3},{5,4},{4,5},{7,6},{6,7},{9,8},{8,9},{11,10... | collective-permute-start | bytes 1769480 | tf_op jit(solution)/shard_map/ppermute | solution.py:242
  162.7 23.3 %collective-permute-start.6 = (bf16[256,3072]{1,0:T(8,128)(2,1)S(1)}, bf16[256,3072]{1,0:T(8,128)(2,1)S(1)}, u32[]{:S(2)}, u32[]{:S(2)}) collective-permute-start(bf16[256,3072]{1,0:T(8,128)(2,1)S(1)} %get-tuple-element.20), channel_id=1, source_target_pairs={{1,0},{0,1},{3,2},{2,3},{5,4},{4,5},{7,6},{6,7},{9,8},{8,9},{11,10... | collective-permute-start | bytes 4718600 | tf_op jit(solution)/shard_map/ppermute | solution.py:242
  162.7 1.8 copy-start.11
  163.0 14.6 %collective-permute-start.8 = (bf16[36,3072]{1,0:T(8,128)(2,1)S(1)}, bf16[36,3072]{1,0:T(8,128)(2,1)S(1)}, u32[]{:S(2)}, u32[]{:S(2)}) collective-permute-start(bf16[36,3072]{1,0:T(8,128)(2,1)S(1)} %pad_maximum_fusion), channel_id=1, source_target_pairs={{0,8},{1,9},{2,10},{3,11},{4,12},{5,13},{6,14},{7,15},{8,0},{9,1},... | collective-permute-start | bytes 663560 | tf_op jit(solution)/shard_map/ppermute | solution.py:242
  177.7 6.5 %collective-permute-start.10 = (bf16[16,3072]{1,0:T(8,128)(2,1)S(1)}, bf16[16,3072]{1,0:T(8,128)(2,1)S(1)}, u32[]{:S(2)}, u32[]{:S(2)}) collective-permute-start(bf16[16,3072]{1,0:T(8,128)(2,1)S(1)} %pad_maximum_fusion.4), channel_id=1, source_target_pairs={{2,0},{3,1},{4,2},{5,3},{6,4},{7,5},{10,8},{11,9},{12,10},{13,11},... | collective-permute-start | bytes 294920 | tf_op jit(solution)/shard_map/ppermute | solution.py:242
  179.1 6.9 %collective-permute-start.9 = (bf16[16,3072]{1,0:T(8,128)(2,1)S(1)}, bf16[16,3072]{1,0:T(8,128)(2,1)S(1)}, u32[]{:S(2)}, u32[]{:S(2)}) collective-permute-start(bf16[16,3072]{1,0:T(8,128)(2,1)S(1)} %pad_maximum_fusion.3), channel_id=1, source_target_pairs={{0,2},{1,3},{2,4},{3,5},{4,6},{5,7},{8,10},{9,11},{10,12},{11,13},... | collective-permute-start | bytes 294920 | tf_op jit(solution)/shard_map/ppermute | solution.py:242
Sparse Core Ops, SparseCore 0:
  9.6 122.5 all-gather.1

commit v2 on v1

v2 whole, which is shorter than its diff:
```python
import functools

import jax
import jax.numpy as jnp
from jax import lax
from jax.experimental import pallas as pl
from jax.experimental.pallas import tpu as pltpu
from jax.sharding import PartitionSpec as P

ROWS = 8
CTILES = 4
BANDS = 2
TCOLS = 16
TILE = ROWS * TCOLS
RIM = 48
SLOT = TILE + RIM
HEAD = 128
STEP = 4

SCALE = HEAD**-0.5
ADAPTER = 0.5
F32 = jnp.float32
BF16 = jnp.bfloat16


def nn(a, b):
    return jnp.dot(a, b, preferred_element_type=F32)


def nt(a, b):
    return lax.dot_general(a, b, (((1,), (1,)), ((), ())), preferred_element_type=F32)


def tn(a, b):
    return lax.dot_general(a, b, (((0,), (0,)), ((), ())), preferred_element_type=F32)


def slot_keys(slots, cols):
    keys, values = [], []
    for core_keys, core_values, rim in slots:
        keys += [core_keys[:, cols], rim[:RIM, cols]]
        values += [core_values[:, cols], rim[RIM:, cols]]
    return jnp.concatenate(keys, axis=0), jnp.concatenate(values, axis=0)


def forward_kernel(n_slots, combo, query, *refs):
    slots = [refs[3 * i : 3 * i + 3] for i in range(n_slots)]
    bias, down, grad_low, upstream, att_ref, log_ref, grads_ref, low_ref, low_acc = refs[
        3 * n_slots :
    ]
    step = pl.program_id(0)
    last = combo.shape[0] - 1

    @pl.when(step == 0)
    def _():
        low_acc[...] = jnp.zeros_like(low_acc)

    for i in range(STEP):
        cols = slice(i * HEAD, (i + 1) * HEAD)
        keys, values = slot_keys(slots, cols)
        scores = nt(keys, query[:, cols]) * SCALE + bias[combo[step * STEP + i]]
        top = jnp.max(scores, axis=0, keepdims=True)
        weights = jnp.exp(scores - top)
        totals = jnp.sum(weights, axis=0, keepdims=True)
        att = (tn(values, weights.astype(BF16)) / totals).astype(BF16)
        att_ref[cols, :] = att
        log_ref[0, i : i + 1, :] = top + jnp.log(totals)
        low_acc[...] += nn(down[:, cols], att)
        at = pl.ds(pl.multiple_of((step * STEP + i) * HEAD, HEAD), HEAD)
        grads_ref[combo[last], :, at] = nt(grad_low[...], att).astype(BF16)

    @pl.when(step == pl.num_programs(0) - 1)
    def _():
        low = low_acc[...].astype(BF16)
        low_ref[...] = low
        grads_ref[1 - combo[last]] = (ADAPTER * nn(low, upstream[...])).astype(BF16)


def backward_kernel(n_slots, combo, query, *refs):
    slots = [refs[3 * i : 3 * i + 3] for i in range(n_slots)]
    bias, att, grad, extra, log_total, grad_query = refs[3 * n_slots : 3 * n_slots + 6]
    terms = refs[3 * n_slots + 6 :]
    step = pl.program_id(0)
    for i in range(STEP):
        cols = slice(i * HEAD, (i + 1) * HEAD)
        keys, values = slot_keys(slots, cols)
        here = query[:, cols]
        scores = nt(keys, here) * SCALE + bias[combo[step * STEP + i]]
        probs = jnp.exp(scores - log_total[0, i : i + 1, :])
        grad_att = (grad[cols, :].astype(F32) + extra[cols, :]).astype(BF16)
        inner = jnp.sum(
            grad_att.astype(F32) * att[cols, :].astype(F32), axis=0, keepdims=True
        )
        value_terms = nt(probs.astype(BF16), grad_att).astype(BF16)
        grad_scores = (probs * (nn(values, grad_att) - inner)).astype(BF16)
        key_terms = (nn(grad_scores, here) * SCALE).astype(BF16)
        grad_query[:, cols] = (tn(grad_scores, keys) * SCALE).astype(BF16)
        for s in range(n_slots):
            core, rim = terms[2 * s : 2 * s + 2]
            at = s * SLOT
            core[:TILE, cols] = key_terms[at : at + TILE]
            core[TILE:, cols] = value_terms[at : at + TILE]
            rim[:RIM, cols] = key_terms[at + TILE : at + SLOT]
            rim[RIM:, cols] = value_terms[at + TILE : at + SLOT]


def column_block(rows):
    return pl.BlockSpec((rows, STEP * HEAD), lambda step, *_: (0, step))


def row_block():
    return pl.BlockSpec((STEP * HEAD, TILE), lambda step, *_: (step, 0))


def whole(shape):
    return pl.BlockSpec(shape, lambda *_: (0,) * len(shape))


def head_call(kernel, steps, in_specs, out_specs, out_shape, scratch):
    call = pl.pallas_call(
        kernel,
        grid_spec=pltpu.PrefetchScalarGridSpec(
            num_scalar_prefetch=1,
            grid=(steps,),
            in_specs=in_specs,
            out_specs=out_specs,
            scratch_shapes=scratch,
        ),
        out_shape=out_shape,
        compiler_params=pltpu.CompilerParams(
            dimension_semantics=("arbitrary",), vmem_limit_bytes=14 * 1024 * 1024
        ),
        cost_estimate=pl.CostEstimate(flops=1000, bytes_accessed=1000, transcendentals=0),
    )

    def from_hbm(scalars, *arrays):
        return call(scalars, *in_hbm(arrays[:3]), *arrays[3:])

    return from_hbm


def in_hbm(arrays):
    return [pltpu.with_memory_space_constraint(array, pltpu.HBM) for array in arrays]


def slot_specs(n_slots):
    return [column_block(TILE), column_block(TILE), column_block(2 * RIM)] * n_slots


def attend(combo, query, slots, bias, down, grad_low, upstream):
    tokens, width = query.shape
    heads = width // HEAD
    rank = down.shape[0]
    n_slots = len(slots)
    return head_call(
        functools.partial(forward_kernel, n_slots),
        heads // STEP,
        [column_block(tokens)]
        + slot_specs(n_slots)
        + [
            whole(bias.shape),
            column_block(rank),
            whole(grad_low.shape),
            whole(upstream.shape),
        ],
        [
            row_block(),
            pl.BlockSpec((1, STEP, tokens), lambda step, *_: (step, 0, 0)),
            whole((2, rank, width)),
            whole((rank, tokens)),
        ],
        [
            jax.ShapeDtypeStruct((width, tokens), BF16),
            jax.ShapeDtypeStruct((heads // STEP, STEP, tokens), F32),
            jax.ShapeDtypeStruct((2, rank, width), BF16),
            jax.ShapeDtypeStruct((rank, tokens), BF16),
        ],
        [pltpu.VMEM((rank, tokens), F32)],
    )(combo, query, *[part for slot in slots for part in slot], bias, down, grad_low, upstream)


def attend_back(combo, query, slots, bias, att, grad, extra, log_total):
    tokens, width = query.shape
    heads = width // HEAD
    n_slots = len(slots)
    out = head_call(
        functools.partial(backward_kernel, n_slots),
        heads // STEP,
        [column_block(tokens)]
        + slot_specs(n_slots)
        + [
            whole(bias.shape),
            row_block(),
            row_block(),
            row_block(),
            pl.BlockSpec((1, STEP, tokens), lambda step, *_: (step, 0, 0)),
        ],
        [column_block(tokens)] + [column_block(2 * TILE), column_block(2 * RIM)] * n_slots,
        [jax.ShapeDtypeStruct((tokens, width), BF16)]
        + [
            jax.ShapeDtypeStruct((2 * TILE, width), BF16),
            jax.ShapeDtypeStruct((2 * RIM, width), BF16),
        ]
        * n_slots,
        [],
    )(
        combo, query, *[part for slot in slots for part in slot], bias, *in_hbm([att]), grad, extra,
        log_total,
    )
    return out[0], [out[1 + 2 * s : 3 + 2 * s] for s in range(n_slots)]


PLACES = [(x, y) for y in range(2) for x in range(2)]
MEMBERS = [(x, y, c) for x, y in PLACES for c in range(2)]


def block_of(member, turn):
    x, y, c = member
    return turn * 8 + y * 4 + c * 2 + x


def plain_call(kernel, grid, in_specs, out_specs, out_shape, scratch):
    return pl.pallas_call(
        kernel,
        grid=grid,
        in_specs=in_specs,
        out_specs=out_specs,
        out_shape=out_shape,
        scratch_shapes=scratch,
        compiler_params=pltpu.CompilerParams(
            dimension_semantics=("arbitrary",) * len(grid), vmem_limit_bytes=14 * 1024 * 1024
        ),
        cost_estimate=pl.CostEstimate(flops=1000, bytes_accessed=1000, transcendentals=0),
    )


def spread_kernel(turns, me, rows_ref, *outs):
    size = rows_ref.shape[0] // (8 * turns)
    for number, member in enumerate(MEMBERS):
        for turn in range(turns):
            at = pl.multiple_of((block_of(member, turn) ^ me[0]) * size, size)
            outs[number % 2][number // 2, turn * size : (turn + 1) * size, :] = rows_ref[
                pl.ds(at, size), :
            ]


def collect_kernel(turns, me, *refs):
    out = refs[-1]
    size = out.shape[0] // (8 * turns)
    for number, member in enumerate(MEMBERS):
        part = refs[number // 2].at[number % 2]
        for turn in range(turns):
            at = pl.multiple_of((block_of(member, turn) ^ me[0]) * size, size)
            out[pl.ds(at, size), :] = part[turn * size : (turn + 1) * size, :]


SCALARS = pl.BlockSpec(memory_space=pltpu.SMEM)


def spread(rows, me, turns):
    total, tokens = rows.shape
    size = total // (8 * turns)
    part = (4, turns * size, tokens)
    if size % 16:
        blocks = rows.reshape(8 * turns, size, tokens)
        order = [[block_of((x, y, c), t) for x, y in PLACES for t in range(turns)] for c in range(2)]
        return [jnp.take(blocks, me ^ jnp.array(o), axis=0).reshape(part) for o in order]
    return plain_call(
        functools.partial(spread_kernel, turns),
        (1,),
        [SCALARS, whole(rows.shape)],
        [whole(part)] * 2,
        [jax.ShapeDtypeStruct(part, rows.dtype)] * 2,
        [],
    )(me[None], *in_hbm([rows]))


def collect(parts, me, turns):
    _, rows, tokens = parts[0].shape
    size = rows // turns
    total = 8 * rows
    if size % 16:
        every = [parts[number // 2][number % 2] for number in range(8)]
        blocks = jnp.concatenate(every).reshape(8 * turns, size, tokens)
        slot = {block_of(m, t): i * turns + t for i, m in enumerate(MEMBERS) for t in range(turns)}
        order = jnp.array([slot[b] for b in range(8 * turns)])
        return jnp.take(blocks, order[me ^ jnp.arange(8 * turns)], axis=0).reshape(total, tokens)
    return plain_call(
        functools.partial(collect_kernel, turns),
        (1,),
        [SCALARS] + [whole(part.shape) for part in parts],
        whole((total, tokens)),
        jax.ShapeDtypeStruct((total, tokens), parts[0].dtype),
        [],
    )(me[None], *parts)


def edge_kernel(where, keys, values, to_left, to_right, edge):
    mark = lax.broadcasted_iota(jnp.int32, (32, TILE), 0)
    cell = lax.broadcasted_iota(jnp.int32, (32, TILE), 1)
    side = jnp.where(mark < 8, mark * TCOLS, (mark - 8) * TCOLS + TCOLS - 1)
    source = jnp.where(mark < 16, side, where[0] * TCOLS + mark - 16)
    pick = (source == cell).astype(F32).astype(BF16)
    key_edges = nn(pick, keys[...])
    value_edges = nn(pick, values[...])
    to_left[...] = jnp.concatenate([key_edges[:8], value_edges[:8]]).astype(BF16)
    to_right[...] = jnp.concatenate([key_edges[8:16], value_edges[8:16]]).astype(BF16)
    edge[...] = jnp.concatenate([key_edges[16:], value_edges[16:]]).astype(BF16)


def outer_kernel(where, left, right, edge, outer):
    sides = [left[...].astype(F32), right[...].astype(F32)]
    last = where[0] == ROWS - 1
    corners = [
        jnp.where(last, side[at + ROWS - 1 : at + ROWS], side[at : at + 1])
        for at in (0, 8)
        for side in sides
    ]
    blank = jnp.zeros((4, edge.shape[1]), F32)
    outer[...] = jnp.concatenate([edge[...].astype(F32), *corners, blank]).astype(BF16)


def rim_kernel(left, right, outer, rim):
    sides = [left[...].astype(F32), right[...].astype(F32)]
    far = outer[...].astype(F32)
    blank = jnp.zeros((14, far.shape[1]), F32)
    rim[...] = jnp.concatenate(
        [
            sides[0][:8], sides[1][:8], far[:16], far[32:34], blank,
            sides[0][8:], sides[1][8:], far[16:32], far[34:36], blank,
        ]
    ).astype(BF16)


def column_call(kernel, scalars, blocks, out_rows):
    width = blocks[0].shape[1]
    step = width // 4
    out = plain_call(
        kernel,
        (4,),
        [SCALARS] * len(scalars)
        + [pl.BlockSpec((block.shape[0], step), lambda j: (0, j)) for block in blocks],
        [pl.BlockSpec((rows, step), lambda j: (0, j)) for rows in out_rows],
        [jax.ShapeDtypeStruct((rows, width), BF16) for rows in out_rows],
        [],
    )(*scalars, *blocks)
    return out if len(out_rows) > 1 else out[0]


def pack_kernel(here, there, *outs):
    for place, out in enumerate(outs):
        out[0] = here[place]
        out[1] = there[place]


def pack(here, there):
    _, rows, tokens = here.shape
    return plain_call(
        pack_kernel,
        (1,),
        [whole(here.shape)] * 2,
        [whole((2, rows, tokens))] * 4,
        [jax.ShapeDtypeStruct((2, rows, tokens), BF16)] * 4,
        [],
    )(here, there)


def weight_block(refs):
    return jnp.concatenate([ref[...] for ref in refs], axis=0) if len(refs) > 1 else refs[0][...]


def grad_kernel(n_parts, *refs):
    weights, tokens, outs, acc = refs[:n_parts], refs[n_parts : n_parts + 8], refs[-3:-1], refs[-1]
    step = pl.program_id(0)

    @pl.when(step == 0)
    def _():
        acc[...] = jnp.zeros_like(acc)

    weight = weight_block(weights)
    for place in range(4):
        here = jnp.concatenate([tokens[2 * place][...], tokens[2 * place + 1][...]], axis=0)
        acc[place] += nt(weight, here)

    @pl.when(step == pl.num_programs(0) - 1)
    def _():
        for place in range(4):
            outs[0][place] = acc[place, :, :TILE].astype(BF16)
            outs[1][place] = acc[place, :, TILE:].astype(BF16)


def grad_parts(weights, tokens):
    rows = sum(part.shape[0] for part in weights)
    width = weights[0].shape[1]
    step = 512
    return plain_call(
        functools.partial(grad_kernel, len(weights)),
        (width // step,),
        [pl.BlockSpec((part.shape[0], step), lambda k: (0, k)) for part in (*weights, *tokens)],
        [whole((4, rows, TILE))] * 2,
        [jax.ShapeDtypeStruct((4, rows, TILE), BF16)] * 2,
        [pltpu.VMEM((4, rows, 2 * TILE), F32)],
    )(*in_hbm(weights), *in_hbm(tokens))


def project_kernel(n_parts, core, split, *refs):
    weights, parts, rest = refs[:n_parts], refs[n_parts : n_parts + 4], refs[n_parts + 4 :]
    turned = rest[-1]
    step = pl.program_id(0)

    @pl.when(step == 0)
    def _():
        for place in range(4):
            turned[place * TILE : (place + 1) * TILE, :] = parts[place][core].T

    result = nn(turned[...], weight_block(weights))
    blocks = [result[place * TILE : (place + 1) * TILE] for place in range(4)]
    second = step >= split
    if core:
        out = rest[0]
        for slot, place in enumerate((0, jnp.where(second, 2, 1), jnp.where(second, 1, 2), 3)):
            out[0, place] = blocks[slot].astype(BF16)
    else:
        added, keep, send_first, send_second = rest[:-1]

        def total(place, slot):
            return (blocks[place] + added[0, slot].astype(F32)).astype(BF16)

        @pl.when(step < split)
        def _():
            for slot in range(2):
                keep[0, slot] = total(slot, slot)
                send_first[slot] = total(2 + slot, 2 + slot)

        @pl.when(second)
        def _():
            for slot in range(2):
                keep[0, slot] = total(2 * slot, slot)
                send_second[slot] = total(2 * slot + 1, 2 + slot)


def project(weights, parts, core, added=()):
    rows = sum(part.shape[0] for part in weights)
    width = weights[0].shape[1]
    step = 512
    split = width // 2 // step
    every = pl.BlockSpec((1, 4, TILE, step), lambda j: (j // split, 0, 0, j % split))
    sent = (2, TILE, width // 2)
    near = [
        pl.BlockSpec((1, 2, TILE, step), lambda j: (j // split, 0, 0, j % split)),
        pl.BlockSpec((2, TILE, step), lambda j: (0, 0, jnp.minimum(j, split - 1))),
        pl.BlockSpec((2, TILE, step), lambda j: (0, 0, jnp.maximum(j - split, 0))),
    ]
    return plain_call(
        functools.partial(project_kernel, len(weights), core, split),
        (width // step,),
        [pl.BlockSpec((part.shape[0], step), lambda j: (0, j)) for part in weights]
        + [whole(part.shape) for part in parts]
        + [every] * len(added),
        every if core else near,
        jax.ShapeDtypeStruct((2, 4, TILE, width // 2), BF16)
        if core
        else [jax.ShapeDtypeStruct(shape, BF16) for shape in ((2, *sent), sent, sent)],
        [pltpu.VMEM((4 * TILE, rows), BF16)],
    )(*in_hbm(weights), *parts, *added)


def bias_kernel(shifts, frames, where, bias):
    band_idx, col_idx, frame_idx = where[0], where[1], where[2]
    at = lax.broadcasted_iota(jnp.int32, (SLOT, TILE), 0)
    query = lax.broadcasted_iota(jnp.int32, (SLOT, TILE), 1)
    rim = at - TILE
    outer = jnp.where(band_idx == 0, ROWS, -1)
    row = jnp.where(rim < 0, at // TCOLS, jnp.where(rim < 16, rim % ROWS, outer))
    col = jnp.where(rim < 16, jnp.where(rim < 8, -1, TCOLS), rim - 16)
    col = jnp.where(rim < 0, at % TCOLS, jnp.where(rim < 32, col, (rim - 32) * (TCOLS + 1) - 1))
    across = col_idx * TCOLS + col
    near = (jnp.abs(col - query % TCOLS) <= 1) & (rim < 34)
    near &= (across >= 0) & (across < CTILES * TCOLS)
    gap = jnp.abs(row - query // TCOLS)
    for row_reach in range(2):
        space = jnp.where(near & (gap <= row_reach), 0.0, -1e30)
        for slot, shift in enumerate(shifts):
            there = (frame_idx + shift >= 0) & (frame_idx + shift < frames) | (frames == 2)
            for frame_reach in range(2):
                time = jnp.where(there & (abs(shift) <= frame_reach), 0.0, -1e30)
                bias[2 * frame_reach + row_reach, slot * SLOT : (slot + 1) * SLOT, :] = (
                    jnp.minimum(space, time)
                )


def window_bias(shifts, frames, where):
    shape = (4, len(shifts) * SLOT, TILE)
    return plain_call(
        functools.partial(bias_kernel, shifts, frames),
        (1,),
        [SCALARS],
        whole(shape),
        jax.ShapeDtypeStruct(shape, F32),
        [],
    )(where)


def permute(block, route):
    return lax.ppermute(block, "tensor", route)


def swap(block, group_bit, bits):
    groups, devices = lax.axis_size("groups"), lax.axis_size("tensor")
    return lax.ppermute(
        block,
        ("groups", "tensor"),
        [
            (g * devices + i, (g ^ group_bit) * devices + (i ^ bits))
            for g in range(groups)
            for i in range(devices)
        ],
    )


def after(value, *done):
    return lax.optimization_barrier((value, done))[0]


def exchange(like, other, until):
    pairs = pack(like, swap(other, 0, 1))
    got = [swap(pair, x, 2 * y) for (x, y), pair in zip(PLACES[1:], pairs[1:])]
    return [pairs[0], *after(got, until)]


def on_device(
    input_queries,
    input_keys,
    input_values,
    output_matrix,
    adapter_down_weight,
    adapter_up_weight,
    upstream,
    window_frame_reach,
    window_row_reach,
):
    devices = lax.axis_size("tensor")
    frames = devices // (BANDS * CTILES)
    position = lax.axis_index("tensor")
    frame_idx = position % frames
    col_idx = position // frames % CTILES
    band_idx = position // (frames * CTILES)
    everyone = range(devices)
    to_right = [(i, i + frames) for i in everyone if i // frames % CTILES < CTILES - 1]
    to_left = [(j, i) for i, j in to_right]
    to_band = [(i, (i + devices // BANDS) % devices) for i in everyone]
    if frames == 1:
        shifts, to_frame = [0], []
    elif frames == 2:
        shifts, to_frame = [0, 1], [[(i, i ^ 1) for i in everyone]]
    else:
        later = [(i, i + 1) for i in everyone if i % frames < frames - 1]
        shifts, to_frame = [0, -1, 1], [later, [(j, i) for i, j in later]]
    edge_row = jnp.where(band_idx == 0, ROWS - 1, 0)
    second = position % 2
    combo = jnp.append(2 * window_frame_reach + window_row_reach, second)

    edge_at = edge_row[None]
    leftmost, rightmost, edge = column_call(
        edge_kernel, [edge_at], [input_keys, input_values], [16, 16, 32]
    )
    right = permute(leftmost, to_left)
    left = permute(rightmost, to_right)
    core_slots = [
        (permute(input_keys, route), permute(input_values, route)) for route in to_frame
    ]
    tokens = {(0, 0, 0): upstream, (0, 0, 1): swap(upstream, 0, 1)}
    group = lax.axis_index("groups")
    turns = devices // 4
    me = position * 2 + group
    share = output_matrix.shape[0] // 2
    own = lax.dynamic_slice_in_dim(output_matrix, group * share, share)
    top, low_rows = own[: share // 2], own[share // 2 :]
    bias = window_bias(shifts, frames, jnp.stack([band_idx, col_idx, frame_idx]))
    down = adapter_down_weight.T
    grad_low = (ADAPTER * nt(adapter_up_weight, upstream)).astype(BF16)
    extra = tn(down, grad_low)
    start = (left, right, core_slots, tokens[0, 0, 1], own, top, low_rows)
    start = (*start, bias, grad_low, extra, combo)
    to_outer = column_call(outer_kernel, [edge_at], [after(left, start), right, edge], [40])

    outer = permute(to_outer, to_band)
    for x, y in ((1, 0), (0, 1)):
        tokens[x, y, 0] = swap(after(upstream, to_outer), x, 2 * y)
    opened = (outer, tokens[1, 0, 0], tokens[0, 1, 0])
    if turns == 4:
        one, two = swap(after(own, to_outer), 0, 4), swap(after(top, to_outer), 0, 8)
        opened = (*opened, one, two)
        three = swap(after(two, opened), 0, 4)
        two_low = swap(after(low_rows, opened), 0, 8)
        fetched = [three, two_low]
    else:
        found = {0: own}
        for bit in [1 << b for b in reversed(range(turns.bit_length() - 1))]:
            found |= {t ^ bit: swap(block, 0, 4 * bit) for t, block in found.items()}
        weights = [found[t] for t in range(turns)]
        fetched = []
    tokens[1, 1, 0] = swap(after(tokens[0, 1, 0], opened), 1, 0)
    for x, y in ((1, 0), (0, 1)):
        tokens[x, y, 1] = swap(after(tokens[x, y, 0], opened), 0, 1)
    fetched.append(tokens[1, 1, 0])

    rim = column_call(rim_kernel, [], [after(left, opened), right, outer], [2 * RIM])
    slots = [(input_keys, input_values, rim)] + [
        (*core, permute(rim, route)) for core, route in zip(core_slots, to_frame)
    ]
    att, log_total, grads, low = attend(
        combo,
        after(input_queries, extra, tokens[1, 0, 1], tokens[0, 1, 1]),
        slots,
        bias, down, grad_low, upstream
    )

    att, log_total, grads, low = after((att, log_total, grads, low), fetched)

    att_like, att_other = spread(att, me, turns)
    got = permute(grads[1], [(i, i ^ 1) for i in everyone])
    part = grads[0].astype(F32) + got.astype(F32)

    def add_over(part, bit, until):
        part = part.astype(BF16)
        got = permute(part, [(i, i ^ bit) for i in everyone])
        return part.astype(F32) + after(got, until).astype(F32)

    bits = [1 << b for b in range(1, devices.bit_length() - 1)]
    if turns == 4:
        three_low = swap(after(two_low, att), 0, 4)
        weights = [own, one, two, two_low, three, three_low]
    if share % 16:
        weights = [jnp.concatenate(weights)]
    att_packed = pack(att_like, swap(att_other, 0, 1))
    att_got = [swap(pair, x, 2 * y) for (x, y), pair in zip(PLACES[1:], att_packed[1:])]
    tokens[1, 1, 1] = swap(after(tokens[1, 1, 0], part, att_packed), 0, 1)
    grads_like, grads_other = grad_parts(
        [after(weights[0], att), *weights[1:]], [tokens[m] for m in MEMBERS]
    )
    att_of = [att_packed[0], *after(att_got, grads_like)]
    far = project(weights, att_of, 1)
    near, first, second_half = project(weights, att_of, 0, (swap(far, 0, 1),))
    grads_of = exchange(grads_like, grads_other, near)
    first, second_half = after((first, second_half), grads_of)
    first, second_half = swap(first, 0, 2), swap(second_half, 1, 0)
    over_two, over_one = bits[-1], bits[1:-1]
    part = add_over(after(part, grads_like), over_two, near)
    grads_of[0] = after(grads_of[0], part)
    grad_att = collect(grads_of, me, turns)
    grad_query, terms = attend_back(
        combo, after(input_queries, near), slots, bias, att, grad_att, extra, log_total
    )
    for bit in over_one:
        part = add_over(part, bit, terms)
    grad_query, terms = after((grad_query, terms), first, second_half, part)
    first = near[0].astype(F32) + after(first, grad_query).astype(F32)
    second_half = near[1].astype(F32) + after(second_half, grad_query).astype(F32)
    core, rim_terms = terms[0]
    rim_terms = rim_terms.astype(F32)
    back = [[(j, i) for i, j in route] for route in to_frame]
    for (_, sent), route in zip(terms[1:], back):
        rim_terms += permute(sent, route).astype(F32)
    core_terms = [core] + [permute(sent, route) for (sent, _), route in zip(terms[1:], back)]
    rim_terms = after(rim_terms, core_terms)
    keys_out, values_out = rim_terms[:RIM], rim_terms[RIM:]
    outer = permute(
        jnp.concatenate(
            [keys_out[16:32], values_out[16:32], keys_out[32:34], values_out[32:34]]
        ).astype(BF16),
        to_band,
    )
    part = add_over(part, bits[0], outer)
    last_rows = swap(first[1].astype(BF16), 1, 0), swap(second_half[1].astype(BF16), 0, 2)
    last_rows = after(last_rows, outer)
    outer = after(outer, last_rows)
    first = first[0] + last_rows[0].astype(F32)
    second_half = second_half[0] + last_rows[1].astype(F32)
    projected = (
        jnp.concatenate([first, second_half], axis=1) + ADAPTER * tn(low, adapter_up_weight)
    ).astype(BF16)

    part = part.astype(BF16)
    other = permute(part, [(i, i ^ 1) for i in everyone])
    grad_down = jnp.where(second == 0, part, other).astype(F32).T
    grad_up = jnp.where(second == 0, other, part).astype(F32)

    at_edge = (jnp.arange(ROWS)[:, None] == edge_row).astype(F32)
    outer_corners = outer[32:].astype(F32)

    def side(number):
        at = 8 * number
        return jnp.concatenate(
            [
                keys_out[at : at + 8] + at_edge * outer_corners[number],
                values_out[at : at + 8] + at_edge * outer_corners[2 + number],
            ]
        ).astype(BF16)

    from_right = permute(side(0), to_left)
    from_left = permute(side(1), to_right)
    cell = jnp.arange(TILE, dtype=jnp.int32)
    mark = jnp.arange(32, dtype=jnp.int32)
    source = jnp.where(
        mark < 8,
        mark * TCOLS,
        jnp.where(mark < 16, (mark - 8) * TCOLS + TCOLS - 1, edge_row * TCOLS + mark - 16),
    )
    pick = (source[:, None] == cell[None, :]).astype(BF16)
    gathered = [
        jnp.concatenate([from_left[at : at + 8], from_right[at : at + 8], outer[row : row + 16]])
        for at, row in ((0, 0), (8, 16))
    ]
    grad_key, grad_value = (
        (
            sum(block[rows].astype(F32) for block in core_terms) + tn(pick, got)
        ).astype(BF16)
        for rows, got in ((slice(0, TILE), gathered[0]), (slice(TILE, None), gathered[1]))
    )
    return (projected, grad_query, grad_key, grad_value, grad_down, grad_up)


def solution(mesh):
    tokens = P(("groups", "tensor"), None)
    return jax.shard_map(
        on_device,
        mesh=mesh,
        in_specs=(tokens, tokens, tokens, P("tensor", None), P(), P(), tokens, P(), P()),
        out_specs=(tokens, tokens, tokens, tokens, P("groups", None), P("groups", None)),
        check_vma=False,
    )
```

time: 197 us -> 173 us (0.88)
  waiting for transfers between devices: 96.5 us -> 48.9 us
  Pallas kernels: 22.1 us -> 48.3 us
  starting transfers between devices: 19.6 us -> 43.5 us
  matrix products: 27.2 us -> 5.86 us
  between operations: 14.5 us -> 1.28 us
  local copies, waits for them, and re-layouts: 8.25 us -> 16.2 us
    ppermute x16, waiting for transfers between devices: 95.8 us -> 25.1 us  [permute(): return lax.ppermute(block, 'tensor', route)]
    ppermute x0 -> x25, starting transfers between devices: none -> 27.4 us  [swap(): lax.ppermute(block, ('groups', 'tensor'), [(g * devices + i, (g ^ group_b...]
    pallas_call x2 -> x13, Pallas kernels: 22.1 us -> 48.3 us  [the longest x2 22.1 us: from_hbm(): return call(scalars, *in_hbm(arrays[:3]), *arrays[3:])]
    ppermute x0 -> x25, waiting for transfers between devices: none -> 23.7 us  [swap(): lax.ppermute(block, ('groups', 'tensor'), [(g * devices + i, (g ^ group_b...]
    dot_general x2 -> x1, matrix products: 10.9 us -> 0.39 us  [nt(): lax.dot_general(a, b, (((1,), (1,)), ((), ())), preferred_element_type=F32)]
    dot_general x5 -> x4, matrix products: 14.6 us -> 5.47 us  [tn(): lax.dot_general(a, b, (((0,), (0,)), ((), ())), preferred_element_type=F32)]
    unnamed x28 -> x74, local copies, waits for them, and re-layouts: 6.29 us -> 13.5 us
    convert_element_type x4 -> x1, other arithmetic: 4.22 us -> 0.1 us  [on_device(): part = part.astype(BF16)]
  transfers between devices with their start and end apart: 17 -> 41, of which waited for: 11 -> 14; matrix products, arithmetic and copies ran while one was open for 17% -> 8% of each run, Pallas kernels for 11% -> 24%
where the time goes in v2:
time: 173 us; the launch traced here: 171 us
  waiting for transfers between devices  48.9 us (28%)
  Pallas kernels  48.3 us (28%)
  starting transfers between devices  43.5 us (25%)
  local copies, waits for them, and re-layouts  16.2 us (9%)
  other arithmetic  7.16 us (4%)
  matrix products  5.86 us (3%)
    ppermute x25, starting transfers between devices, swap(): lax.ppermute(block, ('groups', 'tensor'), [(g * devices + i, (g ^ group_b...  27.4 us
    ppermute x16, waiting for transfers between devices, permute(): return lax.ppermute(block, 'tensor', route)  25.1 us
    ppermute x25, waiting for transfers between devices, swap(): lax.ppermute(block, ('groups', 'tensor'), [(g * devices + i, (g ^ group_b...  23.7 us
    pallas_call x2, Pallas kernels, from_hbm(): return call(scalars, *in_hbm(arrays[:3]), *arrays[3:])  22.1 us
    ppermute x16, starting transfers between devices, permute(): return lax.ppermute(block, 'tensor', route)  16.1 us
    unnamed x74, local copies, waits for them, and re-layouts  13.5 us
    pallas_call x2, Pallas kernels, project(): plain_call(functools.partial(project_kernel, len(weights), core, split),...  11.8 us
    pallas_call x1, Pallas kernels, grad_parts(): plain_call(functools.partial(grad_kernel, len(weights)), (width // step,)...  7.04 us
  transfers between devices with their start and end apart: 41, of which 14 were waited for; matrix products, arithmetic and copies ran while one was open for 8% of the time, Pallas kernels for 24%

profile of v2, /device:TPU:0, one launch (start us, length us, event | category | flops | bytes accessed | tf_op | source)
XLA Modules:
  0.0 171.1 jit_solution(1194119210382853330)
XLA Ops:
  1.3 1.1 copy-done.2
  2.4 1.1 copy-done.3
  3.5 1.9 %shard_map.136 = (bf16[16,3072]{1,0:T(8,128)(2,1)}, bf16[16,3072]{1,0:T(8,128)(2,1)}, bf16[32,3072]{1,0:T(8,128)(2,1)S(1)}) custom-call(s32[1]{0:T(128)} %bitcast.where, bf16[128,3072]{1,0:T(8,128)(2,1)S(1)} %copy-done.2, bf16[128,3072]{1,0:T(8,128)(2,1)S(1)} %copy-done.3), custom_call_target="tpu_custom_call" | custom-call | flops 1000 | bytes 1000 | tf_op jit(solution)/shard_map/pallas_call | solution.py:338
  6.1 5.5 %collective-permute-start = (bf16[16,3072]{1,0:T(8,128)(2,1)}, bf16[16,3072]{1,0:T(8,128)(2,1)}, u32[]{:S(2)}, u32[]{:S(2)}) collective-permute-start(bf16[16,3072]{1,0:T(8,128)(2,1)} %get-tuple-element.75), channel_id=1, source_target_pairs={{0,2},{1,3},{2,4},{3,5},{4,6},{5,7},{8,10},{9,11},{10,12},{11,13},... | collective-permute-start | bytes 294920 | tf_op jit(solution)/shard_map/ppermute | solution.py:505
  11.6 1.3 collective-permute-start.1
  14.2 1.4 convolution_bitcast_fusion.refs_9_
  15.6 1.1 constant_dynamic-slice_fusion.2.refs_0_
  16.8 1.3 constant_dynamic-slice_fusion
  18.4 1.7 shard_map.138
  20.1 1.6 collective-permute-start.8
  21.7 2.5 %collective-permute-start.9 = (bf16[128,3072]{1,0:T(8,128)(2,1)S(1)}, bf16[128,3072]{1,0:T(8,128)(2,1)S(1)}, u32[]{:S(2)}, u32[]{:S(2)}) collective-permute-start(bf16[128,3072]{1,0:T(8,128)(2,1)S(1)} %copy-done.1), channel_id=1, source_target_pairs={{0,2},{1,3},{2,0},{3,1},{4,6},{5,7},{6,4},{7,5},{8,10},{9,11},{10,... | collective-permute-start | bytes 2359304 | tf_op jit(solution)/shard_map/ppermute | solution.py:510
  24.1 1.5 collective-permute-start.5
  25.6 2.6 %collective-permute-start.6 = (bf16[48,3072]{1,0:T(8,128)(2,1)S(1)}, bf16[48,3072]{1,0:T(8,128)(2,1)S(1)}, u32[]{:S(2)}, u32[]{:S(2)}) collective-permute-start(bf16[48,3072]{1,0:T(8,128)(2,1)S(1)} %get-tuple-element.80), channel_id=1, source_target_pairs={{0,8},{1,9},{2,10},{3,11},{4,12},{5,13},{6,14},{7,15},{8,0},{9,1},... | collective-permute-start | bytes 884744 | tf_op jit(solution)/shard_map/ppermute | solution.py:510
  28.5 21.4 %collective-permute-done.7.outer = bf16[40,3072]{1,0:T(8,128)(2,1)S(1)} collective-permute-done((bf16[40,3072]{1,0:T(8,128)(2,1)S(1)}, bf16[40,3072]{1,0:T(8,128)(2,1)S(1)}, u32[]{:S(2)}, u32[]{:S(2)}) %collective-permute-start.7) | collective-permute-done | bytes 245792 | tf_op jit(solution)/shard_map/ppermute | solution.py:505
  52.2 1.6 shard_map.139.refs_2_
  53.9 2.7 %collective-permute-start.11 = (bf16[48,3072]{1,0:T(8,128)(2,1)S(1)}, bf16[48,3072]{1,0:T(8,128)(2,1)S(1)}, u32[]{:S(2)}, u32[]{:S(2)}) collective-permute-start(bf16[48,3072]{1,0:T(8,128)(2,1)S(1)} %collective-permute-done.6.refs_2_), channel_id=1, source_target_pairs={{0,4},{1,5},{2,6},{3,7},{4,0},{5,1},{6,2},{7,3},{8,12},{9,13},{10,... | collective-permute-start | bytes 884744 | tf_op jit(solution)/shard_map/ppermute | solution.py:510
  56.6 1.6 collective-permute-start.10
  59.2 11.6 %shard_map.140 = (bf16[3072,128]{1,0:T(8,128)(2,1)S(1)}, f32[6,4,128]{2,1,0:T(4,128)S(1)}, bf16[2,64,3072]{2,1,0:T(8,128)(2,1)S(1)}, bf16[64,128]{1,0:T(8,128)(2,1)S(1)}) custom-call(s32[25]{0:T(128)S(1)} %pad_add_fusion.1.combo, bf16[128,3072]{1,0:T(8,128)(2,1)} %query.1, bf16[128,3072]{1,0:T(8,128)(2,1)} %refs_0_.3, bf16[128,3072]{1,0:T(8,128)(2,1)} %refs_1_.3, ...), custom_call_target="tpu_custom_call" | custom-call | flops 1000 | bytes 1000 | tf_op jit(solution)/shard_map/pallas_call | solution.py:137
  71.7 1.3 collective-permute-done.10.refs_3_
  74.0 1.3 shard_map.141
  75.8 1.2 convert_add_fusion.3
  78.2 1.0 collective-permute-start.18
  79.8 1.9 %collective-permute-start.20 = (bf16[2,384,128]{2,1,0:T(8,128)(2,1)S(1)}, bf16[2,384,128]{2,1,0:T(8,128)(2,1)S(1)}, u32[]{:S(2)}, u32[]{:S(2)}) collective-permute-start(bf16[2,384,128]{2,1,0:T(8,128)(2,1)S(1)} %get-tuple-element.99), channel_id=1, source_target_pairs={{0,18},{1,19},{2,16},{3,17},{4,22},{5,23},{6,20},{7,21},{8,26},{9,... | collective-permute-start | bytes 589832 | tf_op jit(solution)/shard_map/ppermute | solution.py:510
  81.7 5.0 %collective-permute-done.16.refs_5_ = bf16[48,3072]{1,0:T(8,128)(2,1)S(1)} collective-permute-done((bf16[48,3072]{1,0:T(8,128)(2,1)S(1)}, bf16[48,3072]{1,0:T(8,128)(2,1)S(1)}, u32[]{:S(2)}, u32[]{:S(2)}) %collective-permute-start.16) | collective-permute-done | bytes 294944 | tf_op jit(solution)/shard_map/ppermute | solution.py:510
  88.3 7.0 %shard_map.143 = (bf16[4,384,128]{2,1,0:T(8,128)(2,1)S(1)}, bf16[4,384,128]{2,1,0:T(8,128)(2,1)S(1)}) custom-call(bf16[96,3072]{1,0:T(8,128)(2,1)} %copy-done.21, bf16[96,3072]{1,0:T(8,128)(2,1)} %copy-done.22, bf16[48,3072]{1,0:T(8,128)(2,1)} %copy-done.23, bf16[48,3072]{1,0:T(8,128)(2,1)} %copy-done.25, bf16[48,3072]{1,0:T(8,128)(2,1)} %copy-done.24, ...), custom_call_target="tpu_custom_call" | custom-call | flops 1000 | bytes 1000 | tf_op jit(solution)/shard_map/pallas_call | solution.py:396
  95.4 5.3 %shard_map.144 = bf16[2,4,128,1536]{3,2,1,0:T(8,128)(2,1)S(1)} custom-call(bf16[96,3072]{1,0:T(8,128)(2,1)} %copy-done.21, bf16[96,3072]{1,0:T(8,128)(2,1)} %copy-done.22, bf16[48,3072]{1,0:T(8,128)(2,1)} %copy-done.23, bf16[48,3072]{1,0:T(8,128)(2,1)} %copy-done.25, bf16[48,3072]{1,0:T(8,128)(2,1)} %copy-done.24, bf16[48,3072]{1,0:T(8,128)(2,1)} %copy-done.27, ...), custom_call_target="tpu_custom_call" | custom-call | flops 1000 | bytes 1000 | tf_op jit(solution)/shard_map/pallas_call | solution.py:454
  101.7 5.3 %collective-permute-done.24.there = bf16[4,384,128]{2,1,0:T(8,128)(2,1)S(1)} collective-permute-done((bf16[4,384,128]{2,1,0:T(8,128)(2,1)S(1)}, bf16[4,384,128]{2,1,0:T(8,128)(2,1)S(1)}, u32[]{:S(2)}, u32[]{:S(2)}) %collective-permute-start.24) | collective-permute-done | bytes 393248 | tf_op jit(solution)/shard_map/ppermute | solution.py:510
  107.0 1.6 collective-permute-start.25
  109.2 1.4 collective-permute-start.27
  110.6 6.6 %shard_map.145 = (bf16[2,2,128,1536]{3,2,1,0:T(8,128)(2,1)S(1)}, bf16[2,128,1536]{2,1,0:T(8,128)(2,1)}, bf16[2,128,1536]{2,1,0:T(8,128)(2,1)}) custom-call(bf16[96,3072]{1,0:T(8,128)(2,1)} %copy-done.21, bf16[96,3072]{1,0:T(8,128)(2,1)} %copy-done.22, bf16[48,3072]{1,0:T(8,128)(2,1)} %copy-done.23, bf16[48,3072]{1,0:T(8,128)(2,1)} %copy-done.25, ...), custom_call_target="tpu_custom_call" | custom-call | flops 1000 | bytes 1000 | tf_op jit(solution)/shard_map/pallas_call | solution.py:454
  117.2 1.2 copy-done.9
  121.5 1.0 collective-permute-start.30
  123.6 1.0 copy-done.16
  126.5 10.5 %shard_map.148 = (bf16[128,3072]{1,0:T(8,128)(2,1)}, bf16[256,3072]{1,0:T(8,128)(2,1)S(1)}, bf16[96,3072]{1,0:T(8,128)(2,1)S(1)}, bf16[256,3072]{1,0:T(8,128)(2,1)S(1)}, bf16[96,3072]{1,0:T(8,128)(2,1)S(1)}) custom-call(s32[25]{0:T(128)S(1)} %pad_add_fusion.1.combo, bf16[128,3072]{1,0:T(8,128)(2,1)} %query.1, bf16[128,3072]{1,0:T(8,128)(2,1)} %refs_0_.3, ...), custom_call_target="tpu_custom_call" | custom-call | flops 1000 | bytes 1000 | tf_op jit(solution)/shard_map/pallas_call | solution.py:137
  137.1 2.3 %collective-permute-done.28 = bf16[2,128,1536]{2,1,0:T(8,128)(2,1)} collective-permute-done((bf16[2,128,1536]{2,1,0:T(8,128)(2,1)}, bf16[2,128,1536]{2,1,0:T(8,128)(2,1)}, u32[]{:S(2)}, u32[]{:S(2)}) %collective-permute-start.28) | collective-permute-done | bytes 786464 | tf_op jit(solution)/shard_map/ppermute | solution.py:510
  140.3 1.8 %convert_add_fusion.1 = (f32[2,128,1536]{2,1,0:T(8,128)S(1)}, f32[2,128,1536]{2,1,0:T(8,128)S(1)}) fusion(bf16[2,128,1536]{2,1,0:T(8,128)(2,1)} %collective-permute-done.28, bf16[2,2,128,1536]{3,2,1,0:T(8,128)(2,1)S(1)} %copy-done.10, bf16[2,128,1536]{2,1,0:T(8,128)(2,1)} %collective-permute-done.30), kind=kLoop, calls=%fused_computation.5 | loop fusion | flops 2359296 | bytes 6291456 | tf_op jit(solution)/shard_map/add | solution.py:658
  142.1 1.6 collective-permute-start.32
  143.8 1.5 collective-permute-start.33
  145.9 1.2 fusion.28
  147.9 5.3 %collective-permute-done.32 = bf16[128,1536]{1,0:T(8,128)(2,1)S(1)} collective-permute-done((bf16[128,1536]{1,0:T(8,128)(2,1)S(1)}, bf16[128,1536]{1,0:T(8,128)(2,1)S(1)}, u32[]{:S(2)}, u32[]{:S(2)}) %collective-permute-start.32) | collective-permute-done | bytes 393248 | tf_op jit(solution)/shard_map/ppermute | solution.py:510
  153.2 2.6 %collective-permute-done.33 = bf16[128,1536]{1,0:T(8,128)(2,1)S(1)} collective-permute-done((bf16[128,1536]{1,0:T(8,128)(2,1)S(1)}, bf16[128,1536]{1,0:T(8,128)(2,1)S(1)}, u32[]{:S(2)}, u32[]{:S(2)}) %collective-permute-start.33) | collective-permute-done | bytes 393248 | tf_op jit(solution)/shard_map/ppermute | solution.py:510
  155.8 3.0 %collective-permute-done.36 = bf16[36,3072]{1,0:T(8,128)(2,1)S(1)} collective-permute-done((bf16[36,3072]{1,0:T(8,128)(2,1)S(1)}, bf16[36,3072]{1,0:T(8,128)(2,1)S(1)}, u32[]{:S(2)}, u32[]{:S(2)}) %collective-permute-start.36) | collective-permute-done | bytes 221216 | tf_op jit(solution)/shard_map/ppermute | solution.py:505
  159.0 1.3 collective-permute-start.38
  160.3 4.6 %collective-permute-start.37 = (bf16[16,3072]{1,0:T(8,128)(2,1)S(1)}, bf16[16,3072]{1,0:T(8,128)(2,1)S(1)}, u32[]{:S(2)}, u32[]{:S(2)}) collective-permute-start(bf16[16,3072]{1,0:T(8,128)(2,1)S(1)} %pad_maximum_fusion.1), channel_id=1, source_target_pairs={{0,2},{1,3},{2,4},{3,5},{4,6},{5,7},{8,10},{9,11},{10,12},{11,13},... | collective-permute-start | bytes 294920 | tf_op jit(solution)/shard_map/ppermute | solution.py:505
  165.3 1.3 fusion.1
  167.1 1.4 add_convert_fusion.1
  168.5 1.4 add_convert_fusion
  169.9 1.2 select_convert_fusion
  (156 shorter events, 23.5 us)
Async XLA Ops:
  0.6 12.4 %copy-start = (bf16[64,3072]{1,0:T(8,128)(2,1)S(1)}, bf16[64,3072]{1,0:T(8,128)(2,1)}, u32[]{:S(2)}) copy-start(bf16[64,3072]{1,0:T(8,128)(2,1)} %param.14) | copy-start | bytes 1179652
  0.7 17.8 %collective-permute-start.2 = (bf16[128,3072]{1,0:T(8,128)(2,1)}, bf16[128,3072]{1,0:T(8,128)(2,1)}, u32[]{:S(2)}, u32[]{:S(2)}) collective-permute-start(bf16[128,3072]{1,0:T(8,128)(2,1)} %refs_0_.3), channel_id=1, source_target_pairs={{0,1},{1,0},{2,3},{3,2},{4,5},{5,4},{6,7},{7,6},{8,9},{9,8},{10,11... | collective-permute-start | bytes 2359304 | tf_op jit(solution)/shard_map/ppermute | solution.py:505
  1.2 17.2 %collective-permute-start.3 = (bf16[128,3072]{1,0:T(8,128)(2,1)}, bf16[128,3072]{1,0:T(8,128)(2,1)}, u32[]{:S(2)}, u32[]{:S(2)}) collective-permute-start(bf16[128,3072]{1,0:T(8,128)(2,1)} %refs_1_.3), channel_id=1, source_target_pairs={{0,1},{1,0},{2,3},{3,2},{4,5},{5,4},{6,7},{7,6},{8,9},{9,8},{10,11... | collective-permute-start | bytes 2359304 | tf_op jit(solution)/shard_map/ppermute | solution.py:505
  6.1 12.1 %collective-permute-start = (bf16[16,3072]{1,0:T(8,128)(2,1)}, bf16[16,3072]{1,0:T(8,128)(2,1)}, u32[]{:S(2)}, u32[]{:S(2)}) collective-permute-start(bf16[16,3072]{1,0:T(8,128)(2,1)} %get-tuple-element.75), channel_id=1, source_target_pairs={{0,2},{1,3},{2,4},{3,5},{4,6},{5,7},{8,10},{9,11},{10,12},{11,13},... | collective-permute-start | bytes 294920 | tf_op jit(solution)/shard_map/ppermute | solution.py:505
  11.6 6.8 %collective-permute-start.1 = (bf16[16,3072]{1,0:T(8,128)(2,1)}, bf16[16,3072]{1,0:T(8,128)(2,1)}, u32[]{:S(2)}, u32[]{:S(2)}) collective-permute-start(bf16[16,3072]{1,0:T(8,128)(2,1)} %get-tuple-element.76), channel_id=1, source_target_pairs={{2,0},{3,1},{4,2},{5,3},{6,4},{7,5},{10,8},{11,9},{12,10},{13,11},... | collective-permute-start | bytes 294920 | tf_op jit(solution)/shard_map/ppermute | solution.py:505
  12.9 5.5 %collective-permute-start.4 = (bf16[128,3072]{1,0:T(8,128)(2,1)S(1)}, bf16[128,3072]{1,0:T(8,128)(2,1)}, u32[]{:S(2)}, u32[]{:S(2)}) collective-permute-start(bf16[128,3072]{1,0:T(8,128)(2,1)S(1)} %copy-done.1), channel_id=1, source_target_pairs={{0,1},{1,0},{2,3},{3,2},{4,5},{5,4},{6,7},{7,6},{8,9},{9,8},{10,11... | collective-permute-start | bytes 2359304 | tf_op jit(solution)/shard_map/ppermute | solution.py:510
  16.8 41.5 %copy-start.21 = (bf16[96,3072]{1,0:T(8,128)(2,1)}, bf16[96,3072]{1,0:T(8,128)(2,1)S(1)}, u32[]{:S(2)}) copy-start(bf16[96,3072]{1,0:T(8,128)(2,1)S(1)} %constant_dynamic-slice_fusion.2.refs_0_) | copy-start | bytes 1769476
  16.8 42.4 %copy-start.11 = (bf16[3072,64]{0,1:T(8,128)(2,1)S(1)}, bf16[3072,64]{0,1:T(8,128)(2,1)}, u32[]{:S(2)}) copy-start(bf16[3072,64]{0,1:T(8,128)(2,1)} %param.13) | copy-start | bytes 1179652
  20.1 30.7 %collective-permute-start.8 = (bf16[128,3072]{1,0:T(8,128)(2,1)S(1)}, bf16[128,3072]{1,0:T(8,128)(2,1)S(1)}, u32[]{:S(2)}, u32[]{:S(2)}) collective-permute-start(bf16[128,3072]{1,0:T(8,128)(2,1)S(1)} %copy-done.1), channel_id=1, source_target_pairs={{0,16},{1,17},{2,18},{3,19},{4,20},{5,21},{6,22},{7,23},{8,24},{9,... | collective-permute-start | bytes 2359304 | tf_op jit(solution)/shard_map/ppermute | solution.py:510
  21.7 29.2 %collective-permute-start.9 = (bf16[128,3072]{1,0:T(8,128)(2,1)S(1)}, bf16[128,3072]{1,0:T(8,128)(2,1)S(1)}, u32[]{:S(2)}, u32[]{:S(2)}) collective-permute-start(bf16[128,3072]{1,0:T(8,128)(2,1)S(1)} %copy-done.1), channel_id=1, source_target_pairs={{0,2},{1,3},{2,0},{3,1},{4,6},{5,7},{6,4},{7,5},{8,10},{9,11},{10,... | collective-permute-start | bytes 2359304 | tf_op jit(solution)/shard_map/ppermute | solution.py:510
  24.1 26.7 %collective-permute-start.5 = (bf16[96,3072]{1,0:T(8,128)(2,1)S(1)}, bf16[96,3072]{1,0:T(8,128)(2,1)S(1)}, u32[]{:S(2)}, u32[]{:S(2)}) collective-permute-start(bf16[96,3072]{1,0:T(8,128)(2,1)S(1)} %constant_dynamic-slice_fusion.2.refs_0_), channel_id=1, source_target_pairs={{0,4},{1,5},{2,6},{3,7},{4,0},{5,1},{6,2},{7,3},{8,12},{9,13},{10,... | collective-permute-start | bytes 1769480 | tf_op jit(solution)/shard_map/ppermute | solution.py:510
  25.6 24.3 %collective-permute-start.6 = (bf16[48,3072]{1,0:T(8,128)(2,1)S(1)}, bf16[48,3072]{1,0:T(8,128)(2,1)S(1)}, u32[]{:S(2)}, u32[]{:S(2)}) collective-permute-start(bf16[48,3072]{1,0:T(8,128)(2,1)S(1)} %get-tuple-element.80), channel_id=1, source_target_pairs={{0,8},{1,9},{2,10},{3,11},{4,12},{5,13},{6,14},{7,15},{8,0},{9,1},... | collective-permute-start | bytes 884744 | tf_op jit(solution)/shard_map/ppermute | solution.py:510
  28.2 21.7 %collective-permute-start.7 = (bf16[40,3072]{1,0:T(8,128)(2,1)S(1)}, bf16[40,3072]{1,0:T(8,128)(2,1)S(1)}, u32[]{:S(2)}, u32[]{:S(2)}) collective-permute-start(bf16[40,3072]{1,0:T(8,128)(2,1)S(1)} %shard_map.138), channel_id=1, source_target_pairs={{0,8},{1,9},{2,10},{3,11},{4,12},{5,13},{6,14},{7,15},{8,0},{9,1},... | collective-permute-start | bytes 737288 | tf_op jit(solution)/shard_map/ppermute | solution.py:505
  49.9 23.1 %copy-start.23 = (bf16[48,3072]{1,0:T(8,128)(2,1)}, bf16[48,3072]{1,0:T(8,128)(2,1)S(1)}, u32[]{:S(2)}) copy-start(bf16[48,3072]{1,0:T(8,128)(2,1)S(1)} %collective-permute-done.6.refs_2_) | copy-start | bytes 884740
  50.8 19.9 %copy-start.29 = (bf16[128,3072]{1,0:T(8,128)(2,1)}, bf16[128,3072]{1,0:T(8,128)(2,1)S(1)}, u32[]{:S(2)}) copy-start(bf16[128,3072]{1,0:T(8,128)(2,1)S(1)} %collective-permute-done.9.refs_10_) | copy-start | bytes 2359300
  50.8 5.8 %collective-permute-start.12 = (bf16[128,3072]{1,0:T(8,128)(2,1)S(1)}, bf16[128,3072]{1,0:T(8,128)(2,1)S(1)}, u32[]{:S(2)}, u32[]{:S(2)}) collective-permute-start(bf16[128,3072]{1,0:T(8,128)(2,1)S(1)} %collective-permute-done.8.refs_8_), channel_id=1, source_target_pairs={{0,1},{1,0},{2,3},{3,2},{4,5},{5,4},{6,7},{7,6},{8,9},{9,8},{10,11... | collective-permute-start | bytes 2359304 | tf_op jit(solution)/shard_map/ppermute | solution.py:510
  50.9 7.3 %collective-permute-start.13 = (bf16[128,3072]{1,0:T(8,128)(2,1)S(1)}, bf16[128,3072]{1,0:T(8,128)(2,1)S(1)}, u32[]{:S(2)}, u32[]{:S(2)}) collective-permute-start(bf16[128,3072]{1,0:T(8,128)(2,1)S(1)} %collective-permute-done.9.refs_10_), channel_id=1, source_target_pairs={{0,1},{1,0},{2,3},{3,2},{4,5},{5,4},{6,7},{7,6},{8,9},{9,8},{10,11... | collective-permute-start | bytes 2359304 | tf_op jit(solution)/shard_map/ppermute | solution.py:510
  51.7 21.3 %collective-permute-start.15 = (bf16[128,3072]{1,0:T(8,128)(2,1)S(1)}, bf16[128,3072]{1,0:T(8,128)(2,1)S(1)}, u32[]{:S(2)}, u32[]{:S(2)}) collective-permute-start(bf16[128,3072]{1,0:T(8,128)(2,1)S(1)} %collective-permute-done.9.refs_10_), channel_id=1, source_target_pairs={{0,16},{1,17},{2,18},{3,19},{4,20},{5,21},{6,22},{7,23},{8,24},{9,... | collective-permute-start | bytes 2359304 | tf_op jit(solution)/shard_map/ppermute | solution.py:510
  53.8 16.9 %copy-start.4 = (bf16[96,3072]{1,0:T(8,128)(2,1)}, bf16[96,3072]{1,0:T(8,128)(2,1)S(1)}, u32[]{:S(2)}) copy-start(bf16[96,3072]{1,0:T(8,128)(2,1)S(1)} %shard_map.139.refs_2_) | copy-start | bytes 1769476
  53.9 4.4 %collective-permute-start.14 = (bf16[96,3072]{1,0:T(8,128)(2,1)S(1)}, bf16[96,3072]{1,0:T(8,128)(2,1)S(1)}, u32[]{:S(2)}, u32[]{:S(2)}) collective-permute-start(bf16[96,3072]{1,0:T(8,128)(2,1)S(1)} %shard_map.139.refs_2_), channel_id=1, source_target_pairs={{0,1},{1,0},{2,3},{3,2},{4,5},{5,4},{6,7},{7,6},{8,9},{9,8},{10,11... | collective-permute-start | bytes 1769480 | tf_op jit(solution)/shard_map/ppermute | solution.py:505
  53.9 17.7 %collective-permute-start.11 = (bf16[48,3072]{1,0:T(8,128)(2,1)S(1)}, bf16[48,3072]{1,0:T(8,128)(2,1)S(1)}, u32[]{:S(2)}, u32[]{:S(2)}) collective-permute-start(bf16[48,3072]{1,0:T(8,128)(2,1)S(1)} %collective-permute-done.6.refs_2_), channel_id=1, source_target_pairs={{0,4},{1,5},{2,6},{3,7},{4,0},{5,1},{6,2},{7,3},{8,12},{9,13},{10,... | collective-permute-start | bytes 884744 | tf_op jit(solution)/shard_map/ppermute | solution.py:510
  56.6 16.3 %collective-permute-start.10 = (bf16[48,3072]{1,0:T(8,128)(2,1)S(1)}, bf16[48,3072]{1,0:T(8,128)(2,1)S(1)}, u32[]{:S(2)}, u32[]{:S(2)}) collective-permute-start(bf16[48,3072]{1,0:T(8,128)(2,1)S(1)} %get-tuple-element.82), channel_id=1, source_target_pairs={{0,8},{1,9},{2,10},{3,11},{4,12},{5,13},{6,14},{7,15},{8,0},{9,1},... | collective-permute-start | bytes 884744 | tf_op jit(solution)/shard_map/ppermute | solution.py:510
  73.9 1.9 %collective-permute-start.21 = (bf16[64,3072]{1,0:T(8,128)(2,1)S(1)}, bf16[64,3072]{1,0:T(8,128)(2,1)}, u32[]{:S(2)}, u32[]{:S(2)}) collective-permute-start(bf16[64,3072]{1,0:T(8,128)(2,1)S(1)} %slice_bitcast_fusion.2), channel_id=1, source_target_pairs={{0,1},{1,0},{2,3},{3,2},{4,5},{5,4},{6,7},{7,6},{8,9},{9,8},{10,11... | collective-permute-start | bytes 1179656 | tf_op jit(solution)/shard_map/ppermute | solution.py:505
  75.2 1.9 %collective-permute-start.17 = (bf16[4,384,128]{2,1,0:T(8,128)(2,1)S(1)}, bf16[4,384,128]{2,1,0:T(8,128)(2,1)S(1)}, u32[]{:S(2)}, u32[]{:S(2)}) collective-permute-start(bf16[4,384,128]{2,1,0:T(8,128)(2,1)S(1)} %get-tuple-element.95), channel_id=1, source_target_pairs={{0,1},{1,0},{2,3},{3,2},{4,5},{5,4},{6,7},{7,6},{8,9},{9,8},{10,11... | collective-permute-start | bytes 1179656 | tf_op jit(solution)/shard_map/ppermute | solution.py:510
  77.2 9.5 %collective-permute-start.22 = (bf16[128,3072]{1,0:T(8,128)(2,1)S(1)}, bf16[128,3072]{1,0:T(8,128)(2,1)S(1)}, u32[]{:S(2)}, u32[]{:S(2)}) collective-permute-start(bf16[128,3072]{1,0:T(8,128)(2,1)S(1)} %copy-done.33), channel_id=1, source_target_pairs={{0,1},{1,0},{2,3},{3,2},{4,5},{5,4},{6,7},{7,6},{8,9},{9,8},{10,11... | collective-permute-start | bytes 2359304 | tf_op jit(solution)/shard_map/ppermute | solution.py:510
  77.7 9.0 %collective-permute-start.16 = (bf16[48,3072]{1,0:T(8,128)(2,1)S(1)}, bf16[48,3072]{1,0:T(8,128)(2,1)S(1)}, u32[]{:S(2)}, u32[]{:S(2)}) collective-permute-start(bf16[48,3072]{1,0:T(8,128)(2,1)S(1)} %copy-done.26), channel_id=1, source_target_pairs={{0,4},{1,5},{2,6},{3,7},{4,0},{5,1},{6,2},{7,3},{8,12},{9,13},{10,... | collective-permute-start | bytes 884744 | tf_op jit(solution)/shard_map/ppermute | solution.py:510
  78.2 17.2 %collective-permute-start.18 = (bf16[2,384,128]{2,1,0:T(8,128)(2,1)S(1)}, bf16[2,384,128]{2,1,0:T(8,128)(2,1)S(1)}, u32[]{:S(2)}, u32[]{:S(2)}) collective-permute-start(bf16[2,384,128]{2,1,0:T(8,128)(2,1)S(1)} %get-tuple-element.97), channel_id=1, source_target_pairs={{0,16},{1,17},{2,18},{3,19},{4,20},{5,21},{6,22},{7,23},{8,24},{9,... | collective-permute-start | bytes 589832 | tf_op jit(solution)/shard_map/ppermute | solution.py:510
  79.2 16.2 %collective-permute-start.19 = (bf16[2,384,128]{2,1,0:T(8,128)(2,1)S(1)}, bf16[2,384,128]{2,1,0:T(8,128)(2,1)S(1)}, u32[]{:S(2)}, u32[]{:S(2)}) collective-permute-start(bf16[2,384,128]{2,1,0:T(8,128)(2,1)S(1)} %get-tuple-element.98), channel_id=1, source_target_pairs={{0,2},{1,3},{2,0},{3,1},{4,6},{5,7},{6,4},{7,5},{8,10},{9,11},{10,... | collective-permute-start | bytes 589832 | tf_op jit(solution)/shard_map/ppermute | solution.py:510
  79.8 15.6 %collective-permute-start.20 = (bf16[2,384,128]{2,1,0:T(8,128)(2,1)S(1)}, bf16[2,384,128]{2,1,0:T(8,128)(2,1)S(1)}, u32[]{:S(2)}, u32[]{:S(2)}) collective-permute-start(bf16[2,384,128]{2,1,0:T(8,128)(2,1)S(1)} %get-tuple-element.99), channel_id=1, source_target_pairs={{0,18},{1,19},{2,16},{3,17},{4,22},{5,23},{6,20},{7,21},{8,26},{9,... | collective-permute-start | bytes 589832 | tf_op jit(solution)/shard_map/ppermute | solution.py:510
  100.7 9.9 %collective-permute-start.23 = (bf16[2,4,128,1536]{3,2,1,0:T(8,128)(2,1)S(1)}, bf16[2,4,128,1536]{3,2,1,0:T(8,128)(2,1)S(1)}, u32[]{:S(2)}, u32[]{:S(2)}) collective-permute-start(bf16[2,4,128,1536]{3,2,1,0:T(8,128)(2,1)S(1)} %shard_map.144), channel_id=1, source_target_pairs={{0,1},{1,0},{2,3},{3,2},{4,5},{5,4},{6,7},{7,6},{8,9},{9,8},{10,11... | collective-permute-start | bytes 9437192 | tf_op jit(solution)/shard_map/ppermute | solution.py:510
  100.8 6.2 %collective-permute-start.24 = (bf16[4,384,128]{2,1,0:T(8,128)(2,1)S(1)}, bf16[4,384,128]{2,1,0:T(8,128)(2,1)S(1)}, u32[]{:S(2)}, u32[]{:S(2)}) collective-permute-start(bf16[4,384,128]{2,1,0:T(8,128)(2,1)S(1)} %get-tuple-element.110), channel_id=1, source_target_pairs={{0,1},{1,0},{2,3},{3,2},{4,5},{5,4},{6,7},{7,6},{8,9},{9,8},{10,11... | collective-permute-start | bytes 1179656 | tf_op jit(solution)/shard_map/ppermute | solution.py:510
  101.3 21.2 %collective-permute-start.29 = (bf16[64,3072]{1,0:T(8,128)(2,1)S(1)}, bf16[64,3072]{1,0:T(8,128)(2,1)S(1)}, u32[]{:S(2)}, u32[]{:S(2)}) collective-permute-start(bf16[64,3072]{1,0:T(8,128)(2,1)S(1)} %convert_add_fusion.3), channel_id=1, source_target_pairs={{0,8},{1,9},{2,10},{3,11},{4,12},{5,13},{6,14},{7,15},{8,0},{9,1},... | collective-permute-start | bytes 1179656 | tf_op jit(solution)/shard_map/ppermute | solution.py:505
  107.0 11.3 %collective-permute-start.25 = (bf16[2,384,128]{2,1,0:T(8,128)(2,1)S(1)}, bf16[2,384,128]{2,1,0:T(8,128)(2,1)S(1)}, u32[]{:S(2)}, u32[]{:S(2)}) collective-permute-start(bf16[2,384,128]{2,1,0:T(8,128)(2,1)S(1)} %get-tuple-element.112), channel_id=1, source_target_pairs={{0,16},{1,17},{2,18},{3,19},{4,20},{5,21},{6,22},{7,23},{8,24},{9,... | collective-permute-start | bytes 589832 | tf_op jit(solution)/shard_map/ppermute | solution.py:510
  108.6 10.9 %collective-permute-start.26 = (bf16[2,384,128]{2,1,0:T(8,128)(2,1)S(1)}, bf16[2,384,128]{2,1,0:T(8,128)(2,1)S(1)}, u32[]{:S(2)}, u32[]{:S(2)}) collective-permute-start(bf16[2,384,128]{2,1,0:T(8,128)(2,1)S(1)} %get-tuple-element.113), channel_id=1, source_target_pairs={{0,2},{1,3},{2,0},{3,1},{4,6},{5,7},{6,4},{7,5},{8,10},{9,11},{10,... | collective-permute-start | bytes 589832 | tf_op jit(solution)/shard_map/ppermute | solution.py:510
  109.2 10.9 %collective-permute-start.27 = (bf16[2,384,128]{2,1,0:T(8,128)(2,1)S(1)}, bf16[2,384,128]{2,1,0:T(8,128)(2,1)S(1)}, u32[]{:S(2)}, u32[]{:S(2)}) collective-permute-start(bf16[2,384,128]{2,1,0:T(8,128)(2,1)S(1)} %get-tuple-element.114), channel_id=1, source_target_pairs={{0,18},{1,19},{2,16},{3,17},{4,22},{5,23},{6,20},{7,21},{8,26},{9,... | collective-permute-start | bytes 589832 | tf_op jit(solution)/shard_map/ppermute | solution.py:510
  120.8 18.6 %collective-permute-start.28 = (bf16[2,128,1536]{2,1,0:T(8,128)(2,1)}, bf16[2,128,1536]{2,1,0:T(8,128)(2,1)}, u32[]{:S(2)}, u32[]{:S(2)}) collective-permute-start(bf16[2,128,1536]{2,1,0:T(8,128)(2,1)} %get-tuple-element.118), channel_id=1, source_target_pairs={{0,2},{1,3},{2,0},{3,1},{4,6},{5,7},{6,4},{7,5},{8,10},{9,11},{10,... | collective-permute-start | bytes 2359304 | tf_op jit(solution)/shard_map/ppermute | solution.py:510
  121.5 18.3 %collective-permute-start.30 = (bf16[2,128,1536]{2,1,0:T(8,128)(2,1)}, bf16[2,128,1536]{2,1,0:T(8,128)(2,1)}, u32[]{:S(2)}, u32[]{:S(2)}) collective-permute-start(bf16[2,128,1536]{2,1,0:T(8,128)(2,1)} %get-tuple-element.129), channel_id=1, source_target_pairs={{0,16},{1,17},{2,18},{3,19},{4,20},{5,21},{6,22},{7,23},{8,24},{9,... | collective-permute-start | bytes 2359304 | tf_op jit(solution)/shard_map/ppermute | solution.py:510
  123.3 13.8 %collective-permute-start.31 = (bf16[64,3072]{1,0:T(8,128)(2,1)}, bf16[64,3072]{1,0:T(8,128)(2,1)}, u32[]{:S(2)}, u32[]{:S(2)}) collective-permute-start(bf16[64,3072]{1,0:T(8,128)(2,1)} %fusion.27), channel_id=1, source_target_pairs={{0,4},{1,5},{2,6},{3,7},{4,0},{5,1},{6,2},{7,3},{8,12},{9,13},{10,... | collective-permute-start | bytes 1179656 | tf_op jit(solution)/shard_map/ppermute | solution.py:505
  126.5 13.7 %copy-start.10 = (bf16[2,2,128,1536]{3,2,1,0:T(8,128)(2,1)S(1)}, bf16[2,2,128,1536]{3,2,1,0:T(8,128)(2,1)}, u32[]{:S(2)}) copy-start(bf16[2,2,128,1536]{3,2,1,0:T(8,128)(2,1)} %copy-done.9) | copy-start | bytes 4718596
  139.8 5.5 %collective-permute-start.34 = (bf16[96,3072]{1,0:T(8,128)(2,1)S(1)}, bf16[96,3072]{1,0:T(8,128)(2,1)S(1)}, u32[]{:S(2)}, u32[]{:S(2)}) collective-permute-start(bf16[96,3072]{1,0:T(8,128)(2,1)S(1)} %get-tuple-element.135), channel_id=1, source_target_pairs={{1,0},{0,1},{3,2},{2,3},{5,4},{4,5},{7,6},{6,7},{9,8},{8,9},{11,10... | collective-permute-start | bytes 1769480 | tf_op jit(solution)/shard_map/ppermute | solution.py:505
  139.8 5.6 %collective-permute-start.35 = (bf16[256,3072]{1,0:T(8,128)(2,1)S(1)}, bf16[256,3072]{1,0:T(8,128)(2,1)S(1)}, u32[]{:S(2)}, u32[]{:S(2)}) collective-permute-start(bf16[256,3072]{1,0:T(8,128)(2,1)S(1)} %get-tuple-element.137), channel_id=1, source_target_pairs={{1,0},{0,1},{3,2},{2,3},{5,4},{4,5},{7,6},{6,7},{9,8},{8,9},{11,10... | collective-permute-start | bytes 4718600 | tf_op jit(solution)/shard_map/ppermute | solution.py:505
  142.1 11.1 %collective-permute-start.32 = (bf16[128,1536]{1,0:T(8,128)(2,1)S(1)}, bf16[128,1536]{1,0:T(8,128)(2,1)S(1)}, u32[]{:S(2)}, u32[]{:S(2)}) collective-permute-start(bf16[128,1536]{1,0:T(8,128)(2,1)S(1)} %fusion.5), channel_id=1, source_target_pairs={{0,16},{1,17},{2,18},{3,19},{4,20},{5,21},{6,22},{7,23},{8,24},{9,... | collective-permute-start | bytes 1179656 | tf_op jit(solution)/shard_map/ppermute | solution.py:510
  143.8 12.1 %collective-permute-start.33 = (bf16[128,1536]{1,0:T(8,128)(2,1)S(1)}, bf16[128,1536]{1,0:T(8,128)(2,1)S(1)}, u32[]{:S(2)}, u32[]{:S(2)}) collective-permute-start(bf16[128,1536]{1,0:T(8,128)(2,1)S(1)} %fusion.6), channel_id=1, source_target_pairs={{0,2},{1,3},{2,0},{3,1},{4,6},{5,7},{6,4},{7,5},{8,10},{9,11},{10,... | collective-permute-start | bytes 1179656 | tf_op jit(solution)/shard_map/ppermute | solution.py:510
  145.5 13.3 %collective-permute-start.36 = (bf16[36,3072]{1,0:T(8,128)(2,1)S(1)}, bf16[36,3072]{1,0:T(8,128)(2,1)S(1)}, u32[]{:S(2)}, u32[]{:S(2)}) collective-permute-start(bf16[36,3072]{1,0:T(8,128)(2,1)S(1)} %pad_maximum_fusion), channel_id=1, source_target_pairs={{0,8},{1,9},{2,10},{3,11},{4,12},{5,13},{6,14},{7,15},{8,0},{9,1},... | collective-permute-start | bytes 663560 | tf_op jit(solution)/shard_map/ppermute | solution.py:505
  147.1 18.0 %collective-permute-start.39 = (bf16[64,3072]{1,0:T(8,128)(2,1)S(1)}, bf16[64,3072]{1,0:T(8,128)(2,1)S(1)}, u32[]{:S(2)}, u32[]{:S(2)}) collective-permute-start(bf16[64,3072]{1,0:T(8,128)(2,1)S(1)} %fusion.28), channel_id=1, source_target_pairs={{0,2},{1,3},{2,0},{3,1},{4,6},{5,7},{6,4},{7,5},{8,10},{9,11},{10,... | collective-permute-start | bytes 1179656 | tf_op jit(solution)/shard_map/ppermute | solution.py:505
  159.0 7.6 %collective-permute-start.38 = (bf16[16,3072]{1,0:T(8,128)(2,1)S(1)}, bf16[16,3072]{1,0:T(8,128)(2,1)S(1)}, u32[]{:S(2)}, u32[]{:S(2)}) collective-permute-start(bf16[16,3072]{1,0:T(8,128)(2,1)S(1)} %pad_maximum_fusion.2), channel_id=1, source_target_pairs={{2,0},{3,1},{4,2},{5,3},{6,4},{7,5},{10,8},{11,9},{12,10},{13,11},... | collective-permute-start | bytes 294920 | tf_op jit(solution)/shard_map/ppermute | solution.py:505
  160.3 6.8 %collective-permute-start.37 = (bf16[16,3072]{1,0:T(8,128)(2,1)S(1)}, bf16[16,3072]{1,0:T(8,128)(2,1)S(1)}, u32[]{:S(2)}, u32[]{:S(2)}) collective-permute-start(bf16[16,3072]{1,0:T(8,128)(2,1)S(1)} %pad_maximum_fusion.1), channel_id=1, source_target_pairs={{0,2},{1,3},{2,4},{3,5},{4,6},{5,7},{8,10},{9,11},{10,12},{11,13},... | collective-permute-start | bytes 294920 | tf_op jit(solution)/shard_map/ppermute | solution.py:505
  165.2 4.7 %collective-permute-start.40 = (bf16[64,3072]{1,0:T(8,128)(2,1)S(1)}, bf16[64,3072]{1,0:T(8,128)(2,1)S(1)}, u32[]{:S(2)}, u32[]{:S(2)}) collective-permute-start(bf16[64,3072]{1,0:T(8,128)(2,1)S(1)} %add_convert_fusion.2), channel_id=1, source_target_pairs={{0,1},{1,0},{2,3},{3,2},{4,5},{5,4},{6,7},{7,6},{8,9},{9,8},{10,11... | collective-permute-start | bytes 1179656 | tf_op jit(solution)/shard_map/ppermute | solution.py:505
  (30 other events, 92.7 us)

commit v3 on v2

--- a/solution.py
+++ b/solution.py
@@ -15,7 +15,7 @@
 RIM = 48
 SLOT = TILE + RIM
 HEAD = 128
-STEP = 4
+STEP = 8
 
 SCALE = HEAD**-0.5
 ADAPTER = 0.5
@@ -55,19 +55,24 @@
     def _():
         low_acc[...] = jnp.zeros_like(low_acc)
 
-    for i in range(STEP):
-        cols = slice(i * HEAD, (i + 1) * HEAD)
-        keys, values = slot_keys(slots, cols)
-        scores = nt(keys, query[:, cols]) * SCALE + bias[combo[step * STEP + i]]
-        top = jnp.max(scores, axis=0, keepdims=True)
-        weights = jnp.exp(scores - top)
-        totals = jnp.sum(weights, axis=0, keepdims=True)
-        att = (tn(values, weights.astype(BF16)) / totals).astype(BF16)
-        att_ref[cols, :] = att
-        log_ref[0, i : i + 1, :] = top + jnp.log(totals)
-        low_acc[...] += nn(down[:, cols], att)
-        at = pl.ds(pl.multiple_of((step * STEP + i) * HEAD, HEAD), HEAD)
-        grads_ref[combo[last], :, at] = nt(grad_low[...], att).astype(BF16)
+    columns = [slice(i * HEAD, (i + 1) * HEAD) for i in range(STEP)]
+    pairs = [slot_keys(slots, cols) for cols in columns]
+    scores = [
+        nt(keys, query[:, cols]) * SCALE + bias[combo[step * STEP + i]]
+        for i, (cols, (keys, _)) in enumerate(zip(columns, pairs))
+    ]
+    tops = [jnp.max(block, axis=0, keepdims=True) for block in scores]
+    weights = [jnp.exp(block - top) for block, top in zip(scores, tops)]
+    totals = [jnp.sum(block, axis=0, keepdims=True) for block in weights]
+    mixed = [tn(values, block.astype(BF16)) for (_, values), block in zip(pairs, weights)]
+    att = jnp.concatenate(
+        [(block * (1.0 / total)).astype(BF16) for block, total in zip(mixed, totals)]
+    )
+    att_ref[...] = att
+    log_ref[0] = jnp.concatenate([top + jnp.log(total) for top, total in zip(tops, totals)])
+    low_acc[...] += nn(down[...], att)
+    at = pl.ds(pl.multiple_of(step * STEP * HEAD, STEP * HEAD), STEP * HEAD)
+    grads_ref[combo[last], :, at] = nt(grad_low[...], att).astype(BF16)
 
     @pl.when(step == pl.num_programs(0) - 1)
     def _():
@@ -81,20 +86,26 @@
     bias, att, grad, extra, log_total, grad_query = refs[3 * n_slots : 3 * n_slots + 6]
     terms = refs[3 * n_slots + 6 :]
     step = pl.program_id(0)
-    for i in range(STEP):
-        cols = slice(i * HEAD, (i + 1) * HEAD)
-        keys, values = slot_keys(slots, cols)
-        here = query[:, cols]
-        scores = nt(keys, here) * SCALE + bias[combo[step * STEP + i]]
-        probs = jnp.exp(scores - log_total[0, i : i + 1, :])
-        grad_att = (grad[cols, :].astype(F32) + extra[cols, :]).astype(BF16)
-        inner = jnp.sum(
-            grad_att.astype(F32) * att[cols, :].astype(F32), axis=0, keepdims=True
-        )
-        value_terms = nt(probs.astype(BF16), grad_att).astype(BF16)
-        grad_scores = (probs * (nn(values, grad_att) - inner)).astype(BF16)
-        key_terms = (nn(grad_scores, here) * SCALE).astype(BF16)
-        grad_query[:, cols] = (tn(grad_scores, keys) * SCALE).astype(BF16)
+    columns = [slice(i * HEAD, (i + 1) * HEAD) for i in range(STEP)]
+    pairs = [slot_keys(slots, cols) for cols in columns]
+    scores = [
+        nt(keys, query[:, cols]) * SCALE + bias[combo[step * STEP + i]]
+        for i, (cols, (keys, _)) in enumerate(zip(columns, pairs))
+    ]
+    grad_att = [(grad[cols, :].astype(F32) + extra[cols, :]).astype(BF16) for cols in columns]
+    grad_probs = [nn(values, block) for (_, values), block in zip(pairs, grad_att)]
+    inner = [
+        jnp.sum(block.astype(F32) * att[cols, :].astype(F32), axis=0, keepdims=True)
+        for block, cols in zip(grad_att, columns)
+    ]
+    probs = [jnp.exp(block - log_total[0, i : i + 1, :]) for i, block in enumerate(scores)]
+    grad_scores = [
+        (p * (gp - minus)).astype(BF16) for p, gp, minus in zip(probs, grad_probs, inner)
+    ]
+    for i, cols in enumerate(columns):
+        value_terms = nt(probs[i].astype(BF16), grad_att[i]).astype(BF16)
+        key_terms = (nn(grad_scores[i], query[:, cols]) * SCALE).astype(BF16)
+        grad_query[:, cols] = (tn(grad_scores[i], pairs[i][0]) * SCALE).astype(BF16)
         for s in range(n_slots):
             core, rim = terms[2 * s : 2 * s + 2]
             at = s * SLOT
@@ -116,7 +127,7 @@
     return pl.BlockSpec(shape, lambda *_: (0,) * len(shape))
 
 
-def head_call(kernel, steps, in_specs, out_specs, out_shape, scratch):
+def head_call(kernel, n_slots, steps, in_specs, out_specs, out_shape, scratch):
     call = pl.pallas_call(
         kernel,
         grid_spec=pltpu.PrefetchScalarGridSpec(
@@ -128,7 +139,7 @@
         ),
         out_shape=out_shape,
         compiler_params=pltpu.CompilerParams(
-            dimension_semantics=("arbitrary",), vmem_limit_bytes=14 * 1024 * 1024
+            dimension_semantics=("arbitrary",), vmem_limit_bytes=max(2, n_slots) * 7 * 1024 * 1024
         ),
         cost_estimate=pl.CostEstimate(flops=1000, bytes_accessed=1000, transcendentals=0),
     )
@@ -154,6 +165,7 @@
     n_slots = len(slots)
     return head_call(
         functools.partial(forward_kernel, n_slots),
+        n_slots,
         heads // STEP,
         [column_block(tokens)]
         + slot_specs(n_slots)
@@ -170,13 +182,13 @@
             whole((rank, tokens)),
         ],
         [
-            jax.ShapeDtypeStruct((width, tokens), BF16),
+            pltpu.HBM((width, tokens), BF16),
             jax.ShapeDtypeStruct((heads // STEP, STEP, tokens), F32),
             jax.ShapeDtypeStruct((2, rank, width), BF16),
             jax.ShapeDtypeStruct((rank, tokens), BF16),
         ],
         [pltpu.VMEM((rank, tokens), F32)],
-    )(combo, query, *[part for slot in slots for part in slot], bias, down, grad_low, upstream)
+    )(combo, query, *[part for slot in slots for part in slot], bias, *in_hbm([down]), grad_low, *in_hbm([upstream]))
 
 
 def attend_back(combo, query, slots, bias, att, grad, extra, log_total):
@@ -185,6 +197,7 @@
     n_slots = len(slots)
     out = head_call(
         functools.partial(backward_kernel, n_slots),
+        n_slots,
         heads // STEP,
         [column_block(tokens)]
         + slot_specs(n_slots)
@@ -196,12 +209,8 @@
             pl.BlockSpec((1, STEP, tokens), lambda step, *_: (step, 0, 0)),
         ],
         [column_block(tokens)] + [column_block(2 * TILE), column_block(2 * RIM)] * n_slots,
-        [jax.ShapeDtypeStruct((tokens, width), BF16)]
-        + [
-            jax.ShapeDtypeStruct((2 * TILE, width), BF16),
-            jax.ShapeDtypeStruct((2 * RIM, width), BF16),
-        ]
-        * n_slots,
+        [pltpu.HBM((tokens, width), BF16)]
+        + [pltpu.HBM((2 * TILE, width), BF16), pltpu.HBM((2 * RIM, width), BF16)] * n_slots,
         [],
     )(
         combo, query, *[part for slot in slots for part in slot], bias, *in_hbm([att]), grad, extra,
@@ -292,7 +301,7 @@
         whole((total, tokens)),
         jax.ShapeDtypeStruct((total, tokens), parts[0].dtype),
         [],
-    )(me[None], *parts)
+    )(me[None], *in_hbm(parts))
 
 
 def edge_kernel(where, keys, values, to_left, to_right, edge):
@@ -332,7 +341,7 @@
     ).astype(BF16)
 
 
-def column_call(kernel, scalars, blocks, out_rows):
+def column_call(kernel, scalars, blocks, out_rows, hbm=False):
     width = blocks[0].shape[1]
     step = width // 4
     out = plain_call(
@@ -341,9 +350,9 @@
         [SCALARS] * len(scalars)
         + [pl.BlockSpec((block.shape[0], step), lambda j: (0, j)) for block in blocks],
         [pl.BlockSpec((rows, step), lambda j: (0, j)) for rows in out_rows],
-        [jax.ShapeDtypeStruct((rows, width), BF16) for rows in out_rows],
+        [(pltpu.HBM if hbm else jax.ShapeDtypeStruct)((rows, width), BF16) for rows in out_rows],
         [],
-    )(*scalars, *blocks)
+    )(*scalars, *(in_hbm(blocks) if hbm else blocks))
     return out if len(out_rows) > 1 else out[0]
 
 
@@ -369,8 +378,8 @@
     return jnp.concatenate([ref[...] for ref in refs], axis=0) if len(refs) > 1 else refs[0][...]
 
 
-def grad_kernel(n_parts, *refs):
-    weights, tokens, outs, acc = refs[:n_parts], refs[n_parts : n_parts + 8], refs[-3:-1], refs[-1]
+def grad_kernel(n_parts, counts, *refs):
+    weights, tokens, outs, acc = refs[:n_parts], refs[n_parts:-3], refs[-3:-1], refs[-1]
     step = pl.program_id(0)
 
     @pl.when(step == 0)
@@ -378,9 +387,11 @@
         acc[...] = jnp.zeros_like(acc)
 
     weight = weight_block(weights)
-    for place in range(4):
-        here = jnp.concatenate([tokens[2 * place][...], tokens[2 * place + 1][...]], axis=0)
+    at = 0
+    for place, count in enumerate(counts):
+        here = jnp.concatenate([ref[...] for ref in tokens[at : at + count]], axis=0)
         acc[place] += nt(weight, here)
+        at += count
 
     @pl.when(step == pl.num_programs(0) - 1)
     def _():
@@ -392,9 +403,11 @@
 def grad_parts(weights, tokens):
     rows = sum(part.shape[0] for part in weights)
     width = weights[0].shape[1]
-    step = 512
+    step = 1536
+    counts = [len(parts) for parts in tokens]
+    tokens = [part for parts in tokens for part in parts]
     return plain_call(
-        functools.partial(grad_kernel, len(weights)),
+        functools.partial(grad_kernel, len(weights), counts),
         (width // step,),
         [pl.BlockSpec((part.shape[0], step), lambda k: (0, k)) for part in (*weights, *tokens)],
         [whole((4, rows, TILE))] * 2,
@@ -403,66 +416,48 @@
     )(*in_hbm(weights), *in_hbm(tokens))
 
 
-def project_kernel(n_parts, core, split, *refs):
+def project_kernel(n_parts, core, kept, *refs):
     weights, parts, rest = refs[:n_parts], refs[n_parts : n_parts + 4], refs[n_parts + 4 :]
     turned = rest[-1]
-    step = pl.program_id(0)
-
-    @pl.when(step == 0)
+
+    @pl.when(pl.program_id(0) == 0)
     def _():
         for place in range(4):
             turned[place * TILE : (place + 1) * TILE, :] = parts[place][core].T
 
     result = nn(turned[...], weight_block(weights))
     blocks = [result[place * TILE : (place + 1) * TILE] for place in range(4)]
-    second = step >= split
     if core:
-        out = rest[0]
-        for slot, place in enumerate((0, jnp.where(second, 2, 1), jnp.where(second, 1, 2), 3)):
-            out[0, place] = blocks[slot].astype(BF16)
+        for place in range(4):
+            rest[0][place] = blocks[place].astype(BF16)
     else:
-        added, keep, send_first, send_second = rest[:-1]
-
-        def total(place, slot):
-            return (blocks[place] + added[0, slot].astype(F32)).astype(BF16)
-
-        @pl.when(step < split)
-        def _():
-            for slot in range(2):
-                keep[0, slot] = total(slot, slot)
-                send_first[slot] = total(2 + slot, 2 + slot)
-
-        @pl.when(second)
-        def _():
-            for slot in range(2):
-                keep[0, slot] = total(2 * slot, slot)
-                send_second[slot] = total(2 * slot + 1, 2 + slot)
-
-
-def project(weights, parts, core, added=()):
+        added, keep, send = rest[:-1]
+        for out, places in ((keep, kept), (send, [p for p in range(4) if p not in kept])):
+            for slot, place in enumerate(places):
+                out[slot] = (blocks[place] + added[place].astype(F32)).astype(BF16)
+
+
+def project(weights, parts, core, half, added=()):
     rows = sum(part.shape[0] for part in weights)
-    width = weights[0].shape[1]
-    step = 512
-    split = width // 2 // step
-    every = pl.BlockSpec((1, 4, TILE, step), lambda j: (j // split, 0, 0, j % split))
-    sent = (2, TILE, width // 2)
-    near = [
-        pl.BlockSpec((1, 2, TILE, step), lambda j: (j // split, 0, 0, j % split)),
-        pl.BlockSpec((2, TILE, step), lambda j: (0, 0, jnp.minimum(j, split - 1))),
-        pl.BlockSpec((2, TILE, step), lambda j: (0, 0, jnp.maximum(j - split, 0))),
-    ]
+    width = weights[0].shape[1] // 2
+    step = 768
+    split = width // step
+    kept = [0, 2] if half else [0, 1]
+    four = pl.BlockSpec((4, TILE, step), lambda j: (0, 0, j))
+    two = pl.BlockSpec((2, TILE, step), lambda j: (0, 0, j))
+    shape = (2, TILE, width)
     return plain_call(
-        functools.partial(project_kernel, len(weights), core, split),
-        (width // step,),
-        [pl.BlockSpec((part.shape[0], step), lambda j: (0, j)) for part in weights]
+        functools.partial(project_kernel, len(weights), core, kept),
+        (split,),
+        [pl.BlockSpec((part.shape[0], step), lambda j: (0, half * split + j)) for part in weights]
         + [whole(part.shape) for part in parts]
-        + [every] * len(added),
-        every if core else near,
-        jax.ShapeDtypeStruct((2, 4, TILE, width // 2), BF16)
+        + [four] * len(added),
+        four if core else [two] * 2,
+        jax.ShapeDtypeStruct((4, TILE, width), BF16)
         if core
-        else [jax.ShapeDtypeStruct(shape, BF16) for shape in ((2, *sent), sent, sent)],
+        else [jax.ShapeDtypeStruct(shape, BF16)] * 2,
         [pltpu.VMEM((4 * TILE, rows), BF16)],
-    )(*in_hbm(weights), *parts, *added)
+    )(*in_hbm(weights), *in_hbm(parts), *added)
 
 
 def bias_kernel(shifts, frames, where, bias):
@@ -520,12 +515,6 @@
 
 def after(value, *done):
     return lax.optimization_barrier((value, done))[0]
-
-
-def exchange(like, other, until):
-    pairs = pack(like, swap(other, 0, 1))
-    got = [swap(pair, x, 2 * y) for (x, y), pair in zip(PLACES[1:], pairs[1:])]
-    return [pairs[0], *after(got, until)]
 
 
 def on_device(
@@ -562,14 +551,14 @@
 
     edge_at = edge_row[None]
     leftmost, rightmost, edge = column_call(
-        edge_kernel, [edge_at], [input_keys, input_values], [16, 16, 32]
-    )
+        edge_kernel, [edge_at], [input_keys, input_values], [16, 16, 32], hbm=True
+    )
+    core_slots = [
+        (permute(input_keys, route), permute(input_values, route)) for route in to_frame
+    ]
+    leftmost, rightmost = after((leftmost, rightmost), core_slots)
     right = permute(leftmost, to_left)
     left = permute(rightmost, to_right)
-    core_slots = [
-        (permute(input_keys, route), permute(input_values, route)) for route in to_frame
-    ]
-    tokens = {(0, 0, 0): upstream, (0, 0, 1): swap(upstream, 0, 1)}
     group = lax.axis_index("groups")
     turns = devices // 4
     me = position * 2 + group
@@ -580,30 +569,33 @@
     down = adapter_down_weight.T
     grad_low = (ADAPTER * nt(adapter_up_weight, upstream)).astype(BF16)
     extra = tn(down, grad_low)
-    start = (left, right, core_slots, tokens[0, 0, 1], own, top, low_rows)
-    start = (*start, bias, grad_low, extra, combo)
+    across = swap(after(upstream, edge), 1, 0)
+    start = [left, right, own, low_rows, bias, grad_low, extra, combo, across, core_slots]
+    if turns == 4:
+        one, two = swap(after(own, edge), 0, 4), swap(after(top, edge), 0, 8)
+        start += [one, two]
     to_outer = column_call(outer_kernel, [edge_at], [after(left, start), right, edge], [40])
 
     outer = permute(to_outer, to_band)
-    for x, y in ((1, 0), (0, 1)):
-        tokens[x, y, 0] = swap(after(upstream, to_outer), x, 2 * y)
-    opened = (outer, tokens[1, 0, 0], tokens[0, 1, 0])
+    beside = swap(after(upstream, to_outer), 0, 2)
+    upper = swap(after(across[: TILE // 2], to_outer), 0, 2)
+    opened = (outer, beside, upper)
     if turns == 4:
-        one, two = swap(after(own, to_outer), 0, 4), swap(after(top, to_outer), 0, 8)
-        opened = (*opened, one, two)
-        three = swap(after(two, opened), 0, 4)
-        two_low = swap(after(low_rows, opened), 0, 8)
-        fetched = [three, two_low]
+        two_low = swap(after(low_rows, to_outer), 0, 8)
+        three = swap(after(two, to_outer), 0, 4)
+        opened = (*opened, two_low, three)
+        three_low = swap(after(two_low, opened), 0, 4)
+        weights = [own, one, two, two_low, three, three_low]
+        fetched = [three_low]
     else:
         found = {0: own}
         for bit in [1 << b for b in reversed(range(turns.bit_length() - 1))]:
             found |= {t ^ bit: swap(block, 0, 4 * bit) for t, block in found.items()}
         weights = [found[t] for t in range(turns)]
         fetched = []
-    tokens[1, 1, 0] = swap(after(tokens[0, 1, 0], opened), 1, 0)
-    for x, y in ((1, 0), (0, 1)):
-        tokens[x, y, 1] = swap(after(tokens[x, y, 0], opened), 0, 1)
-    fetched.append(tokens[1, 1, 0])
+    lower = swap(after(beside[TILE // 2 :], opened), 1, 0)
+    across_other = swap(after(across, opened), 0, 1)
+    fetched.append(lower)
 
     rim = column_call(rim_kernel, [], [after(left, opened), right, outer], [2 * RIM])
     slots = [(input_keys, input_values, rim)] + [
@@ -611,7 +603,7 @@
     ]
     att, log_total, grads, low = attend(
         combo,
-        after(input_queries, extra, tokens[1, 0, 1], tokens[0, 1, 1]),
+        after(input_queries, extra, across_other),
         slots,
         bias, down, grad_low, upstream
     )
@@ -624,68 +616,58 @@
 
     def add_over(part, bit, until):
         part = part.astype(BF16)
-        got = permute(part, [(i, i ^ bit) for i in everyone])
-        return part.astype(F32) + after(got, until).astype(F32)
+        got = after(permute(part, [(i, i ^ bit) for i in everyone]), until)
+        return part.astype(F32) + got.astype(F32), got
 
     bits = [1 << b for b in range(1, devices.bit_length() - 1)]
-    if turns == 4:
-        three_low = swap(after(two_low, att), 0, 4)
-        weights = [own, one, two, two_low, three, three_low]
     if share % 16:
         weights = [jnp.concatenate(weights)]
     att_packed = pack(att_like, swap(att_other, 0, 1))
     att_got = [swap(pair, x, 2 * y) for (x, y), pair in zip(PLACES[1:], att_packed[1:])]
-    tokens[1, 1, 1] = swap(after(tokens[1, 1, 0], part, att_packed), 0, 1)
-    grads_like, grads_other = grad_parts(
-        [after(weights[0], att), *weights[1:]], [tokens[m] for m in MEMBERS]
-    )
+    tokens = [
+        [upstream, swap(after(upstream, att), 0, 1)],
+        [across, across_other],
+        [beside, swap(after(beside, att), 0, 1)],
+        [upper, lower, swap(after(upper, att), 0, 1), swap(after(lower, att), 0, 1)],
+    ]
+    grads_like, grads_other = grad_parts([after(weights[0], att), *weights[1:]], tokens)
     att_of = [att_packed[0], *after(att_got, grads_like)]
-    far = project(weights, att_of, 1)
-    near, first, second_half = project(weights, att_of, 0, (swap(far, 0, 1),))
-    grads_of = exchange(grads_like, grads_other, near)
-    first, second_half = after((first, second_half), grads_of)
-    first, second_half = swap(first, 0, 2), swap(second_half, 1, 0)
-    over_two, over_one = bits[-1], bits[1:-1]
-    part = add_over(after(part, grads_like), over_two, near)
-    grads_of[0] = after(grads_of[0], part)
+    for bit in bits[1:-1]:
+        part, got = add_over(part, bit, grads_like)
+    grads_packed = pack(grads_like, swap(after(grads_other, att_of), 0, 1))
+    grads_got = [swap(pair, x, 2 * y) for (x, y), pair in zip(PLACES[1:], grads_packed[1:])]
+    near, sent = [], []
+    for half in range(2):
+        far = swap(after(project(weights, att_of, 1, half), grads_packed, got), 0, 1)
+        keep, send = project(weights, att_of, 0, half, (far,))
+        near.append(keep)
+        sent.append(swap(send, 1, 0) if half else swap(send, 0, 2))
+    grads_of = [grads_packed[0], *after(grads_got, near)]
+    part, got = add_over(after(part, grads_of), bits[-1], near)
     grad_att = collect(grads_of, me, turns)
     grad_query, terms = attend_back(
         combo, after(input_queries, near), slots, bias, att, grad_att, extra, log_total
     )
-    for bit in over_one:
-        part = add_over(part, bit, terms)
-    grad_query, terms = after((grad_query, terms), first, second_half, part)
-    first = near[0].astype(F32) + after(first, grad_query).astype(F32)
-    second_half = near[1].astype(F32) + after(second_half, grad_query).astype(F32)
+    grad_query, terms = after((grad_query, terms), sent, got)
     core, rim_terms = terms[0]
     rim_terms = rim_terms.astype(F32)
     back = [[(j, i) for i, j in route] for route in to_frame]
-    for (_, sent), route in zip(terms[1:], back):
-        rim_terms += permute(sent, route).astype(F32)
-    core_terms = [core] + [permute(sent, route) for (sent, _), route in zip(terms[1:], back)]
-    rim_terms = after(rim_terms, core_terms)
+    for (_, block), route in zip(terms[1:], back):
+        rim_terms += permute(block, route).astype(F32)
+    core_terms = [core] + [
+        permute(after(block, rim_terms), route) for (block, _), route in zip(terms[1:], back)
+    ]
     keys_out, values_out = rim_terms[:RIM], rim_terms[RIM:]
-    outer = permute(
-        jnp.concatenate(
-            [keys_out[16:32], values_out[16:32], keys_out[32:34], values_out[32:34]]
-        ).astype(BF16),
-        to_band,
-    )
-    part = add_over(part, bits[0], outer)
+    to_outer = jnp.concatenate(
+        [keys_out[16:32], values_out[16:32], keys_out[32:34], values_out[32:34]]
+    ).astype(BF16)
+    outer = permute(to_outer, to_band)
+    sent = after(sent, to_outer)
+    first, second_half = (
+        keep.astype(F32) + block.astype(F32) for keep, block in zip(near, sent)
+    )
+    part, _ = add_over(part, bits[0], outer)
     last_rows = swap(first[1].astype(BF16), 1, 0), swap(second_half[1].astype(BF16), 0, 2)
-    last_rows = after(last_rows, outer)
-    outer = after(outer, last_rows)
-    first = first[0] + last_rows[0].astype(F32)
-    second_half = second_half[0] + last_rows[1].astype(F32)
-    projected = (
-        jnp.concatenate([first, second_half], axis=1) + ADAPTER * tn(low, adapter_up_weight)
-    ).astype(BF16)
-
-    part = part.astype(BF16)
-    other = permute(part, [(i, i ^ 1) for i in everyone])
-    grad_down = jnp.where(second == 0, part, other).astype(F32).T
-    grad_up = jnp.where(second == 0, other, part).astype(F32)
-
     at_edge = (jnp.arange(ROWS)[:, None] == edge_row).astype(F32)
     outer_corners = outer[32:].astype(F32)
 
@@ -698,8 +680,22 @@
             ]
         ).astype(BF16)
 
-    from_right = permute(side(0), to_left)
-    from_left = permute(side(1), to_right)
+    sides = side(0), side(1)
+    from_right = permute(sides[0], to_left)
+    from_left = permute(sides[1], to_right)
+    last_rows = after(last_rows, sides)
+    first = first[0] + last_rows[0].astype(F32)
+    second_half = second_half[0] + last_rows[1].astype(F32)
+    projected = (
+        jnp.concatenate([first, second_half], axis=1) + ADAPTER * tn(low, adapter_up_weight)
+    ).astype(BF16)
+
+    part = after(part.astype(BF16), last_rows)
+    other = after(permute(part, [(i, i ^ 1) for i in everyone]), sides)
+    grad_down = jnp.where(second == 0, part, other).astype(F32).T
+    grad_up = jnp.where(second == 0, other, part).astype(F32)
+
+    from_left, from_right = after((from_left, from_right), projected, grad_down, grad_up)
     cell = jnp.arange(TILE, dtype=jnp.int32)
     mark = jnp.arange(32, dtype=jnp.int32)
     source = jnp.where(

time: 173 us -> 166 us (0.960)
  Pallas kernels: 48.3 us -> 40.3 us
  waiting for transfers between devices: 48.9 us -> 54.9 us
  local copies, waits for them, and re-layouts: 16.2 us -> 11.2 us
    ppermute x16, waiting for transfers between devices: 25.1 us -> 43 us  [permute(): return lax.ppermute(block, 'tensor', route)]
    ppermute x25 -> x28, waiting for transfers between devices: 23.7 us -> 11.9 us  [swap(): lax.ppermute(block, ('groups', 'tensor'), [(g * devices + i, (g ^ group_b...]
    pallas_call x2, Pallas kernels: 22.1 us -> 14.6 us  [from_hbm(): return call(scalars, *in_hbm(arrays[:3]), *arrays[3:])]
    unnamed x74 -> x70, local copies, waits for them, and re-layouts: 13.5 us -> 7.44 us
    ppermute x16, starting transfers between devices: 16.1 us -> 14 us  [permute(): return lax.ppermute(block, 'tensor', route)]
    slice x0 -> x2, local copies, waits for them, and re-layouts: none -> 1.79 us  [the longest x1 1.02 us: on_device(): upper = swap(after(across[:TILE // 2], to_outer), 0, 2)]
    ppermute x25 -> x28, starting transfers between devices: 27.4 us -> 29.1 us  [swap(): lax.ppermute(block, ('groups', 'tensor'), [(g * devices + i, (g ^ group_b...]
    add x3 -> x4, other arithmetic: 3.15 us -> 3.8 us  [the longest x2 2.74 us: on_device(): keep.astype(F32) + block.astype(F32)]
  transfers between devices with their start and end apart: 41 -> 44, of which waited for: 14 -> 14; matrix products, arithmetic and copies ran while one was open for 8% -> 9% of each run, Pallas kernels for 24% -> 24%
where the time goes in v3:
time: 166 us; the launch traced here: 165 us
  waiting for transfers between devices  54.9 us (33%)
  starting transfers between devices  43.1 us (26%)
  Pallas kernels  40.3 us (24%)
  local copies, waits for them, and re-layouts  11.2 us (7%)
  matrix products  7.09 us (4%)
  other arithmetic  6.99 us (4%)
    ppermute x16, waiting for transfers between devices, permute(): return lax.ppermute(block, 'tensor', route)  43 us
    ppermute x28, starting transfers between devices, swap(): lax.ppermute(block, ('groups', 'tensor'), [(g * devices + i, (g ^ group_b...  29.1 us
    pallas_call x2, Pallas kernels, from_hbm(): return call(scalars, *in_hbm(arrays[:3]), *arrays[3:])  14.6 us
    ppermute x16, starting transfers between devices, permute(): return lax.ppermute(block, 'tensor', route)  14 us
    pallas_call x4, Pallas kernels, project(): plain_call(functools.partial(project_kernel, len(weights), core, kept), (...  13 us
    ppermute x28, waiting for transfers between devices, swap(): lax.ppermute(block, ('groups', 'tensor'), [(g * devices + i, (g ^ group_b...  11.9 us
    unnamed x70, local copies, waits for them, and re-layouts  7.44 us
    dot_general x4, matrix products, tn(): lax.dot_general(a, b, (((0,), (0,)), ((), ())), preferred_element_type=F32)  5.52 us
  transfers between devices with their start and end apart: 44, of which 14 were waited for; matrix products, arithmetic and copies ran while one was open for 9% of the time, Pallas kernels for 24%

profile of v3, /device:TPU:0, one launch (start us, length us, event | category | flops | bytes accessed | tf_op | source)
XLA Modules:
  0.0 164.9 jit_solution(15048109439466498592)
XLA Ops:
  1.3 3.7 %shard_map.136 = (bf16[16,3072]{1,0:T(8,128)(2,1)}, bf16[16,3072]{1,0:T(8,128)(2,1)}, bf16[32,3072]{1,0:T(8,128)(2,1)}) custom-call(s32[1]{0:T(128)} %bitcast.where, bf16[128,3072]{1,0:T(8,128)(2,1)} %refs_0_.3, bf16[128,3072]{1,0:T(8,128)(2,1)} %refs_1_.3), custom_call_target="tpu_custom_call" | custom-call | flops 1000 | bytes 1000 | tf_op jit(solution)/shard_map/pallas_call | solution.py:347
  5.8 4.0 %collective-permute-start.1 = (bf16[48,3072]{1,0:T(8,128)(2,1)}, bf16[48,3072]{1,0:T(8,128)(2,1)}, u32[]{:S(2)}, u32[]{:S(2)}) collective-permute-start(bf16[48,3072]{1,0:T(8,128)(2,1)} %get-tuple-element.88), channel_id=1, source_target_pairs={{0,8},{1,9},{2,10},{3,11},{4,12},{5,13},{6,14},{7,15},{8,0},{9,1},... | collective-permute-start | bytes 884744 | tf_op jit(solution)/shard_map/ppermute | solution.py:505
  10.7 1.6 collective-permute-start
  12.3 1.5 collective-permute-start.6
  14.5 1.6 fusion.2.refs_8_
  16.1 1.5 convolution_bitcast_fusion.refs_9_
  17.7 1.3 collective-permute-start.5
  19.0 4.6 %collective-permute-start.4 = (bf16[16,3072]{1,0:T(8,128)(2,1)S(1)}, bf16[16,3072]{1,0:T(8,128)(2,1)S(1)}, u32[]{:S(2)}, u32[]{:S(2)}) collective-permute-start(bf16[16,3072]{1,0:T(8,128)(2,1)S(1)} %copy-done.31), channel_id=1, source_target_pairs={{0,2},{1,3},{2,4},{3,5},{4,6},{5,7},{8,10},{9,11},{10,12},{11,13},... | collective-permute-start | bytes 294920 | tf_op jit(solution)/shard_map/ppermute | solution.py:500
  23.8 8.4 %collective-permute-done.refs_1_ = bf16[96,3072]{1,0:T(8,128)(2,1)} collective-permute-done((bf16[96,3072]{1,0:T(8,128)(2,1)}, bf16[96,3072]{1,0:T(8,128)(2,1)}, u32[]{:S(2)}, u32[]{:S(2)}) %collective-permute-start) | collective-permute-done | bytes 589856 | tf_op jit(solution)/shard_map/ppermute | solution.py:505
  32.5 2.4 %collective-permute-start.10 = (bf16[128,3072]{1,0:T(8,128)(2,1)}, bf16[128,3072]{1,0:T(8,128)(2,1)S(1)}, u32[]{:S(2)}, u32[]{:S(2)}) collective-permute-start(bf16[128,3072]{1,0:T(8,128)(2,1)} %refs_6_.1), channel_id=1, source_target_pairs={{0,2},{1,3},{2,0},{3,1},{4,6},{5,7},{6,4},{7,5},{8,10},{9,11},{10,... | collective-permute-start | bytes 2359304 | tf_op jit(solution)/shard_map/ppermute | solution.py:505
  35.0 1.0 slice.148
  36.1 2.1 %collective-permute-start.8 = (bf16[48,3072]{1,0:T(8,128)(2,1)}, bf16[48,3072]{1,0:T(8,128)(2,1)S(1)}, u32[]{:S(2)}, u32[]{:S(2)}) collective-permute-start(bf16[48,3072]{1,0:T(8,128)(2,1)} %collective-permute-done.1.refs_2_), channel_id=1, source_target_pairs={{0,4},{1,5},{2,6},{3,7},{4,0},{5,1},{6,2},{7,3},{8,12},{9,13},{10,... | collective-permute-start | bytes 884744 | tf_op jit(solution)/shard_map/ppermute | solution.py:505
  38.2 2.4 %collective-permute-start.7 = (bf16[48,3072]{1,0:T(8,128)(2,1)S(1)}, bf16[48,3072]{1,0:T(8,128)(2,1)}, u32[]{:S(2)}, u32[]{:S(2)}) collective-permute-start(bf16[48,3072]{1,0:T(8,128)(2,1)S(1)} %copy-done.25), channel_id=1, source_target_pairs={{0,8},{1,9},{2,10},{3,11},{4,12},{5,13},{6,14},{7,15},{8,0},{9,1},... | collective-permute-start | bytes 884744 | tf_op jit(solution)/shard_map/ppermute | solution.py:505
  41.1 22.2 %collective-permute-done.9.outer = bf16[40,3072]{1,0:T(8,128)(2,1)S(1)} collective-permute-done((bf16[40,3072]{1,0:T(8,128)(2,1)S(1)}, bf16[40,3072]{1,0:T(8,128)(2,1)S(1)}, u32[]{:S(2)}, u32[]{:S(2)}) %collective-permute-start.9) | collective-permute-done | bytes 245792 | tf_op jit(solution)/shard_map/ppermute | solution.py:500
  65.8 1.5 collective-permute-start.15
  67.4 1.1 copy-done.3
  68.6 6.7 %shard_map.140 = (bf16[3072,128]{1,0:T(8,128)(2,1)}, f32[3,8,128]{2,1,0:T(8,128)S(1)}, bf16[2,64,3072]{2,1,0:T(8,128)(2,1)S(1)}, bf16[64,128]{1,0:T(8,128)(2,1)S(1)}) custom-call(s32[25]{0:T(128)S(1)} %pad_add_fusion.1.combo, bf16[128,3072]{1,0:T(8,128)(2,1)} %query.1, bf16[128,3072]{1,0:T(8,128)(2,1)} %refs_0_.3, bf16[128,3072]{1,0:T(8,128)(2,1)} %refs_1_.3, ...), custom_call_target="tpu_custom_call" | custom-call | flops 1000 | bytes 1000 | tf_op jit(solution)/shard_map/pallas_call | solution.py:148
  75.3 0.9 collective-permute-done.12.refs_5_
  77.1 1.2 shard_map.141
  80.7 1.5 collective-permute-start.17
  82.5 2.4 %collective-permute-start.19 = (bf16[2,384,128]{2,1,0:T(8,128)(2,1)S(1)}, bf16[2,384,128]{2,1,0:T(8,128)(2,1)S(1)}, u32[]{:S(2)}, u32[]{:S(2)}) collective-permute-start(bf16[2,384,128]{2,1,0:T(8,128)(2,1)S(1)} %get-tuple-element.114), channel_id=1, source_target_pairs={{0,18},{1,19},{2,16},{3,17},{4,22},{5,23},{6,20},{7,21},{8,26},{9,... | collective-permute-start | bytes 589832 | tf_op jit(solution)/shard_map/ppermute | solution.py:505
  86.8 5.3 %shard_map.143 = (bf16[4,384,128]{2,1,0:T(8,128)(2,1)S(1)}, bf16[4,384,128]{2,1,0:T(8,128)(2,1)S(1)}) custom-call(bf16[96,3072]{1,0:T(8,128)(2,1)} %constant_dynamic-slice_fusion.2.refs_0_, bf16[96,3072]{1,0:T(8,128)(2,1)} %collective-permute-done.refs_1_, bf16[48,3072]{1,0:T(8,128)(2,1)} %collective-permute-done.1.refs_2_, ...), custom_call_target="tpu_custom_call" | custom-call | flops 1000 | bytes 1000 | tf_op jit(solution)/shard_map/pallas_call | solution.py:409
  92.2 1.0 collective-permute-done.18.refs_8_
  93.9 2.9 %shard_map.147 = bf16[4,128,1536]{2,1,0:T(8,128)(2,1)S(1)} custom-call(bf16[96,3072]{1,0:T(8,128)(2,1)} %constant_dynamic-slice_fusion.2.refs_0_, bf16[96,3072]{1,0:T(8,128)(2,1)} %collective-permute-done.refs_1_, bf16[48,3072]{1,0:T(8,128)(2,1)} %collective-permute-done.1.refs_2_, bf16[48,3072]{1,0:T(8,128)(2,1)} %collective-permute-done.7.refs_3_, ...), custom_call_target="tpu_custom_call" | custom-call | flops 1000 | bytes 1000 | tf_op jit(solution)/shard_map/pallas_call | solution.py:449
  96.8 2.9 %shard_map.144 = bf16[4,128,1536]{2,1,0:T(8,128)(2,1)S(1)} custom-call(bf16[96,3072]{1,0:T(8,128)(2,1)} %constant_dynamic-slice_fusion.2.refs_0_, bf16[96,3072]{1,0:T(8,128)(2,1)} %collective-permute-done.refs_1_, bf16[48,3072]{1,0:T(8,128)(2,1)} %collective-permute-done.1.refs_2_, bf16[48,3072]{1,0:T(8,128)(2,1)} %collective-permute-done.7.refs_3_, ...), custom_call_target="tpu_custom_call" | custom-call | flops 1000 | bytes 1000 | tf_op jit(solution)/shard_map/pallas_call | solution.py:449
  101.1 1.5 collective-permute-start.31
  102.9 1.6 collective-permute-start.33
  104.5 3.6 %shard_map.148 = (bf16[2,128,1536]{2,1,0:T(8,128)(2,1)S(1)}, bf16[2,128,1536]{2,1,0:T(8,128)(2,1)}) custom-call(bf16[96,3072]{1,0:T(8,128)(2,1)} %constant_dynamic-slice_fusion.2.refs_0_, bf16[96,3072]{1,0:T(8,128)(2,1)} %collective-permute-done.refs_1_, bf16[48,3072]{1,0:T(8,128)(2,1)} %collective-permute-done.1.refs_2_, ...), custom_call_target="tpu_custom_call" | custom-call | flops 1000 | bytes 1000 | tf_op jit(solution)/shard_map/pallas_call | solution.py:449
  108.1 1.6 collective-permute-start.30
  109.7 3.6 %shard_map.146 = (bf16[2,128,1536]{2,1,0:T(8,128)(2,1)S(1)}, bf16[2,128,1536]{2,1,0:T(8,128)(2,1)}) custom-call(bf16[96,3072]{1,0:T(8,128)(2,1)} %constant_dynamic-slice_fusion.2.refs_0_, bf16[96,3072]{1,0:T(8,128)(2,1)} %collective-permute-done.refs_1_, bf16[48,3072]{1,0:T(8,128)(2,1)} %collective-permute-done.1.refs_2_, ...), custom_call_target="tpu_custom_call" | custom-call | flops 1000 | bytes 1000 | tf_op jit(solution)/shard_map/pallas_call | solution.py:449
  116.8 1.3 shard_map.149.refs_8_
  118.3 7.8 %shard_map.150 = (bf16[128,3072]{1,0:T(8,128)(2,1)}, bf16[256,3072]{1,0:T(8,128)(2,1)}, bf16[96,3072]{1,0:T(8,128)(2,1)}, bf16[256,3072]{1,0:T(8,128)(2,1)}, bf16[96,3072]{1,0:T(8,128)(2,1)}) custom-call(s32[25]{0:T(128)S(1)} %pad_add_fusion.1.combo, bf16[128,3072]{1,0:T(8,128)(2,1)} %query.1, bf16[128,3072]{1,0:T(8,128)(2,1)} %refs_0_.3, ...), custom_call_target="tpu_custom_call" | custom-call | flops 1000 | bytes 1000 | tf_op jit(solution)/shard_map/pallas_call | solution.py:148
  126.1 9.4 %collective-permute-done.34 = bf16[64,3072]{1,0:T(8,128)(2,1)} collective-permute-done((bf16[64,3072]{1,0:T(8,128)(2,1)}, bf16[64,3072]{1,0:T(8,128)(2,1)}, u32[]{:S(2)}, u32[]{:S(2)}) %collective-permute-start.34) | collective-permute-done | bytes 393248 | tf_op jit(solution)/shard_map/ppermute | solution.py:500
  135.5 1.2 add_convert_fusion.3
  136.8 1.7 %collective-permute-start.42 = (bf16[64,3072]{1,0:T(8,128)(2,1)S(1)}, bf16[64,3072]{1,0:T(8,128)(2,1)S(1)}, u32[]{:S(2)}, u32[]{:S(2)}) collective-permute-start(bf16[64,3072]{1,0:T(8,128)(2,1)S(1)} %add_convert_fusion.3), channel_id=1, source_target_pairs={{0,2},{1,3},{2,0},{3,1},{4,6},{5,7},{6,4},{7,5},{8,10},{9,11},{10,... | collective-permute-start | bytes 1179656 | tf_op jit(solution)/shard_map/ppermute | solution.py:500
  138.8 1.4 convert_add_fusion.1
  140.3 1.4 collective-permute-start.36
  141.6 1.3 convert_add_fusion
  143.0 1.0 collective-permute-start.37
  144.0 4.7 %collective-permute-done.42 = bf16[64,3072]{1,0:T(8,128)(2,1)S(1)} collective-permute-done((bf16[64,3072]{1,0:T(8,128)(2,1)S(1)}, bf16[64,3072]{1,0:T(8,128)(2,1)S(1)}, u32[]{:S(2)}, u32[]{:S(2)}) %collective-permute-start.42) | collective-permute-done | bytes 393248 | tf_op jit(solution)/shard_map/ppermute | solution.py:500
  148.7 3.8 %collective-permute-done.38 = bf16[36,3072]{1,0:T(8,128)(2,1)S(1)} collective-permute-done((bf16[36,3072]{1,0:T(8,128)(2,1)S(1)}, bf16[36,3072]{1,0:T(8,128)(2,1)S(1)}, u32[]{:S(2)}, u32[]{:S(2)}) %collective-permute-start.38) | collective-permute-done | bytes 221216 | tf_op jit(solution)/shard_map/ppermute | solution.py:500
  152.8 2.7 %collective-permute-start.40 = (bf16[16,3072]{1,0:T(8,128)(2,1)S(1)}, bf16[16,3072]{1,0:T(8,128)(2,1)S(1)}, u32[]{:S(2)}, u32[]{:S(2)}) collective-permute-start(bf16[16,3072]{1,0:T(8,128)(2,1)S(1)} %pad_maximum_fusion.2), channel_id=1, source_target_pairs={{0,2},{1,3},{2,4},{3,5},{4,6},{5,7},{8,10},{9,11},{10,12},{11,13},... | collective-permute-start | bytes 294920 | tf_op jit(solution)/shard_map/ppermute | solution.py:500
  155.6 1.3 collective-permute-start.41
  157.2 1.3 fusion.1
  158.7 1.2 select_convert_fusion
  160.0 2.1 %collective-permute-done.41 = bf16[16,3072]{1,0:T(8,128)(2,1)S(1)} collective-permute-done((bf16[16,3072]{1,0:T(8,128)(2,1)S(1)}, bf16[16,3072]{1,0:T(8,128)(2,1)S(1)}, u32[]{:S(2)}, u32[]{:S(2)}) %collective-permute-start.41) | collective-permute-done | bytes 98336 | tf_op jit(solution)/shard_map/ppermute | solution.py:500
  162.2 1.4 add_convert_fusion
  163.5 1.4 add_convert_fusion.1
  (162 shorter events, 19.4 us)
Async XLA Ops:
  0.6 13.8 %copy-start = (bf16[64,3072]{1,0:T(8,128)(2,1)S(1)}, bf16[64,3072]{1,0:T(8,128)(2,1)}, u32[]{:S(2)}) copy-start(bf16[64,3072]{1,0:T(8,128)(2,1)} %param.14) | copy-start | bytes 1179652
  0.7 17.0 %collective-permute-start.2 = (bf16[128,3072]{1,0:T(8,128)(2,1)}, bf16[128,3072]{1,0:T(8,128)(2,1)S(1)}, u32[]{:S(2)}, u32[]{:S(2)}) collective-permute-start(bf16[128,3072]{1,0:T(8,128)(2,1)} %refs_0_.3), channel_id=1, source_target_pairs={{0,1},{1,0},{2,3},{3,2},{4,5},{5,4},{6,7},{7,6},{8,9},{9,8},{10,11... | collective-permute-start | bytes 2359304 | tf_op jit(solution)/shard_map/ppermute | solution.py:500
  1.2 16.5 %collective-permute-start.3 = (bf16[128,3072]{1,0:T(8,128)(2,1)}, bf16[128,3072]{1,0:T(8,128)(2,1)}, u32[]{:S(2)}, u32[]{:S(2)}) collective-permute-start(bf16[128,3072]{1,0:T(8,128)(2,1)} %refs_1_.3), channel_id=1, source_target_pairs={{0,1},{1,0},{2,3},{3,2},{4,5},{5,4},{6,7},{7,6},{8,9},{9,8},{10,11... | collective-permute-start | bytes 2359304 | tf_op jit(solution)/shard_map/ppermute | solution.py:500
  5.8 18.0 %collective-permute-start.1 = (bf16[48,3072]{1,0:T(8,128)(2,1)}, bf16[48,3072]{1,0:T(8,128)(2,1)}, u32[]{:S(2)}, u32[]{:S(2)}) collective-permute-start(bf16[48,3072]{1,0:T(8,128)(2,1)} %get-tuple-element.88), channel_id=1, source_target_pairs={{0,8},{1,9},{2,10},{3,11},{4,12},{5,13},{6,14},{7,15},{8,0},{9,1},... | collective-permute-start | bytes 884744 | tf_op jit(solution)/shard_map/ppermute | solution.py:505
  10.7 21.6 %collective-permute-start = (bf16[96,3072]{1,0:T(8,128)(2,1)}, bf16[96,3072]{1,0:T(8,128)(2,1)}, u32[]{:S(2)}, u32[]{:S(2)}) collective-permute-start(bf16[96,3072]{1,0:T(8,128)(2,1)} %constant_dynamic-slice_fusion.2.refs_0_), channel_id=1, source_target_pairs={{0,4},{1,5},{2,6},{3,7},{4,0},{5,1},{6,2},{7,3},{8,12},{9,13},{10,... | collective-permute-start | bytes 1769480 | tf_op jit(solution)/shard_map/ppermute | solution.py:505
  12.3 19.9 %collective-permute-start.6 = (bf16[128,3072]{1,0:T(8,128)(2,1)}, bf16[128,3072]{1,0:T(8,128)(2,1)}, u32[]{:S(2)}, u32[]{:S(2)}) collective-permute-start(bf16[128,3072]{1,0:T(8,128)(2,1)} %refs_6_.1), channel_id=1, source_target_pairs={{0,16},{1,17},{2,18},{3,19},{4,20},{5,21},{6,22},{7,23},{8,24},{9,... | collective-permute-start | bytes 2359304 | tf_op jit(solution)/shard_map/ppermute | solution.py:505
  14.5 17.7 %copy-start.9 = (bf16[32,3072]{1,0:T(8,128)(2,1)S(1)}, bf16[32,3072]{1,0:T(8,128)(2,1)}, u32[]{:S(2)}) copy-start(bf16[32,3072]{1,0:T(8,128)(2,1)} %get-tuple-element.86.edge) | copy-start | bytes 589828
  16.1 22.1 %copy-start.25 = (bf16[48,3072]{1,0:T(8,128)(2,1)S(1)}, bf16[48,3072]{1,0:T(8,128)(2,1)}, u32[]{:S(2)}) copy-start(bf16[48,3072]{1,0:T(8,128)(2,1)} %get-tuple-element.95) | copy-start | bytes 884740
  17.7 45.7 %copy-start.2 = (bf16[128,3072]{1,0:T(8,128)(2,1)}, bf16[128,3072]{1,0:T(8,128)(2,1)S(1)}, u32[]{:S(2)}) copy-start(bf16[128,3072]{1,0:T(8,128)(2,1)S(1)} %collective-permute-done.2.refs_3_) | copy-start | bytes 2359300
  17.7 14.6 %collective-permute-start.5 = (bf16[16,3072]{1,0:T(8,128)(2,1)S(1)}, bf16[16,3072]{1,0:T(8,128)(2,1)S(1)}, u32[]{:S(2)}, u32[]{:S(2)}) collective-permute-start(bf16[16,3072]{1,0:T(8,128)(2,1)S(1)} %copy-done.32), channel_id=1, source_target_pairs={{2,0},{3,1},{4,2},{5,3},{6,4},{7,5},{10,8},{11,9},{12,10},{13,11},... | collective-permute-start | bytes 294920 | tf_op jit(solution)/shard_map/ppermute | solution.py:500
  19.0 13.2 %collective-permute-start.4 = (bf16[16,3072]{1,0:T(8,128)(2,1)S(1)}, bf16[16,3072]{1,0:T(8,128)(2,1)S(1)}, u32[]{:S(2)}, u32[]{:S(2)}) collective-permute-start(bf16[16,3072]{1,0:T(8,128)(2,1)S(1)} %copy-done.31), channel_id=1, source_target_pairs={{0,2},{1,3},{2,4},{3,5},{4,6},{5,7},{8,10},{9,11},{10,12},{11,13},... | collective-permute-start | bytes 294920 | tf_op jit(solution)/shard_map/ppermute | solution.py:500
  32.5 30.8 %collective-permute-start.10 = (bf16[128,3072]{1,0:T(8,128)(2,1)}, bf16[128,3072]{1,0:T(8,128)(2,1)S(1)}, u32[]{:S(2)}, u32[]{:S(2)}) collective-permute-start(bf16[128,3072]{1,0:T(8,128)(2,1)} %refs_6_.1), channel_id=1, source_target_pairs={{0,2},{1,3},{2,0},{3,1},{4,6},{5,7},{6,4},{7,5},{8,10},{9,11},{10,... | collective-permute-start | bytes 2359304 | tf_op jit(solution)/shard_map/ppermute | solution.py:505
  36.0 27.3 %collective-permute-start.11 = (bf16[64,3072]{1,0:T(8,128)(2,1)S(1)}, bf16[64,3072]{1,0:T(8,128)(2,1)S(1)}, u32[]{:S(2)}, u32[]{:S(2)}) collective-permute-start(bf16[64,3072]{1,0:T(8,128)(2,1)S(1)} %slice.148), channel_id=1, source_target_pairs={{0,2},{1,3},{2,0},{3,1},{4,6},{5,7},{6,4},{7,5},{8,10},{9,11},{10,... | collective-permute-start | bytes 1179656 | tf_op jit(solution)/shard_map/ppermute | solution.py:505
  36.1 27.2 %collective-permute-start.8 = (bf16[48,3072]{1,0:T(8,128)(2,1)}, bf16[48,3072]{1,0:T(8,128)(2,1)S(1)}, u32[]{:S(2)}, u32[]{:S(2)}) collective-permute-start(bf16[48,3072]{1,0:T(8,128)(2,1)} %collective-permute-done.1.refs_2_), channel_id=1, source_target_pairs={{0,4},{1,5},{2,6},{3,7},{4,0},{5,1},{6,2},{7,3},{8,12},{9,13},{10,... | collective-permute-start | bytes 884744 | tf_op jit(solution)/shard_map/ppermute | solution.py:505
  38.2 25.1 %collective-permute-start.7 = (bf16[48,3072]{1,0:T(8,128)(2,1)S(1)}, bf16[48,3072]{1,0:T(8,128)(2,1)}, u32[]{:S(2)}, u32[]{:S(2)}) collective-permute-start(bf16[48,3072]{1,0:T(8,128)(2,1)S(1)} %copy-done.25), channel_id=1, source_target_pairs={{0,8},{1,9},{2,10},{3,11},{4,12},{5,13},{6,14},{7,15},{8,0},{9,1},... | collective-permute-start | bytes 884744 | tf_op jit(solution)/shard_map/ppermute | solution.py:505
  40.7 22.7 %collective-permute-start.9 = (bf16[40,3072]{1,0:T(8,128)(2,1)S(1)}, bf16[40,3072]{1,0:T(8,128)(2,1)S(1)}, u32[]{:S(2)}, u32[]{:S(2)}) collective-permute-start(bf16[40,3072]{1,0:T(8,128)(2,1)S(1)} %shard_map.138), channel_id=1, source_target_pairs={{0,8},{1,9},{2,10},{3,11},{4,12},{5,13},{6,14},{7,15},{8,0},{9,1},... | collective-permute-start | bytes 737288 | tf_op jit(solution)/shard_map/ppermute | solution.py:500
  64.2 3.2 %collective-permute-start.13 = (bf16[128,3072]{1,0:T(8,128)(2,1)}, bf16[128,3072]{1,0:T(8,128)(2,1)}, u32[]{:S(2)}, u32[]{:S(2)}) collective-permute-start(bf16[128,3072]{1,0:T(8,128)(2,1)} %collective-permute-done.6.refs_8_), channel_id=1, source_target_pairs={{0,1},{1,0},{2,3},{3,2},{4,5},{5,4},{6,7},{7,6},{8,9},{9,8},{10,11... | collective-permute-start | bytes 2359304 | tf_op jit(solution)/shard_map/ppermute | solution.py:505
  64.4 3.0 %collective-permute-start.14 = (bf16[96,3072]{1,0:T(8,128)(2,1)S(1)}, bf16[96,3072]{1,0:T(8,128)(2,1)}, u32[]{:S(2)}, u32[]{:S(2)}) collective-permute-start(bf16[96,3072]{1,0:T(8,128)(2,1)S(1)} %shard_map.139.refs_2_), channel_id=1, source_target_pairs={{0,1},{1,0},{2,3},{3,2},{4,5},{5,4},{6,7},{7,6},{8,9},{9,8},{10,11... | collective-permute-start | bytes 1769480 | tf_op jit(solution)/shard_map/ppermute | solution.py:500
  65.8 11.3 %collective-permute-start.15 = (bf16[64,3072]{1,0:T(8,128)(2,1)}, bf16[64,3072]{1,0:T(8,128)(2,1)}, u32[]{:S(2)}, u32[]{:S(2)}) collective-permute-start(bf16[64,3072]{1,0:T(8,128)(2,1)} %slice.149), channel_id=1, source_target_pairs={{0,16},{1,17},{2,18},{3,19},{4,20},{5,21},{6,22},{7,23},{8,24},{9,... | collective-permute-start | bytes 1179656 | tf_op jit(solution)/shard_map/ppermute | solution.py:505
  67.3 8.9 %collective-permute-start.12 = (bf16[48,3072]{1,0:T(8,128)(2,1)}, bf16[48,3072]{1,0:T(8,128)(2,1)}, u32[]{:S(2)}, u32[]{:S(2)}) collective-permute-start(bf16[48,3072]{1,0:T(8,128)(2,1)} %collective-permute-done.7.refs_3_), channel_id=1, source_target_pairs={{0,4},{1,5},{2,6},{3,7},{4,0},{5,1},{6,2},{7,3},{8,12},{9,13},{10,... | collective-permute-start | bytes 884744 | tf_op jit(solution)/shard_map/ppermute | solution.py:505
  78.3 1.8 %collective-permute-start.16 = (bf16[4,384,128]{2,1,0:T(8,128)(2,1)S(1)}, bf16[4,384,128]{2,1,0:T(8,128)(2,1)S(1)}, u32[]{:S(2)}, u32[]{:S(2)}) collective-permute-start(bf16[4,384,128]{2,1,0:T(8,128)(2,1)S(1)} %get-tuple-element.110), channel_id=1, source_target_pairs={{0,1},{1,0},{2,3},{3,2},{4,5},{5,4},{6,7},{7,6},{8,9},{9,8},{10,11... | collective-permute-start | bytes 1179656 | tf_op jit(solution)/shard_map/ppermute | solution.py:505
  78.4 2.2 %collective-permute-start.25 = (bf16[64,3072]{1,0:T(8,128)(2,1)S(1)}, bf16[64,3072]{1,0:T(8,128)(2,1)S(1)}, u32[]{:S(2)}, u32[]{:S(2)}) collective-permute-start(bf16[64,3072]{1,0:T(8,128)(2,1)S(1)} %slice_bitcast_fusion.2), channel_id=1, source_target_pairs={{0,1},{1,0},{2,3},{3,2},{4,5},{5,4},{6,7},{7,6},{8,9},{9,8},{10,11... | collective-permute-start | bytes 1179656 | tf_op jit(solution)/shard_map/ppermute | solution.py:500
  79.0 3.2 %collective-permute-start.23 = (bf16[64,3072]{1,0:T(8,128)(2,1)}, bf16[64,3072]{1,0:T(8,128)(2,1)S(1)}, u32[]{:S(2)}, u32[]{:S(2)}) collective-permute-start(bf16[64,3072]{1,0:T(8,128)(2,1)} %collective-permute-done.15.refs_13_), channel_id=1, source_target_pairs={{0,1},{1,0},{2,3},{3,2},{4,5},{5,4},{6,7},{7,6},{8,9},{9,8},{10,11... | collective-permute-start | bytes 1179656 | tf_op jit(solution)/shard_map/ppermute | solution.py:505
  79.1 3.5 %collective-permute-start.22 = (bf16[64,3072]{1,0:T(8,128)(2,1)S(1)}, bf16[64,3072]{1,0:T(8,128)(2,1)S(1)}, u32[]{:S(2)}, u32[]{:S(2)}) collective-permute-start(bf16[64,3072]{1,0:T(8,128)(2,1)S(1)} %copy-done.22), channel_id=1, source_target_pairs={{0,1},{1,0},{2,3},{3,2},{4,5},{5,4},{6,7},{7,6},{8,9},{9,8},{10,11... | collective-permute-start | bytes 1179656 | tf_op jit(solution)/shard_map/ppermute | solution.py:505
  79.5 5.6 %collective-permute-start.21 = (bf16[128,3072]{1,0:T(8,128)(2,1)S(1)}, bf16[128,3072]{1,0:T(8,128)(2,1)S(1)}, u32[]{:S(2)}, u32[]{:S(2)}) collective-permute-start(bf16[128,3072]{1,0:T(8,128)(2,1)S(1)} %copy-done.16), channel_id=1, source_target_pairs={{0,1},{1,0},{2,3},{3,2},{4,5},{5,4},{6,7},{7,6},{8,9},{9,8},{10,11... | collective-permute-start | bytes 2359304 | tf_op jit(solution)/shard_map/ppermute | solution.py:505
  80.1 5.1 %collective-permute-start.20 = (bf16[128,3072]{1,0:T(8,128)(2,1)}, bf16[128,3072]{1,0:T(8,128)(2,1)S(1)}, u32[]{:S(2)}, u32[]{:S(2)}) collective-permute-start(bf16[128,3072]{1,0:T(8,128)(2,1)} %refs_6_.1), channel_id=1, source_target_pairs={{0,1},{1,0},{2,3},{3,2},{4,5},{5,4},{6,7},{7,6},{8,9},{9,8},{10,11... | collective-permute-start | bytes 2359304 | tf_op jit(solution)/shard_map/ppermute | solution.py:505
  80.7 11.5 %collective-permute-start.17 = (bf16[2,384,128]{2,1,0:T(8,128)(2,1)S(1)}, bf16[2,384,128]{2,1,0:T(8,128)(2,1)S(1)}, u32[]{:S(2)}, u32[]{:S(2)}) collective-permute-start(bf16[2,384,128]{2,1,0:T(8,128)(2,1)S(1)} %get-tuple-element.112), channel_id=1, source_target_pairs={{0,16},{1,17},{2,18},{3,19},{4,20},{5,21},{6,22},{7,23},{8,24},{9,... | collective-permute-start | bytes 589832 | tf_op jit(solution)/shard_map/ppermute | solution.py:505
  82.2 11.0 %collective-permute-start.18 = (bf16[2,384,128]{2,1,0:T(8,128)(2,1)S(1)}, bf16[2,384,128]{2,1,0:T(8,128)(2,1)S(1)}, u32[]{:S(2)}, u32[]{:S(2)}) collective-permute-start(bf16[2,384,128]{2,1,0:T(8,128)(2,1)S(1)} %get-tuple-element.113), channel_id=1, source_target_pairs={{0,2},{1,3},{2,0},{3,1},{4,6},{5,7},{6,4},{7,5},{8,10},{9,11},{10,... | collective-permute-start | bytes 589832 | tf_op jit(solution)/shard_map/ppermute | solution.py:505
  82.5 10.6 %collective-permute-start.19 = (bf16[2,384,128]{2,1,0:T(8,128)(2,1)S(1)}, bf16[2,384,128]{2,1,0:T(8,128)(2,1)S(1)}, u32[]{:S(2)}, u32[]{:S(2)}) collective-permute-start(bf16[2,384,128]{2,1,0:T(8,128)(2,1)S(1)} %get-tuple-element.114), channel_id=1, source_target_pairs={{0,18},{1,19},{2,16},{3,17},{4,22},{5,23},{6,20},{7,21},{8,26},{9,... | collective-permute-start | bytes 589832 | tf_op jit(solution)/shard_map/ppermute | solution.py:505
  85.1 14.7 %collective-permute-start.26 = (bf16[64,3072]{1,0:T(8,128)(2,1)S(1)}, bf16[64,3072]{1,0:T(8,128)(2,1)S(1)}, u32[]{:S(2)}, u32[]{:S(2)}) collective-permute-start(bf16[64,3072]{1,0:T(8,128)(2,1)S(1)} %fusion.5), channel_id=1, source_target_pairs={{0,4},{1,5},{2,6},{3,7},{4,0},{5,1},{6,2},{7,3},{8,12},{9,13},{10,... | collective-permute-start | bytes 1179656 | tf_op jit(solution)/shard_map/ppermute | solution.py:500
  93.2 6.6 %collective-permute-start.24 = (bf16[4,384,128]{2,1,0:T(8,128)(2,1)S(1)}, bf16[4,384,128]{2,1,0:T(8,128)(2,1)S(1)}, u32[]{:S(2)}, u32[]{:S(2)}) collective-permute-start(bf16[4,384,128]{2,1,0:T(8,128)(2,1)S(1)} %get-tuple-element.125), channel_id=1, source_target_pairs={{0,1},{1,0},{2,3},{3,2},{4,5},{5,4},{6,7},{7,6},{8,9},{9,8},{10,11... | collective-permute-start | bytes 1179656 | tf_op jit(solution)/shard_map/ppermute | solution.py:505
  100.5 4.0 %collective-permute-start.29 = (bf16[4,128,1536]{2,1,0:T(8,128)(2,1)S(1)}, bf16[4,128,1536]{2,1,0:T(8,128)(2,1)S(1)}, u32[]{:S(2)}, u32[]{:S(2)}) collective-permute-start(bf16[4,128,1536]{2,1,0:T(8,128)(2,1)S(1)} %shard_map.147), channel_id=1, source_target_pairs={{0,1},{1,0},{2,3},{3,2},{4,5},{5,4},{6,7},{7,6},{8,9},{9,8},{10,11... | collective-permute-start | bytes 4718600 | tf_op jit(solution)/shard_map/ppermute | solution.py:505
  100.5 9.1 %collective-permute-start.27 = (bf16[4,128,1536]{2,1,0:T(8,128)(2,1)S(1)}, bf16[4,128,1536]{2,1,0:T(8,128)(2,1)S(1)}, u32[]{:S(2)}, u32[]{:S(2)}) collective-permute-start(bf16[4,128,1536]{2,1,0:T(8,128)(2,1)S(1)} %shard_map.144), channel_id=1, source_target_pairs={{0,1},{1,0},{2,3},{3,2},{4,5},{5,4},{6,7},{7,6},{8,9},{9,8},{10,11... | collective-permute-start | bytes 4718600 | tf_op jit(solution)/shard_map/ppermute | solution.py:505
  101.1 14.3 %collective-permute-start.31 = (bf16[2,384,128]{2,1,0:T(8,128)(2,1)S(1)}, bf16[2,384,128]{2,1,0:T(8,128)(2,1)S(1)}, u32[]{:S(2)}, u32[]{:S(2)}) collective-permute-start(bf16[2,384,128]{2,1,0:T(8,128)(2,1)S(1)} %get-tuple-element.127), channel_id=1, source_target_pairs={{0,16},{1,17},{2,18},{3,19},{4,20},{5,21},{6,22},{7,23},{8,24},{9,... | collective-permute-start | bytes 589832 | tf_op jit(solution)/shard_map/ppermute | solution.py:505
  102.6 12.9 %collective-permute-start.32 = (bf16[2,384,128]{2,1,0:T(8,128)(2,1)S(1)}, bf16[2,384,128]{2,1,0:T(8,128)(2,1)S(1)}, u32[]{:S(2)}, u32[]{:S(2)}) collective-permute-start(bf16[2,384,128]{2,1,0:T(8,128)(2,1)S(1)} %get-tuple-element.128), channel_id=1, source_target_pairs={{0,2},{1,3},{2,0},{3,1},{4,6},{5,7},{6,4},{7,5},{8,10},{9,11},{10,... | collective-permute-start | bytes 589832 | tf_op jit(solution)/shard_map/ppermute | solution.py:505
  102.9 12.5 %collective-permute-start.33 = (bf16[2,384,128]{2,1,0:T(8,128)(2,1)S(1)}, bf16[2,384,128]{2,1,0:T(8,128)(2,1)S(1)}, u32[]{:S(2)}, u32[]{:S(2)}) collective-permute-start(bf16[2,384,128]{2,1,0:T(8,128)(2,1)S(1)} %get-tuple-element.129), channel_id=1, source_target_pairs={{0,18},{1,19},{2,16},{3,17},{4,22},{5,23},{6,20},{7,21},{8,26},{9,... | collective-permute-start | bytes 589832 | tf_op jit(solution)/shard_map/ppermute | solution.py:505
  108.1 27.4 %collective-permute-start.30 = (bf16[2,128,1536]{2,1,0:T(8,128)(2,1)}, bf16[2,128,1536]{2,1,0:T(8,128)(2,1)}, u32[]{:S(2)}, u32[]{:S(2)}) collective-permute-start(bf16[2,128,1536]{2,1,0:T(8,128)(2,1)} %get-tuple-element.136), channel_id=1, source_target_pairs={{0,16},{1,17},{2,18},{3,19},{4,20},{5,21},{6,22},{7,23},{8,24},{9,... | collective-permute-start | bytes 2359304 | tf_op jit(solution)/shard_map/ppermute | solution.py:505
  114.1 21.4 %collective-permute-start.28 = (bf16[2,128,1536]{2,1,0:T(8,128)(2,1)}, bf16[2,128,1536]{2,1,0:T(8,128)(2,1)}, u32[]{:S(2)}, u32[]{:S(2)}) collective-permute-start(bf16[2,128,1536]{2,1,0:T(8,128)(2,1)} %get-tuple-element.134), channel_id=1, source_target_pairs={{0,2},{1,3},{2,0},{3,1},{4,6},{5,7},{6,4},{7,5},{8,10},{9,11},{10,... | collective-permute-start | bytes 2359304 | tf_op jit(solution)/shard_map/ppermute | solution.py:505
  116.8 18.7 %collective-permute-start.34 = (bf16[64,3072]{1,0:T(8,128)(2,1)}, bf16[64,3072]{1,0:T(8,128)(2,1)}, u32[]{:S(2)}, u32[]{:S(2)}) collective-permute-start(bf16[64,3072]{1,0:T(8,128)(2,1)} %convert_add_fusion.4), channel_id=1, source_target_pairs={{0,8},{1,9},{2,10},{3,11},{4,12},{5,13},{6,14},{7,15},{8,0},{9,1},... | collective-permute-start | bytes 1179656 | tf_op jit(solution)/shard_map/ppermute | solution.py:500
  135.5 2.9 %collective-permute-start.35 = (bf16[96,3072]{1,0:T(8,128)(2,1)}, bf16[96,3072]{1,0:T(8,128)(2,1)S(1)}, u32[]{:S(2)}, u32[]{:S(2)}) collective-permute-start(bf16[96,3072]{1,0:T(8,128)(2,1)} %get-tuple-element.151), channel_id=1, source_target_pairs={{1,0},{0,1},{3,2},{2,3},{5,4},{4,5},{7,6},{6,7},{9,8},{8,9},{11,10... | collective-permute-start | bytes 1769480 | tf_op jit(solution)/shard_map/ppermute | solution.py:500
  136.8 12.0 %collective-permute-start.42 = (bf16[64,3072]{1,0:T(8,128)(2,1)S(1)}, bf16[64,3072]{1,0:T(8,128)(2,1)S(1)}, u32[]{:S(2)}, u32[]{:S(2)}) collective-permute-start(bf16[64,3072]{1,0:T(8,128)(2,1)S(1)} %add_convert_fusion.3), channel_id=1, source_target_pairs={{0,2},{1,3},{2,0},{3,1},{4,6},{5,7},{6,4},{7,5},{8,10},{9,11},{10,... | collective-permute-start | bytes 1179656 | tf_op jit(solution)/shard_map/ppermute | solution.py:500
  138.7 13.8 %collective-permute-start.38 = (bf16[36,3072]{1,0:T(8,128)(2,1)S(1)}, bf16[36,3072]{1,0:T(8,128)(2,1)S(1)}, u32[]{:S(2)}, u32[]{:S(2)}) collective-permute-start(bf16[36,3072]{1,0:T(8,128)(2,1)S(1)} %pad_maximum_fusion), channel_id=1, source_target_pairs={{0,8},{1,9},{2,10},{3,11},{4,12},{5,13},{6,14},{7,15},{8,0},{9,1},... | collective-permute-start | bytes 663560 | tf_op jit(solution)/shard_map/ppermute | solution.py:500
  140.3 16.7 %collective-permute-start.36 = (bf16[128,1536]{1,0:T(8,128)(2,1)S(1)}, bf16[128,1536]{1,0:T(8,128)(2,1)S(1)}, u32[]{:S(2)}, u32[]{:S(2)}) collective-permute-start(bf16[128,1536]{1,0:T(8,128)(2,1)S(1)} %fusion.6), channel_id=1, source_target_pairs={{0,16},{1,17},{2,18},{3,19},{4,20},{5,21},{6,22},{7,23},{8,24},{9,... | collective-permute-start | bytes 1179656 | tf_op jit(solution)/shard_map/ppermute | solution.py:505
  143.0 13.9 %collective-permute-start.37 = (bf16[128,1536]{1,0:T(8,128)(2,1)S(1)}, bf16[128,1536]{1,0:T(8,128)(2,1)S(1)}, u32[]{:S(2)}, u32[]{:S(2)}) collective-permute-start(bf16[128,1536]{1,0:T(8,128)(2,1)S(1)} %fusion.7), channel_id=1, source_target_pairs={{0,2},{1,3},{2,0},{3,1},{4,6},{5,7},{6,4},{7,5},{8,10},{9,11},{10,... | collective-permute-start | bytes 1179656 | tf_op jit(solution)/shard_map/ppermute | solution.py:505
  144.0 18.2 %collective-permute-start.39 = (bf16[256,3072]{1,0:T(8,128)(2,1)S(1)}, bf16[256,3072]{1,0:T(8,128)(2,1)S(1)}, u32[]{:S(2)}, u32[]{:S(2)}) collective-permute-start(bf16[256,3072]{1,0:T(8,128)(2,1)S(1)} %copy-done.30), channel_id=1, source_target_pairs={{1,0},{0,1},{3,2},{2,3},{5,4},{4,5},{7,6},{6,7},{9,8},{8,9},{11,10... | collective-permute-start | bytes 4718600 | tf_op jit(solution)/shard_map/ppermute | solution.py:500
  152.8 7.1 %collective-permute-start.40 = (bf16[16,3072]{1,0:T(8,128)(2,1)S(1)}, bf16[16,3072]{1,0:T(8,128)(2,1)S(1)}, u32[]{:S(2)}, u32[]{:S(2)}) collective-permute-start(bf16[16,3072]{1,0:T(8,128)(2,1)S(1)} %pad_maximum_fusion.2), channel_id=1, source_target_pairs={{0,2},{1,3},{2,4},{3,5},{4,6},{5,7},{8,10},{9,11},{10,12},{11,13},... | collective-permute-start | bytes 294920 | tf_op jit(solution)/shard_map/ppermute | solution.py:500
  155.6 6.5 %collective-permute-start.41 = (bf16[16,3072]{1,0:T(8,128)(2,1)S(1)}, bf16[16,3072]{1,0:T(8,128)(2,1)S(1)}, u32[]{:S(2)}, u32[]{:S(2)}) collective-permute-start(bf16[16,3072]{1,0:T(8,128)(2,1)S(1)} %pad_maximum_fusion.1), channel_id=1, source_target_pairs={{2,0},{3,1},{4,2},{5,3},{6,4},{7,5},{10,8},{11,9},{12,10},{13,11},... | collective-permute-start | bytes 294920 | tf_op jit(solution)/shard_map/ppermute | solution.py:500
  157.0 1.8 %collective-permute-start.43 = (bf16[64,3072]{1,0:T(8,128)(2,1)S(1)}, bf16[64,3072]{1,0:T(8,128)(2,1)S(1)}, u32[]{:S(2)}, u32[]{:S(2)}) collective-permute-start(bf16[64,3072]{1,0:T(8,128)(2,1)S(1)} %add_convert_fusion.2), channel_id=1, source_target_pairs={{0,1},{1,0},{2,3},{3,2},{4,5},{5,4},{6,7},{7,6},{8,9},{9,8},{10,11... | collective-permute-start | bytes 1179656 | tf_op jit(solution)/shard_map/ppermute | solution.py:500
  (31 other events, 87.2 us)

commit v4 on v3

--- a/solution.py
+++ b/solution.py
@@ -43,13 +43,14 @@
     return jnp.concatenate(keys, axis=0), jnp.concatenate(values, axis=0)
 
 
-def forward_kernel(n_slots, combo, query, *refs):
+def forward_kernel(n_slots, turns, combo, query, *refs):
     slots = [refs[3 * i : 3 * i + 3] for i in range(n_slots)]
-    bias, down, grad_low, upstream, att_ref, log_ref, grads_ref, low_ref, low_acc = refs[
-        3 * n_slots :
-    ]
+    bias, down, grad_low, upstream, att_ref, log_ref, grads_ref, low_ref = refs[
+        3 * n_slots : 3 * n_slots + 8
+    ]
+    low_acc, members = refs[-1], refs[3 * n_slots + 8 : -1]
     step = pl.program_id(0)
-    last = combo.shape[0] - 1
+    second = combo.shape[0] - 2
 
     @pl.when(step == 0)
     def _():
@@ -69,16 +70,21 @@
         [(block * (1.0 / total)).astype(BF16) for block, total in zip(mixed, totals)]
     )
     att_ref[...] = att
+    if members:
+        rows = STEP * HEAD
+        members[2][pl.ds(pl.multiple_of(step * rows, rows), rows), :] = att
     log_ref[0] = jnp.concatenate([top + jnp.log(total) for top, total in zip(tops, totals)])
     low_acc[...] += nn(down[...], att)
     at = pl.ds(pl.multiple_of(step * STEP * HEAD, STEP * HEAD), STEP * HEAD)
-    grads_ref[combo[last], :, at] = nt(grad_low[...], att).astype(BF16)
+    grads_ref[combo[second], :, at] = nt(grad_low[...], att).astype(BF16)
 
     @pl.when(step == pl.num_programs(0) - 1)
     def _():
         low = low_acc[...].astype(BF16)
         low_ref[...] = low
-        grads_ref[1 - combo[last]] = (ADAPTER * nn(low, upstream[...])).astype(BF16)
+        if members:
+            spread_kernel(turns, combo[second + 1], members[2], *members[:2])
+        grads_ref[1 - combo[second]] = (ADAPTER * nn(low, upstream[...])).astype(BF16)
 
 
 def backward_kernel(n_slots, combo, query, *refs):
@@ -158,13 +164,15 @@
     return [column_block(TILE), column_block(TILE), column_block(2 * RIM)] * n_slots
 
 
-def attend(combo, query, slots, bias, down, grad_low, upstream):
+def attend(combo, query, slots, bias, down, grad_low, upstream, turns):
     tokens, width = query.shape
     heads = width // HEAD
     rank = down.shape[0]
     n_slots = len(slots)
+    aligned = width // (8 * turns) % 16 == 0
+    member = (4, width // 8, tokens)
     return head_call(
-        functools.partial(forward_kernel, n_slots),
+        functools.partial(forward_kernel, n_slots, turns),
         n_slots,
         heads // STEP,
         [column_block(tokens)]
@@ -180,15 +188,20 @@
             pl.BlockSpec((1, STEP, tokens), lambda step, *_: (step, 0, 0)),
             whole((2, rank, width)),
             whole((rank, tokens)),
-        ],
+        ]
+        + [whole(member)] * 2 * aligned,
         [
             pltpu.HBM((width, tokens), BF16),
             jax.ShapeDtypeStruct((heads // STEP, STEP, tokens), F32),
             jax.ShapeDtypeStruct((2, rank, width), BF16),
             jax.ShapeDtypeStruct((rank, tokens), BF16),
-        ],
-        [pltpu.VMEM((rank, tokens), F32)],
-    )(combo, query, *[part for slot in slots for part in slot], bias, *in_hbm([down]), grad_low, *in_hbm([upstream]))
+        ]
+        + [jax.ShapeDtypeStruct(member, BF16)] * 2 * aligned,
+        [pltpu.VMEM((width, tokens), BF16)] * aligned + [pltpu.VMEM((rank, tokens), F32)],
+    )(
+        combo, query, *[part for slot in slots for part in slot], bias, *in_hbm([down]), grad_low,
+        *in_hbm([upstream]),
+    )
 
 
 def attend_back(combo, query, slots, bias, att, grad, extra, log_total):
@@ -247,7 +260,7 @@
     size = rows_ref.shape[0] // (8 * turns)
     for number, member in enumerate(MEMBERS):
         for turn in range(turns):
-            at = pl.multiple_of((block_of(member, turn) ^ me[0]) * size, size)
+            at = pl.multiple_of((block_of(member, turn) ^ me) * size, size)
             outs[number % 2][number // 2, turn * size : (turn + 1) * size, :] = rows_ref[
                 pl.ds(at, size), :
             ]
@@ -269,19 +282,11 @@
 def spread(rows, me, turns):
     total, tokens = rows.shape
     size = total // (8 * turns)
-    part = (4, turns * size, tokens)
-    if size % 16:
-        blocks = rows.reshape(8 * turns, size, tokens)
-        order = [[block_of((x, y, c), t) for x, y in PLACES for t in range(turns)] for c in range(2)]
-        return [jnp.take(blocks, me ^ jnp.array(o), axis=0).reshape(part) for o in order]
-    return plain_call(
-        functools.partial(spread_kernel, turns),
-        (1,),
-        [SCALARS, whole(rows.shape)],
-        [whole(part)] * 2,
-        [jax.ShapeDtypeStruct(part, rows.dtype)] * 2,
-        [],
-    )(me[None], *in_hbm([rows]))
+    blocks = rows.reshape(8 * turns, size, tokens)
+    order = [[block_of((x, y, c), t) for x, y in PLACES for t in range(turns)] for c in range(2)]
+    return [
+        jnp.take(blocks, me ^ jnp.array(o), axis=0).reshape(4, turns * size, tokens) for o in order
+    ]
 
 
 def collect(parts, me, turns):
@@ -413,7 +418,7 @@
         [whole((4, rows, TILE))] * 2,
         [jax.ShapeDtypeStruct((4, rows, TILE), BF16)] * 2,
         [pltpu.VMEM((4, rows, 2 * TILE), F32)],
-    )(*in_hbm(weights), *in_hbm(tokens))
+    )(*in_hbm(weights), *tokens)
 
 
 def project_kernel(n_parts, core, kept, *refs):
@@ -547,7 +552,8 @@
         shifts, to_frame = [0, -1, 1], [later, [(j, i) for i, j in later]]
     edge_row = jnp.where(band_idx == 0, ROWS - 1, 0)
     second = position % 2
-    combo = jnp.append(2 * window_frame_reach + window_row_reach, second)
+    me = position * 2 + lax.axis_index("groups")
+    combo = jnp.append(2 * window_frame_reach + window_row_reach, jnp.stack([second, me]))
 
     edge_at = edge_row[None]
     leftmost, rightmost, edge = column_call(
@@ -561,7 +567,6 @@
     left = permute(rightmost, to_right)
     group = lax.axis_index("groups")
     turns = devices // 4
-    me = position * 2 + group
     share = output_matrix.shape[0] // 2
     own = lax.dynamic_slice_in_dim(output_matrix, group * share, share)
     top, low_rows = own[: share // 2], own[share // 2 :]
@@ -569,10 +574,10 @@
     down = adapter_down_weight.T
     grad_low = (ADAPTER * nt(adapter_up_weight, upstream)).astype(BF16)
     extra = tn(down, grad_low)
-    across = swap(after(upstream, edge), 1, 0)
+    across = swap(after(upstream, bias), 1, 0)
     start = [left, right, own, low_rows, bias, grad_low, extra, combo, across, core_slots]
     if turns == 4:
-        one, two = swap(after(own, edge), 0, 4), swap(after(top, edge), 0, 8)
+        one, two = swap(own, 0, 4), swap(top, 0, 8)
         start += [one, two]
     to_outer = column_call(outer_kernel, [edge_at], [after(left, start), right, edge], [40])
 
@@ -601,16 +606,16 @@
     slots = [(input_keys, input_values, rim)] + [
         (*core, permute(rim, route)) for core, route in zip(core_slots, to_frame)
     ]
-    att, log_total, grads, low = attend(
+    forward = attend(
         combo,
         after(input_queries, extra, across_other),
         slots,
-        bias, down, grad_low, upstream
-    )
-
-    att, log_total, grads, low = after((att, log_total, grads, low), fetched)
-
-    att_like, att_other = spread(att, me, turns)
+        bias, down, grad_low, upstream,
+        turns,
+    )
+    att, log_total, grads, low, *att_members = after(forward, fetched)
+
+    att_like, att_other = att_members or spread(att, me, turns)
     got = permute(grads[1], [(i, i ^ 1) for i in everyone])
     part = grads[0].astype(F32) + got.astype(F32)
 
@@ -624,8 +629,9 @@
         weights = [jnp.concatenate(weights)]
     att_packed = pack(att_like, swap(att_other, 0, 1))
     att_got = [swap(pair, x, 2 * y) for (x, y), pair in zip(PLACES[1:], att_packed[1:])]
+    upstream_here, across, across_other, beside = in_hbm([upstream, across, across_other, beside])
     tokens = [
-        [upstream, swap(after(upstream, att), 0, 1)],
+        [upstream_here, swap(after(upstream, att), 0, 1)],
         [across, across_other],
         [beside, swap(after(beside, att), 0, 1)],
         [upper, lower, swap(after(upper, att), 0, 1), swap(after(lower, att), 0, 1)],

time: 166 us -> 162 us (0.976)
  waiting for transfers between devices: 54.9 us -> 57.6 us
  starting transfers between devices: 43.1 us -> 40.8 us
  local copies, waits for them, and re-layouts: 11.2 us -> 9.53 us
    ppermute x28, starting transfers between devices: 29.1 us -> 26.9 us  [swap(): lax.ppermute(block, ('groups', 'tensor'), [(g * devices + i, (g ^ group_b...]
    ppermute x28, waiting for transfers between devices: 11.9 us -> 14 us  [swap(): lax.ppermute(block, ('groups', 'tensor'), [(g * devices + i, (g ^ group_b...]
    unnamed x70 -> x74, local copies, waits for them, and re-layouts: 7.44 us -> 5.42 us
  transfers between devices with their start and end apart: 44 -> 44, of which waited for: 14 -> 13; matrix products, arithmetic and copies ran while one was open for 9% -> 9% of each run, Pallas kernels for 24% -> 23%
where the time goes in v4:
time: 162 us; the launch traced here: 161 us
  waiting for transfers between devices  57.6 us (36%)
  starting transfers between devices  40.8 us (25%)
  Pallas kernels  38.8 us (24%)
  local copies, waits for them, and re-layouts  9.53 us (6%)
  other arithmetic  6.98 us (4%)
  matrix products  5.95 us (4%)
    ppermute x16, waiting for transfers between devices, permute(): return lax.ppermute(block, 'tensor', route)  43.5 us
    ppermute x28, starting transfers between devices, swap(): lax.ppermute(block, ('groups', 'tensor'), [(g * devices + i, (g ^ group_b...  26.9 us
    pallas_call x2, Pallas kernels, from_hbm(): return call(scalars, *in_hbm(arrays[:3]), *arrays[3:])  14.5 us
    ppermute x28, waiting for transfers between devices, swap(): lax.ppermute(block, ('groups', 'tensor'), [(g * devices + i, (g ^ group_b...  14 us
    ppermute x16, starting transfers between devices, permute(): return lax.ppermute(block, 'tensor', route)  13.9 us
    pallas_call x4, Pallas kernels, project(): plain_call(functools.partial(project_kernel, len(weights), core, kept), (...  13 us
    dot_general x4, matrix products, tn(): lax.dot_general(a, b, (((0,), (0,)), ((), ())), preferred_element_type=F32)  5.56 us
    unnamed x74, local copies, waits for them, and re-layouts  5.42 us
  transfers between devices with their start and end apart: 44, of which 13 were waited for; matrix products, arithmetic and copies ran while one was open for 9% of the time, Pallas kernels for 23%

profile of v4, /device:TPU:0, one launch (start us, length us, event | category | flops | bytes accessed | tf_op | source)
XLA Modules:
  0.0 161.0 jit_solution(18078080732965055922)
XLA Ops:
  1.4 3.0 %collective-permute-start.6 = (bf16[128,3072]{1,0:T(8,128)(2,1)}, bf16[128,3072]{1,0:T(8,128)(2,1)}, u32[]{:S(2)}, u32[]{:S(2)}) collective-permute-start(bf16[128,3072]{1,0:T(8,128)(2,1)} %refs_6_.1), channel_id=1, source_target_pairs={{0,16},{1,17},{2,18},{3,19},{4,20},{5,21},{6,22},{7,23},{8,24},{9,... | collective-permute-start | bytes 2359304 | tf_op jit(solution)/shard_map/ppermute | solution.py:510
  4.9 2.0 %constant_dynamic-slice_fusion.1 = (bf16[48,3072]{1,0:T(8,128)(2,1)}, bf16[48,3072]{1,0:T(8,128)(2,1)}) fusion(bf16[192,3072]{1,0:T(8,128)(2,1)} %param.12, s32[]{:T(128)S(6)} %select_n.54, s32[]{:T(128)S(6)} %add.131), kind=kLoop, calls=%fused_computation.58 | loop fusion | bytes 1179656 | tf_op jit(solution)/shard_map/slice | solution.py:572
  6.9 2.6 %collective-permute-start.1 = (bf16[48,3072]{1,0:T(8,128)(2,1)}, bf16[48,3072]{1,0:T(8,128)(2,1)}, u32[]{:S(2)}, u32[]{:S(2)}) collective-permute-start(bf16[48,3072]{1,0:T(8,128)(2,1)} %get-tuple-element.172), channel_id=1, source_target_pairs={{0,8},{1,9},{2,10},{3,11},{4,12},{5,13},{6,14},{7,15},{8,0},{9,1},... | collective-permute-start | bytes 884744 | tf_op jit(solution)/shard_map/ppermute | solution.py:510
  9.5 0.9 constant_dynamic-slice_fusion.2.refs_0_
  10.4 1.6 collective-permute-start
  11.9 3.7 %shard_map.136 = (bf16[16,3072]{1,0:T(8,128)(2,1)}, bf16[16,3072]{1,0:T(8,128)(2,1)}, bf16[32,3072]{1,0:T(8,128)(2,1)}) custom-call(s32[1]{0:T(128)} %bitcast.where, bf16[128,3072]{1,0:T(8,128)(2,1)} %refs_0_.3, bf16[128,3072]{1,0:T(8,128)(2,1)} %refs_1_.3), custom_call_target="tpu_custom_call" | custom-call | flops 1000 | bytes 1000 | tf_op jit(solution)/shard_map/pallas_call | solution.py:352
  16.2 1.5 convolution_bitcast_fusion.refs_9_
  17.8 1.3 collective-permute-start.5
  19.1 4.6 %collective-permute-start.4 = (bf16[16,3072]{1,0:T(8,128)(2,1)S(1)}, bf16[16,3072]{1,0:T(8,128)(2,1)S(1)}, u32[]{:S(2)}, u32[]{:S(2)}) collective-permute-start(bf16[16,3072]{1,0:T(8,128)(2,1)S(1)} %copy-done.33), channel_id=1, source_target_pairs={{0,2},{1,3},{2,4},{3,5},{4,6},{5,7},{8,10},{9,11},{10,12},{11,13},... | collective-permute-start | bytes 294920 | tf_op jit(solution)/shard_map/ppermute | solution.py:505
  23.7 8.2 %collective-permute-done.refs_1_ = bf16[96,3072]{1,0:T(8,128)(2,1)} collective-permute-done((bf16[96,3072]{1,0:T(8,128)(2,1)}, bf16[96,3072]{1,0:T(8,128)(2,1)}, u32[]{:S(2)}, u32[]{:S(2)}) %collective-permute-start) | collective-permute-done | bytes 589856 | tf_op jit(solution)/shard_map/ppermute | solution.py:510
  32.2 2.4 %collective-permute-start.10 = (bf16[128,3072]{1,0:T(8,128)(2,1)S(1)}, bf16[128,3072]{1,0:T(8,128)(2,1)S(1)}, u32[]{:S(2)}, u32[]{:S(2)}) collective-permute-start(bf16[128,3072]{1,0:T(8,128)(2,1)S(1)} %copy-done.17), channel_id=1, source_target_pairs={{0,2},{1,3},{2,0},{3,1},{4,6},{5,7},{6,4},{7,5},{8,10},{9,11},{10,... | collective-permute-start | bytes 2359304 | tf_op jit(solution)/shard_map/ppermute | solution.py:510
  34.6 1.0 slice.148
  35.7 2.1 %collective-permute-start.8 = (bf16[48,3072]{1,0:T(8,128)(2,1)}, bf16[48,3072]{1,0:T(8,128)(2,1)S(1)}, u32[]{:S(2)}, u32[]{:S(2)}) collective-permute-start(bf16[48,3072]{1,0:T(8,128)(2,1)} %collective-permute-done.1.refs_2_), channel_id=1, source_target_pairs={{0,4},{1,5},{2,6},{3,7},{4,0},{5,1},{6,2},{7,3},{8,12},{9,13},{10,... | collective-permute-start | bytes 884744 | tf_op jit(solution)/shard_map/ppermute | solution.py:510
  37.8 2.5 %collective-permute-start.7 = (bf16[48,3072]{1,0:T(8,128)(2,1)S(1)}, bf16[48,3072]{1,0:T(8,128)(2,1)S(1)}, u32[]{:S(2)}, u32[]{:S(2)}) collective-permute-start(bf16[48,3072]{1,0:T(8,128)(2,1)S(1)} %copy-done.27), channel_id=1, source_target_pairs={{0,8},{1,9},{2,10},{3,11},{4,12},{5,13},{6,14},{7,15},{8,0},{9,1},... | collective-permute-start | bytes 884744 | tf_op jit(solution)/shard_map/ppermute | solution.py:510
  40.7 22.1 %collective-permute-done.9.outer = bf16[40,3072]{1,0:T(8,128)(2,1)S(1)} collective-permute-done((bf16[40,3072]{1,0:T(8,128)(2,1)S(1)}, bf16[40,3072]{1,0:T(8,128)(2,1)S(1)}, u32[]{:S(2)}, u32[]{:S(2)}) %collective-permute-start.9) | collective-permute-done | bytes 245792 | tf_op jit(solution)/shard_map/ppermute | solution.py:505
  64.4 1.1 collective-permute-done.13.refs_9_
  66.1 6.8 %shard_map.140 = (bf16[3072,128]{1,0:T(8,128)(2,1)}, f32[3,8,128]{2,1,0:T(8,128)S(1)}, bf16[2,64,3072]{2,1,0:T(8,128)(2,1)S(1)}, bf16[64,128]{1,0:T(8,128)(2,1)S...) custom-call(s32[26]{0:T(128)S(1)} %pad_add_fusion.1.combo, bf16[128,3072]{1,0:T(8,128)(2,1)} %query.1, ...), custom_call_target="tpu_custom_call" | custom-call | flops 1000 | bytes 1000 | tf_op jit(solution)/shard_map/pallas_call | solution.py:154
  73.1 1.8 %collective-permute-done.15.refs_13_ = bf16[64,3072]{1,0:T(8,128)(2,1)S(1)} collective-permute-done((bf16[64,3072]{1,0:T(8,128)(2,1)S(1)}, bf16[64,3072]{1,0:T(8,128)(2,1)S(1)}, u32[]{:S(2)}, u32[]{:S(2)}) %collective-permute-start.15) | collective-permute-done | bytes 393248 | tf_op jit(solution)/shard_map/ppermute | solution.py:510
  78.4 2.6 %collective-permute-start.19 = (bf16[2,384,128]{2,1,0:T(8,128)(2,1)S(1)}, bf16[2,384,128]{2,1,0:T(8,128)(2,1)S(1)}, u32[]{:S(2)}, u32[]{:S(2)}) collective-permute-start(bf16[2,384,128]{2,1,0:T(8,128)(2,1)S(1)} %get-tuple-element.113), channel_id=1, source_target_pairs={{0,18},{1,19},{2,16},{3,17},{4,22},{5,23},{6,20},{7,21},{8,26},{9,... | collective-permute-start | bytes 589832 | tf_op jit(solution)/shard_map/ppermute | solution.py:510
  81.3 0.8 copy-done.25
  82.0 5.0 %shard_map.142 = (bf16[4,384,128]{2,1,0:T(8,128)(2,1)S(1)}, bf16[4,384,128]{2,1,0:T(8,128)(2,1)S(1)}) custom-call(bf16[96,3072]{1,0:T(8,128)(2,1)} %constant_dynamic-slice_fusion.2.refs_0_, bf16[96,3072]{1,0:T(8,128)(2,1)} %collective-permute-done.refs_1_, bf16[48,3072]{1,0:T(8,128)(2,1)} %collective-permute-done.1.refs_2_, bf16[48,3072]{1,0:T(8,128)(2,1)} %copy-done.14, ...), custom_call_target="tpu_custom_call" | custom-call | flops 1000 | bytes 1000 | tf_op jit(solution)/shard_map/pallas_call | solution.py:414
  87.0 2.2 %collective-permute-done.18.refs_8_ = bf16[2,384,128]{2,1,0:T(8,128)(2,1)S(1)} collective-permute-done((bf16[2,384,128]{2,1,0:T(8,128)(2,1)S(1)}, bf16[2,384,128]{2,1,0:T(8,128)(2,1)S(1)}, u32[]{:S(2)}, u32[]{:S(2)}) %collective-permute-start.18) | collective-permute-done | bytes 196640 | tf_op jit(solution)/shard_map/ppermute | solution.py:510
  89.9 2.9 %shard_map.146 = bf16[4,128,1536]{2,1,0:T(8,128)(2,1)S(1)} custom-call(bf16[96,3072]{1,0:T(8,128)(2,1)} %constant_dynamic-slice_fusion.2.refs_0_, bf16[96,3072]{1,0:T(8,128)(2,1)} %collective-permute-done.refs_1_, bf16[48,3072]{1,0:T(8,128)(2,1)} %collective-permute-done.1.refs_2_, bf16[48,3072]{1,0:T(8,128)(2,1)} %copy-done.14, ...), custom_call_target="tpu_custom_call" | custom-call | flops 1000 | bytes 1000 | tf_op jit(solution)/shard_map/pallas_call | solution.py:454
  92.9 2.9 %shard_map.143 = bf16[4,128,1536]{2,1,0:T(8,128)(2,1)S(1)} custom-call(bf16[96,3072]{1,0:T(8,128)(2,1)} %constant_dynamic-slice_fusion.2.refs_0_, bf16[96,3072]{1,0:T(8,128)(2,1)} %collective-permute-done.refs_1_, bf16[48,3072]{1,0:T(8,128)(2,1)} %collective-permute-done.1.refs_2_, bf16[48,3072]{1,0:T(8,128)(2,1)} %copy-done.14, ...), custom_call_target="tpu_custom_call" | custom-call | flops 1000 | bytes 1000 | tf_op jit(solution)/shard_map/pallas_call | solution.py:454
  97.1 1.5 collective-permute-start.31
  98.9 1.6 %collective-permute-start.33 = (bf16[2,384,128]{2,1,0:T(8,128)(2,1)S(1)}, bf16[2,384,128]{2,1,0:T(8,128)(2,1)S(1)}, u32[]{:S(2)}, u32[]{:S(2)}) collective-permute-start(bf16[2,384,128]{2,1,0:T(8,128)(2,1)S(1)} %get-tuple-element.129), channel_id=1, source_target_pairs={{0,18},{1,19},{2,16},{3,17},{4,22},{5,23},{6,20},{7,21},{8,26},{9,... | collective-permute-start | bytes 589832 | tf_op jit(solution)/shard_map/ppermute | solution.py:510
  100.6 3.6 %shard_map.147 = (bf16[2,128,1536]{2,1,0:T(8,128)(2,1)S(1)}, bf16[2,128,1536]{2,1,0:T(8,128)(2,1)}) custom-call(bf16[96,3072]{1,0:T(8,128)(2,1)} %constant_dynamic-slice_fusion.2.refs_0_, bf16[96,3072]{1,0:T(8,128)(2,1)} %collective-permute-done.refs_1_, bf16[48,3072]{1,0:T(8,128)(2,1)} %collective-permute-done.1.refs_2_, bf16[48,3072]{1,0:T(8,128)(2,1)} %copy-done.14, ...), custom_call_target="tpu_custom_call" | custom-call | flops 1000 | bytes 1000 | tf_op jit(solution)/shard_map/pallas_call | solution.py:454
  104.2 1.6 collective-permute-start.30
  105.7 3.6 %shard_map.145 = (bf16[2,128,1536]{2,1,0:T(8,128)(2,1)S(1)}, bf16[2,128,1536]{2,1,0:T(8,128)(2,1)}) custom-call(bf16[96,3072]{1,0:T(8,128)(2,1)} %constant_dynamic-slice_fusion.2.refs_0_, bf16[96,3072]{1,0:T(8,128)(2,1)} %collective-permute-done.refs_1_, bf16[48,3072]{1,0:T(8,128)(2,1)} %collective-permute-done.1.refs_2_, bf16[48,3072]{1,0:T(8,128)(2,1)} %copy-done.14, ...), custom_call_target="tpu_custom_call" | custom-call | flops 1000 | bytes 1000 | tf_op jit(solution)/shard_map/pallas_call | solution.py:454
  109.3 0.9 copy-done.9
  110.5 0.9 convert_add_fusion.4
  112.9 1.4 shard_map.148.refs_8_
  114.5 7.7 %shard_map.149 = (bf16[128,3072]{1,0:T(8,128)(2,1)}, bf16[256,3072]{1,0:T(8,128)(2,1)}, bf16[96,3072]{1,0:T(8,128)(2,1)}, bf16[256,3072]{1,0:T(8,128)(2,1)}, bf16[96,3072]{1,0:T(8,128)(2,1)}) custom-call(s32[26]{0:T(128)S(1)} %pad_add_fusion.1.combo, bf16[128,3072]{1,0:T(8,128)(2,1)} %query.1, bf16[128,3072]{1,0:T(8,128)(2,1)} %refs_0_.3, ...), custom_call_target="tpu_custom_call" | custom-call | flops 1000 | bytes 1000 | tf_op jit(solution)/shard_map/pallas_call | solution.py:154
  122.2 9.3 %collective-permute-done.34 = bf16[64,3072]{1,0:T(8,128)(2,1)} collective-permute-done((bf16[64,3072]{1,0:T(8,128)(2,1)}, bf16[64,3072]{1,0:T(8,128)(2,1)}, u32[]{:S(2)}, u32[]{:S(2)}) %collective-permute-start.34) | collective-permute-done | bytes 393248 | tf_op jit(solution)/shard_map/ppermute | solution.py:505
  131.6 1.2 add_convert_fusion.3
  132.8 1.7 %collective-permute-start.42 = (bf16[64,3072]{1,0:T(8,128)(2,1)S(1)}, bf16[64,3072]{1,0:T(8,128)(2,1)S(1)}, u32[]{:S(2)}, u32[]{:S(2)}) collective-permute-start(bf16[64,3072]{1,0:T(8,128)(2,1)S(1)} %add_convert_fusion.3), channel_id=1, source_target_pairs={{0,2},{1,3},{2,0},{3,1},{4,6},{5,7},{6,4},{7,5},{8,10},{9,11},{10,... | collective-permute-start | bytes 1179656 | tf_op jit(solution)/shard_map/ppermute | solution.py:505
  134.8 1.4 convert_add_fusion.1
  136.9 1.3 convert_add_fusion
  138.3 1.2 collective-permute-start.37
  139.5 5.3 %collective-permute-done.42 = bf16[64,3072]{1,0:T(8,128)(2,1)S(1)} collective-permute-done((bf16[64,3072]{1,0:T(8,128)(2,1)S(1)}, bf16[64,3072]{1,0:T(8,128)(2,1)S(1)}, u32[]{:S(2)}, u32[]{:S(2)}) %collective-permute-start.42) | collective-permute-done | bytes 393248 | tf_op jit(solution)/shard_map/ppermute | solution.py:505
  144.8 3.8 %collective-permute-done.38 = bf16[36,3072]{1,0:T(8,128)(2,1)S(1)} collective-permute-done((bf16[36,3072]{1,0:T(8,128)(2,1)S(1)}, bf16[36,3072]{1,0:T(8,128)(2,1)S(1)}, u32[]{:S(2)}, u32[]{:S(2)}) %collective-permute-start.38) | collective-permute-done | bytes 221216 | tf_op jit(solution)/shard_map/ppermute | solution.py:505
  148.9 2.7 %collective-permute-start.40 = (bf16[16,3072]{1,0:T(8,128)(2,1)S(1)}, bf16[16,3072]{1,0:T(8,128)(2,1)S(1)}, u32[]{:S(2)}, u32[]{:S(2)}) collective-permute-start(bf16[16,3072]{1,0:T(8,128)(2,1)S(1)} %pad_maximum_fusion.2), channel_id=1, source_target_pairs={{0,2},{1,3},{2,4},{3,5},{4,6},{5,7},{8,10},{9,11},{10,12},{11,13},... | collective-permute-start | bytes 294920 | tf_op jit(solution)/shard_map/ppermute | solution.py:505
  151.6 1.3 collective-permute-start.41
  153.3 1.3 fusion.1
  154.8 1.2 select_convert_fusion
  156.0 2.1 %collective-permute-done.41 = bf16[16,3072]{1,0:T(8,128)(2,1)S(1)} collective-permute-done((bf16[16,3072]{1,0:T(8,128)(2,1)S(1)}, bf16[16,3072]{1,0:T(8,128)(2,1)S(1)}, u32[]{:S(2)}, u32[]{:S(2)}) %collective-permute-start.41) | collective-permute-done | bytes 98336 | tf_op jit(solution)/shard_map/ppermute | solution.py:505
  158.2 1.4 add_convert_fusion
  159.6 1.4 add_convert_fusion.1
  (165 shorter events, 14.8 us)
Async XLA Ops:
  1.4 30.5 %collective-permute-start.6 = (bf16[128,3072]{1,0:T(8,128)(2,1)}, bf16[128,3072]{1,0:T(8,128)(2,1)}, u32[]{:S(2)}, u32[]{:S(2)}) collective-permute-start(bf16[128,3072]{1,0:T(8,128)(2,1)} %refs_6_.1), channel_id=1, source_target_pairs={{0,16},{1,17},{2,18},{3,19},{4,20},{5,21},{6,22},{7,23},{8,24},{9,... | collective-permute-start | bytes 2359304 | tf_op jit(solution)/shard_map/ppermute | solution.py:510
  4.4 13.3 %collective-permute-start.2 = (bf16[128,3072]{1,0:T(8,128)(2,1)}, bf16[128,3072]{1,0:T(8,128)(2,1)S(1)}, u32[]{:S(2)}, u32[]{:S(2)}) collective-permute-start(bf16[128,3072]{1,0:T(8,128)(2,1)} %refs_0_.3), channel_id=1, source_target_pairs={{0,1},{1,0},{2,3},{3,2},{4,5},{5,4},{6,7},{7,6},{8,9},{9,8},{10,11... | collective-permute-start | bytes 2359304 | tf_op jit(solution)/shard_map/ppermute | solution.py:505
  4.4 13.3 %collective-permute-start.3 = (bf16[128,3072]{1,0:T(8,128)(2,1)}, bf16[128,3072]{1,0:T(8,128)(2,1)}, u32[]{:S(2)}, u32[]{:S(2)}) collective-permute-start(bf16[128,3072]{1,0:T(8,128)(2,1)} %refs_1_.3), channel_id=1, source_target_pairs={{0,1},{1,0},{2,3},{3,2},{4,5},{5,4},{6,7},{7,6},{8,9},{9,8},{10,11... | collective-permute-start | bytes 2359304 | tf_op jit(solution)/shard_map/ppermute | solution.py:505
  6.9 16.8 %collective-permute-start.1 = (bf16[48,3072]{1,0:T(8,128)(2,1)}, bf16[48,3072]{1,0:T(8,128)(2,1)}, u32[]{:S(2)}, u32[]{:S(2)}) collective-permute-start(bf16[48,3072]{1,0:T(8,128)(2,1)} %get-tuple-element.172), channel_id=1, source_target_pairs={{0,8},{1,9},{2,10},{3,11},{4,12},{5,13},{6,14},{7,15},{8,0},{9,1},... | collective-permute-start | bytes 884744 | tf_op jit(solution)/shard_map/ppermute | solution.py:510
  10.4 21.5 %collective-permute-start = (bf16[96,3072]{1,0:T(8,128)(2,1)}, bf16[96,3072]{1,0:T(8,128)(2,1)}, u32[]{:S(2)}, u32[]{:S(2)}) collective-permute-start(bf16[96,3072]{1,0:T(8,128)(2,1)} %constant_dynamic-slice_fusion.2.refs_0_), channel_id=1, source_target_pairs={{0,4},{1,5},{2,6},{3,7},{4,0},{5,1},{6,2},{7,3},{8,12},{9,13},{10,... | collective-permute-start | bytes 1769480 | tf_op jit(solution)/shard_map/ppermute | solution.py:510
  15.7 16.2 %copy-start.11 = (bf16[32,3072]{1,0:T(8,128)(2,1)S(1)}, bf16[32,3072]{1,0:T(8,128)(2,1)}, u32[]{:S(2)}) copy-start(bf16[32,3072]{1,0:T(8,128)(2,1)} %get-tuple-element.92.edge) | copy-start | bytes 589828
  16.1 16.1 %copy-start.17 = (bf16[128,3072]{1,0:T(8,128)(2,1)S(1)}, bf16[128,3072]{1,0:T(8,128)(2,1)}, u32[]{:S(2)}) copy-start(bf16[128,3072]{1,0:T(8,128)(2,1)} %refs_6_.1) | copy-start | bytes 2359300
  16.1 21.7 %copy-start.27 = (bf16[48,3072]{1,0:T(8,128)(2,1)S(1)}, bf16[48,3072]{1,0:T(8,128)(2,1)}, u32[]{:S(2)}) copy-start(bf16[48,3072]{1,0:T(8,128)(2,1)} %get-tuple-element.93) | copy-start | bytes 884740
  17.7 45.2 %copy-start.2 = (bf16[128,3072]{1,0:T(8,128)(2,1)}, bf16[128,3072]{1,0:T(8,128)(2,1)S(1)}, u32[]{:S(2)}) copy-start(bf16[128,3072]{1,0:T(8,128)(2,1)S(1)} %collective-permute-done.2.refs_3_) | copy-start | bytes 2359300
  17.8 14.1 %collective-permute-start.5 = (bf16[16,3072]{1,0:T(8,128)(2,1)S(1)}, bf16[16,3072]{1,0:T(8,128)(2,1)S(1)}, u32[]{:S(2)}, u32[]{:S(2)}) collective-permute-start(bf16[16,3072]{1,0:T(8,128)(2,1)S(1)} %copy-done.34), channel_id=1, source_target_pairs={{2,0},{3,1},{4,2},{5,3},{6,4},{7,5},{10,8},{11,9},{12,10},{13,11},... | collective-permute-start | bytes 294920 | tf_op jit(solution)/shard_map/ppermute | solution.py:505
  19.1 12.8 %collective-permute-start.4 = (bf16[16,3072]{1,0:T(8,128)(2,1)S(1)}, bf16[16,3072]{1,0:T(8,128)(2,1)S(1)}, u32[]{:S(2)}, u32[]{:S(2)}) collective-permute-start(bf16[16,3072]{1,0:T(8,128)(2,1)S(1)} %copy-done.33), channel_id=1, source_target_pairs={{0,2},{1,3},{2,4},{3,5},{4,6},{5,7},{8,10},{9,11},{10,12},{11,13},... | collective-permute-start | bytes 294920 | tf_op jit(solution)/shard_map/ppermute | solution.py:505
  32.2 30.7 %collective-permute-start.10 = (bf16[128,3072]{1,0:T(8,128)(2,1)S(1)}, bf16[128,3072]{1,0:T(8,128)(2,1)S(1)}, u32[]{:S(2)}, u32[]{:S(2)}) collective-permute-start(bf16[128,3072]{1,0:T(8,128)(2,1)S(1)} %copy-done.17), channel_id=1, source_target_pairs={{0,2},{1,3},{2,0},{3,1},{4,6},{5,7},{6,4},{7,5},{8,10},{9,11},{10,... | collective-permute-start | bytes 2359304 | tf_op jit(solution)/shard_map/ppermute | solution.py:510
  35.7 27.2 %collective-permute-start.11 = (bf16[64,3072]{1,0:T(8,128)(2,1)S(1)}, bf16[64,3072]{1,0:T(8,128)(2,1)S(1)}, u32[]{:S(2)}, u32[]{:S(2)}) collective-permute-start(bf16[64,3072]{1,0:T(8,128)(2,1)S(1)} %slice.148), channel_id=1, source_target_pairs={{0,2},{1,3},{2,0},{3,1},{4,6},{5,7},{6,4},{7,5},{8,10},{9,11},{10,... | collective-permute-start | bytes 1179656 | tf_op jit(solution)/shard_map/ppermute | solution.py:510
  35.7 27.1 %collective-permute-start.8 = (bf16[48,3072]{1,0:T(8,128)(2,1)}, bf16[48,3072]{1,0:T(8,128)(2,1)S(1)}, u32[]{:S(2)}, u32[]{:S(2)}) collective-permute-start(bf16[48,3072]{1,0:T(8,128)(2,1)} %collective-permute-done.1.refs_2_), channel_id=1, source_target_pairs={{0,4},{1,5},{2,6},{3,7},{4,0},{5,1},{6,2},{7,3},{8,12},{9,13},{10,... | collective-permute-start | bytes 884744 | tf_op jit(solution)/shard_map/ppermute | solution.py:510
  37.8 25.0 %collective-permute-start.7 = (bf16[48,3072]{1,0:T(8,128)(2,1)S(1)}, bf16[48,3072]{1,0:T(8,128)(2,1)S(1)}, u32[]{:S(2)}, u32[]{:S(2)}) collective-permute-start(bf16[48,3072]{1,0:T(8,128)(2,1)S(1)} %copy-done.27), channel_id=1, source_target_pairs={{0,8},{1,9},{2,10},{3,11},{4,12},{5,13},{6,14},{7,15},{8,0},{9,1},... | collective-permute-start | bytes 884744 | tf_op jit(solution)/shard_map/ppermute | solution.py:510
  40.3 22.6 %collective-permute-start.9 = (bf16[40,3072]{1,0:T(8,128)(2,1)S(1)}, bf16[40,3072]{1,0:T(8,128)(2,1)S(1)}, u32[]{:S(2)}, u32[]{:S(2)}) collective-permute-start(bf16[40,3072]{1,0:T(8,128)(2,1)S(1)} %shard_map.138), channel_id=1, source_target_pairs={{0,8},{1,9},{2,10},{3,11},{4,12},{5,13},{6,14},{7,15},{8,0},{9,1},... | collective-permute-start | bytes 737288 | tf_op jit(solution)/shard_map/ppermute | solution.py:505
  62.9 2.6 %collective-permute-start.13 = (bf16[128,3072]{1,0:T(8,128)(2,1)}, bf16[128,3072]{1,0:T(8,128)(2,1)S(1)}, u32[]{:S(2)}, u32[]{:S(2)}) collective-permute-start(bf16[128,3072]{1,0:T(8,128)(2,1)} %collective-permute-done.6.refs_8_), channel_id=1, source_target_pairs={{0,1},{1,0},{2,3},{3,2},{4,5},{5,4},{6,7},{7,6},{8,9},{9,8},{10,11... | collective-permute-start | bytes 2359304 | tf_op jit(solution)/shard_map/ppermute | solution.py:510
  63.2 2.9 %collective-permute-start.14 = (bf16[96,3072]{1,0:T(8,128)(2,1)S(1)}, bf16[96,3072]{1,0:T(8,128)(2,1)S(1)}, u32[]{:S(2)}, u32[]{:S(2)}) collective-permute-start(bf16[96,3072]{1,0:T(8,128)(2,1)S(1)} %shard_map.139.refs_2_), channel_id=1, source_target_pairs={{0,1},{1,0},{2,3},{3,2},{4,5},{5,4},{6,7},{7,6},{8,9},{9,8},{10,11... | collective-permute-start | bytes 1769480 | tf_op jit(solution)/shard_map/ppermute | solution.py:505
  63.8 11.1 %collective-permute-start.15 = (bf16[64,3072]{1,0:T(8,128)(2,1)S(1)}, bf16[64,3072]{1,0:T(8,128)(2,1)S(1)}, u32[]{:S(2)}, u32[]{:S(2)}) collective-permute-start(bf16[64,3072]{1,0:T(8,128)(2,1)S(1)} %slice.149), channel_id=1, source_target_pairs={{0,16},{1,17},{2,18},{3,19},{4,20},{5,21},{6,22},{7,23},{8,24},{9,... | collective-permute-start | bytes 1179656 | tf_op jit(solution)/shard_map/ppermute | solution.py:510
  64.4 8.7 %collective-permute-start.12 = (bf16[48,3072]{1,0:T(8,128)(2,1)S(1)}, bf16[48,3072]{1,0:T(8,128)(2,1)S(1)}, u32[]{:S(2)}, u32[]{:S(2)}) collective-permute-start(bf16[48,3072]{1,0:T(8,128)(2,1)S(1)} %collective-permute-done.7.refs_3_), channel_id=1, source_target_pairs={{0,4},{1,5},{2,6},{3,7},{4,0},{5,1},{6,2},{7,3},{8,12},{9,13},{10,... | collective-permute-start | bytes 884744 | tf_op jit(solution)/shard_map/ppermute | solution.py:510
  74.9 1.7 %collective-permute-start.16 = (bf16[4,384,128]{2,1,0:T(8,128)(2,1)S(1)}, bf16[4,384,128]{2,1,0:T(8,128)(2,1)S(1)}, u32[]{:S(2)}, u32[]{:S(2)}) collective-permute-start(bf16[4,384,128]{2,1,0:T(8,128)(2,1)S(1)} %get-tuple-element.109), channel_id=1, source_target_pairs={{0,1},{1,0},{2,3},{3,2},{4,5},{5,4},{6,7},{7,6},{8,9},{9,8},{10,11... | collective-permute-start | bytes 1179656 | tf_op jit(solution)/shard_map/ppermute | solution.py:510
  75.0 2.6 %collective-permute-start.25 = (bf16[64,3072]{1,0:T(8,128)(2,1)S(1)}, bf16[64,3072]{1,0:T(8,128)(2,1)S(1)}, u32[]{:S(2)}, u32[]{:S(2)}) collective-permute-start(bf16[64,3072]{1,0:T(8,128)(2,1)S(1)} %slice_bitcast_fusion.2), channel_id=1, source_target_pairs={{0,1},{1,0},{2,3},{3,2},{4,5},{5,4},{6,7},{7,6},{8,9},{9,8},{10,11... | collective-permute-start | bytes 1179656 | tf_op jit(solution)/shard_map/ppermute | solution.py:505
  75.5 2.5 %collective-permute-start.23 = (bf16[64,3072]{1,0:T(8,128)(2,1)S(1)}, bf16[64,3072]{1,0:T(8,128)(2,1)S(1)}, u32[]{:S(2)}, u32[]{:S(2)}) collective-permute-start(bf16[64,3072]{1,0:T(8,128)(2,1)S(1)} %collective-permute-done.15.refs_13_), channel_id=1, source_target_pairs={{0,1},{1,0},{2,3},{3,2},{4,5},{5,4},{6,7},{7,6},{8,9},{9,8},{10,11... | collective-permute-start | bytes 1179656 | tf_op jit(solution)/shard_map/ppermute | solution.py:510
  75.6 2.8 %collective-permute-start.22 = (bf16[64,3072]{1,0:T(8,128)(2,1)S(1)}, bf16[64,3072]{1,0:T(8,128)(2,1)S(1)}, u32[]{:S(2)}, u32[]{:S(2)}) collective-permute-start(bf16[64,3072]{1,0:T(8,128)(2,1)S(1)} %collective-permute-done.11.refs_12_), channel_id=1, source_target_pairs={{0,1},{1,0},{2,3},{3,2},{4,5},{5,4},{6,7},{7,6},{8,9},{9,8},{10,11... | collective-permute-start | bytes 1179656 | tf_op jit(solution)/shard_map/ppermute | solution.py:510
  76.0 5.1 %collective-permute-start.21 = (bf16[128,3072]{1,0:T(8,128)(2,1)S(1)}, bf16[128,3072]{1,0:T(8,128)(2,1)S(1)}, u32[]{:S(2)}, u32[]{:S(2)}) collective-permute-start(bf16[128,3072]{1,0:T(8,128)(2,1)S(1)} %collective-permute-done.10.refs_10_), channel_id=1, source_target_pairs={{0,1},{1,0},{2,3},{3,2},{4,5},{5,4},{6,7},{7,6},{8,9},{9,8},{10,11... | collective-permute-start | bytes 2359304 | tf_op jit(solution)/shard_map/ppermute | solution.py:510
  76.7 4.6 %collective-permute-start.20 = (bf16[128,3072]{1,0:T(8,128)(2,1)S(1)}, bf16[128,3072]{1,0:T(8,128)(2,1)S(1)}, u32[]{:S(2)}, u32[]{:S(2)}) collective-permute-start(bf16[128,3072]{1,0:T(8,128)(2,1)S(1)} %copy-done.18), channel_id=1, source_target_pairs={{0,1},{1,0},{2,3},{3,2},{4,5},{5,4},{6,7},{7,6},{8,9},{9,8},{10,11... | collective-permute-start | bytes 2359304 | tf_op jit(solution)/shard_map/ppermute | solution.py:510
  77.5 9.5 %collective-permute-start.17 = (bf16[2,384,128]{2,1,0:T(8,128)(2,1)S(1)}, bf16[2,384,128]{2,1,0:T(8,128)(2,1)S(1)}, u32[]{:S(2)}, u32[]{:S(2)}) collective-permute-start(bf16[2,384,128]{2,1,0:T(8,128)(2,1)S(1)} %get-tuple-element.111), channel_id=1, source_target_pairs={{0,16},{1,17},{2,18},{3,19},{4,20},{5,21},{6,22},{7,23},{8,24},{9,... | collective-permute-start | bytes 589832 | tf_op jit(solution)/shard_map/ppermute | solution.py:510
  78.1 11.1 %collective-permute-start.18 = (bf16[2,384,128]{2,1,0:T(8,128)(2,1)S(1)}, bf16[2,384,128]{2,1,0:T(8,128)(2,1)S(1)}, u32[]{:S(2)}, u32[]{:S(2)}) collective-permute-start(bf16[2,384,128]{2,1,0:T(8,128)(2,1)S(1)} %get-tuple-element.112), channel_id=1, source_target_pairs={{0,2},{1,3},{2,0},{3,1},{4,6},{5,7},{6,4},{7,5},{8,10},{9,11},{10,... | collective-permute-start | bytes 589832 | tf_op jit(solution)/shard_map/ppermute | solution.py:510
  78.4 10.7 %collective-permute-start.19 = (bf16[2,384,128]{2,1,0:T(8,128)(2,1)S(1)}, bf16[2,384,128]{2,1,0:T(8,128)(2,1)S(1)}, u32[]{:S(2)}, u32[]{:S(2)}) collective-permute-start(bf16[2,384,128]{2,1,0:T(8,128)(2,1)S(1)} %get-tuple-element.113), channel_id=1, source_target_pairs={{0,18},{1,19},{2,16},{3,17},{4,22},{5,23},{6,20},{7,21},{8,26},{9,... | collective-permute-start | bytes 589832 | tf_op jit(solution)/shard_map/ppermute | solution.py:510
  81.2 14.7 %collective-permute-start.26 = (bf16[64,3072]{1,0:T(8,128)(2,1)S(1)}, bf16[64,3072]{1,0:T(8,128)(2,1)S(1)}, u32[]{:S(2)}, u32[]{:S(2)}) collective-permute-start(bf16[64,3072]{1,0:T(8,128)(2,1)S(1)} %fusion.5), channel_id=1, source_target_pairs={{0,4},{1,5},{2,6},{3,7},{4,0},{5,1},{6,2},{7,3},{8,12},{9,13},{10,... | collective-permute-start | bytes 1179656 | tf_op jit(solution)/shard_map/ppermute | solution.py:505
  89.2 6.6 %collective-permute-start.24 = (bf16[4,384,128]{2,1,0:T(8,128)(2,1)S(1)}, bf16[4,384,128]{2,1,0:T(8,128)(2,1)S(1)}, u32[]{:S(2)}, u32[]{:S(2)}) collective-permute-start(bf16[4,384,128]{2,1,0:T(8,128)(2,1)S(1)} %get-tuple-element.125), channel_id=1, source_target_pairs={{0,1},{1,0},{2,3},{3,2},{4,5},{5,4},{6,7},{7,6},{8,9},{9,8},{10,11... | collective-permute-start | bytes 1179656 | tf_op jit(solution)/shard_map/ppermute | solution.py:510
  96.6 4.0 %collective-permute-start.29 = (bf16[4,128,1536]{2,1,0:T(8,128)(2,1)S(1)}, bf16[4,128,1536]{2,1,0:T(8,128)(2,1)S(1)}, u32[]{:S(2)}, u32[]{:S(2)}) collective-permute-start(bf16[4,128,1536]{2,1,0:T(8,128)(2,1)S(1)} %shard_map.146), channel_id=1, source_target_pairs={{0,1},{1,0},{2,3},{3,2},{4,5},{5,4},{6,7},{7,6},{8,9},{9,8},{10,11... | collective-permute-start | bytes 4718600 | tf_op jit(solution)/shard_map/ppermute | solution.py:510
  96.6 9.1 %collective-permute-start.27 = (bf16[4,128,1536]{2,1,0:T(8,128)(2,1)S(1)}, bf16[4,128,1536]{2,1,0:T(8,128)(2,1)S(1)}, u32[]{:S(2)}, u32[]{:S(2)}) collective-permute-start(bf16[4,128,1536]{2,1,0:T(8,128)(2,1)S(1)} %shard_map.143), channel_id=1, source_target_pairs={{0,1},{1,0},{2,3},{3,2},{4,5},{5,4},{6,7},{7,6},{8,9},{9,8},{10,11... | collective-permute-start | bytes 4718600 | tf_op jit(solution)/shard_map/ppermute | solution.py:510
  97.1 14.3 %collective-permute-start.31 = (bf16[2,384,128]{2,1,0:T(8,128)(2,1)S(1)}, bf16[2,384,128]{2,1,0:T(8,128)(2,1)S(1)}, u32[]{:S(2)}, u32[]{:S(2)}) collective-permute-start(bf16[2,384,128]{2,1,0:T(8,128)(2,1)S(1)} %get-tuple-element.127), channel_id=1, source_target_pairs={{0,16},{1,17},{2,18},{3,19},{4,20},{5,21},{6,22},{7,23},{8,24},{9,... | collective-permute-start | bytes 589832 | tf_op jit(solution)/shard_map/ppermute | solution.py:510
  98.6 12.8 %collective-permute-start.32 = (bf16[2,384,128]{2,1,0:T(8,128)(2,1)S(1)}, bf16[2,384,128]{2,1,0:T(8,128)(2,1)S(1)}, u32[]{:S(2)}, u32[]{:S(2)}) collective-permute-start(bf16[2,384,128]{2,1,0:T(8,128)(2,1)S(1)} %get-tuple-element.128), channel_id=1, source_target_pairs={{0,2},{1,3},{2,0},{3,1},{4,6},{5,7},{6,4},{7,5},{8,10},{9,11},{10,... | collective-permute-start | bytes 589832 | tf_op jit(solution)/shard_map/ppermute | solution.py:510
  98.9 12.5 %collective-permute-start.33 = (bf16[2,384,128]{2,1,0:T(8,128)(2,1)S(1)}, bf16[2,384,128]{2,1,0:T(8,128)(2,1)S(1)}, u32[]{:S(2)}, u32[]{:S(2)}) collective-permute-start(bf16[2,384,128]{2,1,0:T(8,128)(2,1)S(1)} %get-tuple-element.129), channel_id=1, source_target_pairs={{0,18},{1,19},{2,16},{3,17},{4,22},{5,23},{6,20},{7,21},{8,26},{9,... | collective-permute-start | bytes 589832 | tf_op jit(solution)/shard_map/ppermute | solution.py:510
  104.2 27.4 %collective-permute-start.30 = (bf16[2,128,1536]{2,1,0:T(8,128)(2,1)}, bf16[2,128,1536]{2,1,0:T(8,128)(2,1)}, u32[]{:S(2)}, u32[]{:S(2)}) collective-permute-start(bf16[2,128,1536]{2,1,0:T(8,128)(2,1)} %get-tuple-element.136), channel_id=1, source_target_pairs={{0,16},{1,17},{2,18},{3,19},{4,20},{5,21},{6,22},{7,23},{8,24},{9,... | collective-permute-start | bytes 2359304 | tf_op jit(solution)/shard_map/ppermute | solution.py:510
  110.2 21.4 %collective-permute-start.28 = (bf16[2,128,1536]{2,1,0:T(8,128)(2,1)}, bf16[2,128,1536]{2,1,0:T(8,128)(2,1)}, u32[]{:S(2)}, u32[]{:S(2)}) collective-permute-start(bf16[2,128,1536]{2,1,0:T(8,128)(2,1)} %get-tuple-element.134), channel_id=1, source_target_pairs={{0,2},{1,3},{2,0},{3,1},{4,6},{5,7},{6,4},{7,5},{8,10},{9,11},{10,... | collective-permute-start | bytes 2359304 | tf_op jit(solution)/shard_map/ppermute | solution.py:510
  112.8 18.7 %collective-permute-start.34 = (bf16[64,3072]{1,0:T(8,128)(2,1)}, bf16[64,3072]{1,0:T(8,128)(2,1)}, u32[]{:S(2)}, u32[]{:S(2)}) collective-permute-start(bf16[64,3072]{1,0:T(8,128)(2,1)} %convert_add_fusion.4), channel_id=1, source_target_pairs={{0,8},{1,9},{2,10},{3,11},{4,12},{5,13},{6,14},{7,15},{8,0},{9,1},... | collective-permute-start | bytes 1179656 | tf_op jit(solution)/shard_map/ppermute | solution.py:505
  131.6 2.9 %collective-permute-start.35 = (bf16[96,3072]{1,0:T(8,128)(2,1)}, bf16[96,3072]{1,0:T(8,128)(2,1)S(1)}, u32[]{:S(2)}, u32[]{:S(2)}) collective-permute-start(bf16[96,3072]{1,0:T(8,128)(2,1)} %get-tuple-element.151), channel_id=1, source_target_pairs={{1,0},{0,1},{3,2},{2,3},{5,4},{4,5},{7,6},{6,7},{9,8},{8,9},{11,10... | collective-permute-start | bytes 1769480 | tf_op jit(solution)/shard_map/ppermute | solution.py:505
  132.8 12.0 %collective-permute-start.42 = (bf16[64,3072]{1,0:T(8,128)(2,1)S(1)}, bf16[64,3072]{1,0:T(8,128)(2,1)S(1)}, u32[]{:S(2)}, u32[]{:S(2)}) collective-permute-start(bf16[64,3072]{1,0:T(8,128)(2,1)S(1)} %add_convert_fusion.3), channel_id=1, source_target_pairs={{0,2},{1,3},{2,0},{3,1},{4,6},{5,7},{6,4},{7,5},{8,10},{9,11},{10,... | collective-permute-start | bytes 1179656 | tf_op jit(solution)/shard_map/ppermute | solution.py:505
  134.7 13.8 %collective-permute-start.38 = (bf16[36,3072]{1,0:T(8,128)(2,1)S(1)}, bf16[36,3072]{1,0:T(8,128)(2,1)S(1)}, u32[]{:S(2)}, u32[]{:S(2)}) collective-permute-start(bf16[36,3072]{1,0:T(8,128)(2,1)S(1)} %pad_maximum_fusion), channel_id=1, source_target_pairs={{0,8},{1,9},{2,10},{3,11},{4,12},{5,13},{6,14},{7,15},{8,0},{9,1},... | collective-permute-start | bytes 663560 | tf_op jit(solution)/shard_map/ppermute | solution.py:505
  136.3 16.7 %collective-permute-start.36 = (bf16[128,1536]{1,0:T(8,128)(2,1)S(1)}, bf16[128,1536]{1,0:T(8,128)(2,1)S(1)}, u32[]{:S(2)}, u32[]{:S(2)}) collective-permute-start(bf16[128,1536]{1,0:T(8,128)(2,1)S(1)} %fusion.6), channel_id=1, source_target_pairs={{0,16},{1,17},{2,18},{3,19},{4,20},{5,21},{6,22},{7,23},{8,24},{9,... | collective-permute-start | bytes 1179656 | tf_op jit(solution)/shard_map/ppermute | solution.py:510
  138.3 14.7 %collective-permute-start.37 = (bf16[128,1536]{1,0:T(8,128)(2,1)S(1)}, bf16[128,1536]{1,0:T(8,128)(2,1)S(1)}, u32[]{:S(2)}, u32[]{:S(2)}) collective-permute-start(bf16[128,1536]{1,0:T(8,128)(2,1)S(1)} %fusion.7), channel_id=1, source_target_pairs={{0,2},{1,3},{2,0},{3,1},{4,6},{5,7},{6,4},{7,5},{8,10},{9,11},{10,... | collective-permute-start | bytes 1179656 | tf_op jit(solution)/shard_map/ppermute | solution.py:510
  139.5 18.7 %collective-permute-start.39 = (bf16[256,3072]{1,0:T(8,128)(2,1)S(1)}, bf16[256,3072]{1,0:T(8,128)(2,1)S(1)}, u32[]{:S(2)}, u32[]{:S(2)}) collective-permute-start(bf16[256,3072]{1,0:T(8,128)(2,1)S(1)} %copy-done.32), channel_id=1, source_target_pairs={{1,0},{0,1},{3,2},{2,3},{5,4},{4,5},{7,6},{6,7},{9,8},{8,9},{11,10... | collective-permute-start | bytes 4718600 | tf_op jit(solution)/shard_map/ppermute | solution.py:505
  148.9 7.1 %collective-permute-start.40 = (bf16[16,3072]{1,0:T(8,128)(2,1)S(1)}, bf16[16,3072]{1,0:T(8,128)(2,1)S(1)}, u32[]{:S(2)}, u32[]{:S(2)}) collective-permute-start(bf16[16,3072]{1,0:T(8,128)(2,1)S(1)} %pad_maximum_fusion.2), channel_id=1, source_target_pairs={{0,2},{1,3},{2,4},{3,5},{4,6},{5,7},{8,10},{9,11},{10,12},{11,13},... | collective-permute-start | bytes 294920 | tf_op jit(solution)/shard_map/ppermute | solution.py:505
  151.6 6.5 %collective-permute-start.41 = (bf16[16,3072]{1,0:T(8,128)(2,1)S(1)}, bf16[16,3072]{1,0:T(8,128)(2,1)S(1)}, u32[]{:S(2)}, u32[]{:S(2)}) collective-permute-start(bf16[16,3072]{1,0:T(8,128)(2,1)S(1)} %pad_maximum_fusion.1), channel_id=1, source_target_pairs={{2,0},{3,1},{4,2},{5,3},{6,4},{7,5},{10,8},{11,9},{12,10},{13,11},... | collective-permute-start | bytes 294920 | tf_op jit(solution)/shard_map/ppermute | solution.py:505
  153.0 1.8 %collective-permute-start.43 = (bf16[64,3072]{1,0:T(8,128)(2,1)S(1)}, bf16[64,3072]{1,0:T(8,128)(2,1)S(1)}, u32[]{:S(2)}, u32[]{:S(2)}) collective-permute-start(bf16[64,3072]{1,0:T(8,128)(2,1)S(1)} %add_convert_fusion.2), channel_id=1, source_target_pairs={{0,1},{1,0},{2,3},{3,2},{4,5},{5,4},{6,7},{7,6},{8,9},{9,8},{10,11... | collective-permute-start | bytes 1179656 | tf_op jit(solution)/shard_map/ppermute | solution.py:505
  (33 other events, 148.3 us)

commit v5 on v4

--- a/solution.py
+++ b/solution.py
@@ -306,7 +306,7 @@
         whole((total, tokens)),
         jax.ShapeDtypeStruct((total, tokens), parts[0].dtype),
         [],
-    )(me[None], *in_hbm(parts))
+    )(me[None], *in_hbm(parts[:1]), *parts[1:])
 
 
 def edge_kernel(where, keys, values, to_left, to_right, edge):
@@ -374,7 +374,8 @@
         (1,),
         [whole(here.shape)] * 2,
         [whole((2, rows, tokens))] * 4,
-        [jax.ShapeDtypeStruct((2, rows, tokens), BF16)] * 4,
+        [pltpu.HBM((2, rows, tokens), BF16)]
+        + [jax.ShapeDtypeStruct((2, rows, tokens), BF16)] * 3,
         [],
     )(here, there)
 
@@ -460,9 +461,9 @@
         four if core else [two] * 2,
         jax.ShapeDtypeStruct((4, TILE, width), BF16)
         if core
-        else [jax.ShapeDtypeStruct(shape, BF16)] * 2,
+        else [pltpu.HBM(shape, BF16), jax.ShapeDtypeStruct(shape, BF16)],
         [pltpu.VMEM((4 * TILE, rows), BF16)],
-    )(*in_hbm(weights), *in_hbm(parts), *added)
+    )(*in_hbm(weights), *in_hbm(parts[:1]), *parts[1:], *added)
 
 
 def bias_kernel(shifts, frames, where, bias):
@@ -583,7 +584,7 @@
 
     outer = permute(to_outer, to_band)
     beside = swap(after(upstream, to_outer), 0, 2)
-    upper = swap(after(across[: TILE // 2], to_outer), 0, 2)
+    upper = swap(after(across[: TILE * 5 // 8], to_outer), 0, 2)
     opened = (outer, beside, upper)
     if turns == 4:
         two_low = swap(after(low_rows, to_outer), 0, 8)
@@ -598,9 +599,10 @@
             found |= {t ^ bit: swap(block, 0, 4 * bit) for t, block in found.items()}
         weights = [found[t] for t in range(turns)]
         fetched = []
-    lower = swap(after(beside[TILE // 2 :], opened), 1, 0)
+    lower = swap(after(beside[TILE * 5 // 8 :], opened), 1, 0)
     across_other = swap(after(across, opened), 0, 1)
-    fetched.append(lower)
+    beside_other = swap(after(beside, opened), 0, 1)
+    fetched += [lower, beside_other]
 
     rim = column_call(rim_kernel, [], [after(left, opened), right, outer], [2 * RIM])
     slots = [(input_keys, input_values, rim)] + [
@@ -631,12 +633,12 @@
     att_got = [swap(pair, x, 2 * y) for (x, y), pair in zip(PLACES[1:], att_packed[1:])]
     upstream_here, across, across_other, beside = in_hbm([upstream, across, across_other, beside])
     tokens = [
-        [upstream_here, swap(after(upstream, att), 0, 1)],
+        [upstream_here, swap(after(upstream, att_packed), 0, 1)],
         [across, across_other],
-        [beside, swap(after(beside, att), 0, 1)],
-        [upper, lower, swap(after(upper, att), 0, 1), swap(after(lower, att), 0, 1)],
-    ]
-    grads_like, grads_other = grad_parts([after(weights[0], att), *weights[1:]], tokens)
+        [beside, beside_other],
+        [upper, lower, swap(after(upper, att_packed), 0, 1), swap(after(lower, att), 0, 1)],
+    ]
+    grads_like, grads_other = grad_parts([after(weights[0], att, got), *weights[1:]], tokens)
     att_of = [att_packed[0], *after(att_got, grads_like)]
     for bit in bits[1:-1]:
         part, got = add_over(part, bit, grads_like)

time: 162 us -> 159 us (0.981)
  waiting for transfers between devices: 57.6 us -> 55.3 us
  starting transfers between devices: 40.8 us -> 42.8 us
  local copies, waits for them, and re-layouts: 9.53 us -> 7.58 us
    unnamed x74 -> x60, local copies, waits for them, and re-layouts: 5.42 us -> 3.44 us
where the time goes in v5:
time: 159 us
  waiting for transfers between devices  55.3 us (35%)
  starting transfers between devices  42.8 us (27%)
  Pallas kernels  38.8 us (24%)
  local copies, waits for them, and re-layouts  7.58 us (5%)
  other arithmetic  6.98 us (4%)
  matrix products  5.94 us (4%)
    ppermute x16, waiting for transfers between devices, permute(): return lax.ppermute(block, 'tensor', route)  42.4 us
    ppermute x28, starting transfers between devices, swap(): lax.ppermute(block, ('groups', 'tensor'), [(g * devices + i, (g ^ group_b...  28.1 us
    ppermute x16, starting transfers between devices, permute(): return lax.ppermute(block, 'tensor', route)  14.7 us
    pallas_call x2, Pallas kernels, from_hbm(): return call(scalars, *in_hbm(arrays[:3]), *arrays[3:])  14.3 us
    ppermute x28, waiting for transfers between devices, swap(): lax.ppermute(block, ('groups', 'tensor'), [(g * devices + i, (g ^ group_b...  12.8 us
    pallas_call x4, Pallas kernels, project(): plain_call(functools.partial(project_kernel, len(weights), core, kept), (...  12.4 us
    dot_general x4, matrix products, tn(): lax.dot_general(a, b, (((0,), (0,)), ((), ())), preferred_element_type=F32)  5.55 us
    pallas_call x1, Pallas kernels, grad_parts(): plain_call(functools.partial(grad_kernel, len(weights), counts), (width /...  4.85 us
  transfers between devices with their start and end apart: 44, of which 13 were waited for; matrix products, arithmetic and copies ran while one was open for 9% of the time, Pallas kernels for 23%

profile of v5, /device:TPU:0, one launch (start us, length us, event | category | flops | bytes accessed | tf_op | source)
XLA Modules:
  0.0 158.7 jit_solution(1767293020067622077)
XLA Ops:
  1.4 3.0 %collective-permute-start.6 = (bf16[128,3072]{1,0:T(8,128)(2,1)}, bf16[128,3072]{1,0:T(8,128)(2,1)}, u32[]{:S(2)}, u32[]{:S(2)}) collective-permute-start(bf16[128,3072]{1,0:T(8,128)(2,1)} %refs_6_.1), channel_id=1, source_target_pairs={{0,16},{1,17},{2,18},{3,19},{4,20},{5,21},{6,22},{7,23},{8,24},{9,... | collective-permute-start | bytes 2359304 | tf_op jit(solution)/shard_map/ppermute | solution.py:511
  4.9 2.0 %constant_dynamic-slice_fusion.1 = (bf16[48,3072]{1,0:T(8,128)(2,1)}, bf16[48,3072]{1,0:T(8,128)(2,1)}) fusion(bf16[192,3072]{1,0:T(8,128)(2,1)} %param.12, s32[]{:T(128)S(6)} %select_n.54, s32[]{:T(128)S(6)} %add.131), kind=kLoop, calls=%fused_computation.58 | loop fusion | bytes 1179656 | tf_op jit(solution)/shard_map/slice | solution.py:573
  6.9 2.6 %collective-permute-start.1 = (bf16[48,3072]{1,0:T(8,128)(2,1)}, bf16[48,3072]{1,0:T(8,128)(2,1)}, u32[]{:S(2)}, u32[]{:S(2)}) collective-permute-start(bf16[48,3072]{1,0:T(8,128)(2,1)} %get-tuple-element.172), channel_id=1, source_target_pairs={{0,8},{1,9},{2,10},{3,11},{4,12},{5,13},{6,14},{7,15},{8,0},{9,1},... | collective-permute-start | bytes 884744 | tf_op jit(solution)/shard_map/ppermute | solution.py:511
  10.4 1.6 collective-permute-start
  11.9 3.7 %shard_map.136 = (bf16[16,3072]{1,0:T(8,128)(2,1)}, bf16[16,3072]{1,0:T(8,128)(2,1)}, bf16[32,3072]{1,0:T(8,128)(2,1)}) custom-call(s32[1]{0:T(128)} %bitcast.where, bf16[128,3072]{1,0:T(8,128)(2,1)} %refs_0_.3, bf16[128,3072]{1,0:T(8,128)(2,1)} %refs_1_.3), custom_call_target="tpu_custom_call" | custom-call | flops 1000 | bytes 1000 | tf_op jit(solution)/shard_map/pallas_call | solution.py:352
  16.1 1.5 convolution_bitcast_fusion.refs_9_
  17.7 1.3 collective-permute-start.5
  19.1 4.6 %collective-permute-start.4 = (bf16[16,3072]{1,0:T(8,128)(2,1)S(1)}, bf16[16,3072]{1,0:T(8,128)(2,1)S(1)}, u32[]{:S(2)}, u32[]{:S(2)}) collective-permute-start(bf16[16,3072]{1,0:T(8,128)(2,1)S(1)} %copy-done.26), channel_id=1, source_target_pairs={{0,2},{1,3},{2,4},{3,5},{4,6},{5,7},{8,10},{9,11},{10,12},{11,13},... | collective-permute-start | bytes 294920 | tf_op jit(solution)/shard_map/ppermute | solution.py:506
  23.7 8.2 %collective-permute-done.refs_1_ = bf16[96,3072]{1,0:T(8,128)(2,1)} collective-permute-done((bf16[96,3072]{1,0:T(8,128)(2,1)}, bf16[96,3072]{1,0:T(8,128)(2,1)}, u32[]{:S(2)}, u32[]{:S(2)}) %collective-permute-start) | collective-permute-done | bytes 589856 | tf_op jit(solution)/shard_map/ppermute | solution.py:511
  32.2 2.4 %collective-permute-start.10 = (bf16[128,3072]{1,0:T(8,128)(2,1)S(1)}, bf16[128,3072]{1,0:T(8,128)(2,1)S(1)}, u32[]{:S(2)}, u32[]{:S(2)}) collective-permute-start(bf16[128,3072]{1,0:T(8,128)(2,1)S(1)} %copy-done.15), channel_id=1, source_target_pairs={{0,2},{1,3},{2,0},{3,1},{4,6},{5,7},{6,4},{7,5},{8,10},{9,11},{10,... | collective-permute-start | bytes 2359304 | tf_op jit(solution)/shard_map/ppermute | solution.py:511
  34.6 1.1 slice.148
  35.8 2.1 %collective-permute-start.8 = (bf16[48,3072]{1,0:T(8,128)(2,1)}, bf16[48,3072]{1,0:T(8,128)(2,1)S(1)}, u32[]{:S(2)}, u32[]{:S(2)}) collective-permute-start(bf16[48,3072]{1,0:T(8,128)(2,1)} %collective-permute-done.1.refs_2_), channel_id=1, source_target_pairs={{0,4},{1,5},{2,6},{3,7},{4,0},{5,1},{6,2},{7,3},{8,12},{9,13},{10,... | collective-permute-start | bytes 884744 | tf_op jit(solution)/shard_map/ppermute | solution.py:511
  37.9 2.4 %collective-permute-start.7 = (bf16[48,3072]{1,0:T(8,128)(2,1)S(1)}, bf16[48,3072]{1,0:T(8,128)(2,1)S(1)}, u32[]{:S(2)}, u32[]{:S(2)}) collective-permute-start(bf16[48,3072]{1,0:T(8,128)(2,1)S(1)} %copy-done.23), channel_id=1, source_target_pairs={{0,8},{1,9},{2,10},{3,11},{4,12},{5,13},{6,14},{7,15},{8,0},{9,1},... | collective-permute-start | bytes 884744 | tf_op jit(solution)/shard_map/ppermute | solution.py:511
  40.8 22.1 %collective-permute-done.9.outer = bf16[40,3072]{1,0:T(8,128)(2,1)S(1)} collective-permute-done((bf16[40,3072]{1,0:T(8,128)(2,1)S(1)}, bf16[40,3072]{1,0:T(8,128)(2,1)S(1)}, u32[]{:S(2)}, u32[]{:S(2)}) %collective-permute-start.9) | collective-permute-done | bytes 245792 | tf_op jit(solution)/shard_map/ppermute | solution.py:506
  65.7 1.5 collective-permute-done.14.refs_5_
  67.3 6.6 %shard_map.140 = (bf16[3072,128]{1,0:T(8,128)(2,1)}, f32[3,8,128]{2,1,0:T(8,128)S(1)}, bf16[2,64,3072]{2,1,0:T(8,128)(2,1)S(1)}, bf16[64,128]{1,0:T(8,128)(2,1)S...) custom-call(s32[26]{0:T(128)S(1)} %pad_add_fusion.1.combo, bf16[128,3072]{1,0:T(8,128)(2,1)} %query.1, ...), custom_call_target="tpu_custom_call" | custom-call | flops 1000 | bytes 1000 | tf_op jit(solution)/shard_map/pallas_call | solution.py:154
  76.6 1.0 collective-permute-start.18
  78.1 2.1 %collective-permute-start.20 = (bf16[2,384,128]{2,1,0:T(8,128)(2,1)S(1)}, bf16[2,384,128]{2,1,0:T(8,128)(2,1)S(1)}, u32[]{:S(2)}, u32[]{:S(2)}) collective-permute-start(bf16[2,384,128]{2,1,0:T(8,128)(2,1)S(1)} %get-tuple-element.114), channel_id=1, source_target_pairs={{0,18},{1,19},{2,16},{3,17},{4,22},{5,23},{6,20},{7,21},{8,26},{9,... | collective-permute-start | bytes 589832 | tf_op jit(solution)/shard_map/ppermute | solution.py:511
  80.3 1.8 %collective-permute-done.23.refs_14_ = bf16[80,3072]{1,0:T(8,128)(2,1)S(1)} collective-permute-done((bf16[80,3072]{1,0:T(8,128)(2,1)S(1)}, bf16[80,3072]{1,0:T(8,128)(2,1)S(1)}, u32[]{:S(2)}, u32[]{:S(2)}) %collective-permute-start.23) | collective-permute-done | bytes 491552 | tf_op jit(solution)/shard_map/ppermute | solution.py:511
  82.9 4.8 %shard_map.142 = (bf16[4,384,128]{2,1,0:T(8,128)(2,1)S(1)}, bf16[4,384,128]{2,1,0:T(8,128)(2,1)S(1)}) custom-call(bf16[96,3072]{1,0:T(8,128)(2,1)} %constant_dynamic-slice_fusion.2.refs_0_, bf16[96,3072]{1,0:T(8,128)(2,1)} %collective-permute-done.refs_1_, bf16[48,3072]{1,0:T(8,128)(2,1)} %collective-permute-done.1.refs_2_, bf16[48,3072]{1,0:T(8,128)(2,1)} %copy-done.12, ...), custom_call_target="tpu_custom_call" | custom-call | flops 1000 | bytes 1000 | tf_op jit(solution)/shard_map/pallas_call | solution.py:415
  87.7 1.1 collective-permute-done.19.refs_8_
  88.8 2.7 %shard_map.146 = bf16[4,128,1536]{2,1,0:T(8,128)(2,1)S(1)} custom-call(bf16[96,3072]{1,0:T(8,128)(2,1)} %constant_dynamic-slice_fusion.2.refs_0_, bf16[96,3072]{1,0:T(8,128)(2,1)} %collective-permute-done.refs_1_, bf16[48,3072]{1,0:T(8,128)(2,1)} %collective-permute-done.1.refs_2_, bf16[48,3072]{1,0:T(8,128)(2,1)} %copy-done.12, ...), custom_call_target="tpu_custom_call" | custom-call | flops 1000 | bytes 1000 | tf_op jit(solution)/shard_map/pallas_call | solution.py:455
  91.5 2.7 %shard_map.143 = bf16[4,128,1536]{2,1,0:T(8,128)(2,1)S(1)} custom-call(bf16[96,3072]{1,0:T(8,128)(2,1)} %constant_dynamic-slice_fusion.2.refs_0_, bf16[96,3072]{1,0:T(8,128)(2,1)} %collective-permute-done.refs_1_, bf16[48,3072]{1,0:T(8,128)(2,1)} %collective-permute-done.1.refs_2_, bf16[48,3072]{1,0:T(8,128)(2,1)} %copy-done.12, ...), custom_call_target="tpu_custom_call" | custom-call | flops 1000 | bytes 1000 | tf_op jit(solution)/shard_map/pallas_call | solution.py:455
  95.6 1.0 collective-permute-start.31
  97.3 1.8 %collective-permute-start.33 = (bf16[2,384,128]{2,1,0:T(8,128)(2,1)S(1)}, bf16[2,384,128]{2,1,0:T(8,128)(2,1)S(1)}, u32[]{:S(2)}, u32[]{:S(2)}) collective-permute-start(bf16[2,384,128]{2,1,0:T(8,128)(2,1)S(1)} %get-tuple-element.130), channel_id=1, source_target_pairs={{0,18},{1,19},{2,16},{3,17},{4,22},{5,23},{6,20},{7,21},{8,26},{9,... | collective-permute-start | bytes 589832 | tf_op jit(solution)/shard_map/ppermute | solution.py:511
  99.1 3.5 %shard_map.147 = (bf16[2,128,1536]{2,1,0:T(8,128)(2,1)}, bf16[2,128,1536]{2,1,0:T(8,128)(2,1)}) custom-call(bf16[96,3072]{1,0:T(8,128)(2,1)} %constant_dynamic-slice_fusion.2.refs_0_, bf16[96,3072]{1,0:T(8,128)(2,1)} %collective-permute-done.refs_1_, bf16[48,3072]{1,0:T(8,128)(2,1)} %collective-permute-done.1.refs_2_, bf16[48,3072]{1,0:T(8,128)(2,1)} %copy-done.12, ...), custom_call_target="tpu_custom_call" | custom-call | flops 1000 | bytes 1000 | tf_op jit(solution)/shard_map/pallas_call | solution.py:455
  102.5 1.0 collective-permute-start.30
  103.5 3.4 %shard_map.145 = (bf16[2,128,1536]{2,1,0:T(8,128)(2,1)}, bf16[2,128,1536]{2,1,0:T(8,128)(2,1)}) custom-call(bf16[96,3072]{1,0:T(8,128)(2,1)} %constant_dynamic-slice_fusion.2.refs_0_, bf16[96,3072]{1,0:T(8,128)(2,1)} %collective-permute-done.refs_1_, bf16[48,3072]{1,0:T(8,128)(2,1)} %collective-permute-done.1.refs_2_, bf16[48,3072]{1,0:T(8,128)(2,1)} %copy-done.12, ...), custom_call_target="tpu_custom_call" | custom-call | flops 1000 | bytes 1000 | tf_op jit(solution)/shard_map/pallas_call | solution.py:455
  109.9 1.0 collective-permute-start.34
  111.0 1.0 copy-done.8
  112.9 1.0 shard_map.148.refs_8_
  113.9 7.7 %shard_map.149 = (bf16[128,3072]{1,0:T(8,128)(2,1)}, bf16[256,3072]{1,0:T(8,128)(2,1)}, bf16[96,3072]{1,0:T(8,128)(2,1)}, bf16[256,3072]{1,0:T(8,128)(2,1)}, bf16[96,3072]{1,0:T(8,128)(2,1)}) custom-call(s32[26]{0:T(128)S(1)} %pad_add_fusion.1.combo, bf16[128,3072]{1,0:T(8,128)(2,1)} %query.1, bf16[128,3072]{1,0:T(8,128)(2,1)} %refs_0_.3, ...), custom_call_target="tpu_custom_call" | custom-call | flops 1000 | bytes 1000 | tf_op jit(solution)/shard_map/pallas_call | solution.py:154
  121.7 8.2 %collective-permute-done.34 = bf16[64,3072]{1,0:T(8,128)(2,1)} collective-permute-done((bf16[64,3072]{1,0:T(8,128)(2,1)}, bf16[64,3072]{1,0:T(8,128)(2,1)}, u32[]{:S(2)}, u32[]{:S(2)}) %collective-permute-start.34) | collective-permute-done | bytes 393248 | tf_op jit(solution)/shard_map/ppermute | solution.py:506
  129.9 1.2 add_convert_fusion.3
  131.1 1.3 collective-permute-start.42
  132.8 1.4 convert_add_fusion.1
  134.3 1.1 collective-permute-start.36
  135.4 1.3 convert_add_fusion
  136.8 1.0 collective-permute-start.37
  137.8 5.3 %collective-permute-done.42 = bf16[64,3072]{1,0:T(8,128)(2,1)S(1)} collective-permute-done((bf16[64,3072]{1,0:T(8,128)(2,1)S(1)}, bf16[64,3072]{1,0:T(8,128)(2,1)S(1)}, u32[]{:S(2)}, u32[]{:S(2)}) %collective-permute-start.42) | collective-permute-done | bytes 393248 | tf_op jit(solution)/shard_map/ppermute | solution.py:506
  143.1 3.2 %collective-permute-done.38 = bf16[36,3072]{1,0:T(8,128)(2,1)S(1)} collective-permute-done((bf16[36,3072]{1,0:T(8,128)(2,1)S(1)}, bf16[36,3072]{1,0:T(8,128)(2,1)S(1)}, u32[]{:S(2)}, u32[]{:S(2)}) %collective-permute-start.38) | collective-permute-done | bytes 221216 | tf_op jit(solution)/shard_map/ppermute | solution.py:506
  146.6 2.7 %collective-permute-start.40 = (bf16[16,3072]{1,0:T(8,128)(2,1)S(1)}, bf16[16,3072]{1,0:T(8,128)(2,1)S(1)}, u32[]{:S(2)}, u32[]{:S(2)}) collective-permute-start(bf16[16,3072]{1,0:T(8,128)(2,1)S(1)} %pad_maximum_fusion.2), channel_id=1, source_target_pairs={{0,2},{1,3},{2,4},{3,5},{4,6},{5,7},{8,10},{9,11},{10,12},{11,13},... | collective-permute-start | bytes 294920 | tf_op jit(solution)/shard_map/ppermute | solution.py:506
  149.4 1.3 collective-permute-start.41
  151.4 1.3 fusion.1
  152.9 1.2 select_convert_fusion
  154.1 1.8 %collective-permute-done.41 = bf16[16,3072]{1,0:T(8,128)(2,1)S(1)} collective-permute-done((bf16[16,3072]{1,0:T(8,128)(2,1)S(1)}, bf16[16,3072]{1,0:T(8,128)(2,1)S(1)}, u32[]{:S(2)}, u32[]{:S(2)}) %collective-permute-start.41) | collective-permute-done | bytes 98336 | tf_op jit(solution)/shard_map/ppermute | solution.py:506
  156.0 1.4 add_convert_fusion
  157.3 1.4 add_convert_fusion.1
  (151 shorter events, 17.8 us)
Async XLA Ops:
  1.4 30.5 %collective-permute-start.6 = (bf16[128,3072]{1,0:T(8,128)(2,1)}, bf16[128,3072]{1,0:T(8,128)(2,1)}, u32[]{:S(2)}, u32[]{:S(2)}) collective-permute-start(bf16[128,3072]{1,0:T(8,128)(2,1)} %refs_6_.1), channel_id=1, source_target_pairs={{0,16},{1,17},{2,18},{3,19},{4,20},{5,21},{6,22},{7,23},{8,24},{9,... | collective-permute-start | bytes 2359304 | tf_op jit(solution)/shard_map/ppermute | solution.py:511
  4.4 13.3 %collective-permute-start.2 = (bf16[128,3072]{1,0:T(8,128)(2,1)}, bf16[128,3072]{1,0:T(8,128)(2,1)S(1)}, u32[]{:S(2)}, u32[]{:S(2)}) collective-permute-start(bf16[128,3072]{1,0:T(8,128)(2,1)} %refs_0_.3), channel_id=1, source_target_pairs={{0,1},{1,0},{2,3},{3,2},{4,5},{5,4},{6,7},{7,6},{8,9},{9,8},{10,11... | collective-permute-start | bytes 2359304 | tf_op jit(solution)/shard_map/ppermute | solution.py:506
  4.4 13.3 %collective-permute-start.3 = (bf16[128,3072]{1,0:T(8,128)(2,1)}, bf16[128,3072]{1,0:T(8,128)(2,1)}, u32[]{:S(2)}, u32[]{:S(2)}) collective-permute-start(bf16[128,3072]{1,0:T(8,128)(2,1)} %refs_1_.3), channel_id=1, source_target_pairs={{0,1},{1,0},{2,3},{3,2},{4,5},{5,4},{6,7},{7,6},{8,9},{9,8},{10,11... | collective-permute-start | bytes 2359304 | tf_op jit(solution)/shard_map/ppermute | solution.py:506
  6.9 16.8 %collective-permute-start.1 = (bf16[48,3072]{1,0:T(8,128)(2,1)}, bf16[48,3072]{1,0:T(8,128)(2,1)}, u32[]{:S(2)}, u32[]{:S(2)}) collective-permute-start(bf16[48,3072]{1,0:T(8,128)(2,1)} %get-tuple-element.172), channel_id=1, source_target_pairs={{0,8},{1,9},{2,10},{3,11},{4,12},{5,13},{6,14},{7,15},{8,0},{9,1},... | collective-permute-start | bytes 884744 | tf_op jit(solution)/shard_map/ppermute | solution.py:511
  10.4 21.5 %collective-permute-start = (bf16[96,3072]{1,0:T(8,128)(2,1)}, bf16[96,3072]{1,0:T(8,128)(2,1)}, u32[]{:S(2)}, u32[]{:S(2)}) collective-permute-start(bf16[96,3072]{1,0:T(8,128)(2,1)} %constant_dynamic-slice_fusion.2.refs_0_), channel_id=1, source_target_pairs={{0,4},{1,5},{2,6},{3,7},{4,0},{5,1},{6,2},{7,3},{8,12},{9,13},{10,... | collective-permute-start | bytes 1769480 | tf_op jit(solution)/shard_map/ppermute | solution.py:511
  15.7 16.2 %copy-start.6 = (bf16[32,3072]{1,0:T(8,128)(2,1)S(1)}, bf16[32,3072]{1,0:T(8,128)(2,1)}, u32[]{:S(2)}) copy-start(bf16[32,3072]{1,0:T(8,128)(2,1)} %get-tuple-element.92.edge) | copy-start | bytes 589828
  16.1 16.1 %copy-start.15 = (bf16[128,3072]{1,0:T(8,128)(2,1)S(1)}, bf16[128,3072]{1,0:T(8,128)(2,1)}, u32[]{:S(2)}) copy-start(bf16[128,3072]{1,0:T(8,128)(2,1)} %refs_6_.1) | copy-start | bytes 2359300
  16.1 21.7 %copy-start.23 = (bf16[48,3072]{1,0:T(8,128)(2,1)S(1)}, bf16[48,3072]{1,0:T(8,128)(2,1)}, u32[]{:S(2)}) copy-start(bf16[48,3072]{1,0:T(8,128)(2,1)} %get-tuple-element.93) | copy-start | bytes 884740
  17.7 45.3 %copy-start.1 = (bf16[128,3072]{1,0:T(8,128)(2,1)}, bf16[128,3072]{1,0:T(8,128)(2,1)S(1)}, u32[]{:S(2)}) copy-start(bf16[128,3072]{1,0:T(8,128)(2,1)S(1)} %collective-permute-done.2.refs_3_) | copy-start | bytes 2359300
  17.7 14.2 %collective-permute-start.5 = (bf16[16,3072]{1,0:T(8,128)(2,1)S(1)}, bf16[16,3072]{1,0:T(8,128)(2,1)S(1)}, u32[]{:S(2)}, u32[]{:S(2)}) collective-permute-start(bf16[16,3072]{1,0:T(8,128)(2,1)S(1)} %copy-done.27), channel_id=1, source_target_pairs={{2,0},{3,1},{4,2},{5,3},{6,4},{7,5},{10,8},{11,9},{12,10},{13,11},... | collective-permute-start | bytes 294920 | tf_op jit(solution)/shard_map/ppermute | solution.py:506
  19.1 12.8 %collective-permute-start.4 = (bf16[16,3072]{1,0:T(8,128)(2,1)S(1)}, bf16[16,3072]{1,0:T(8,128)(2,1)S(1)}, u32[]{:S(2)}, u32[]{:S(2)}) collective-permute-start(bf16[16,3072]{1,0:T(8,128)(2,1)S(1)} %copy-done.26), channel_id=1, source_target_pairs={{0,2},{1,3},{2,4},{3,5},{4,6},{5,7},{8,10},{9,11},{10,12},{11,13},... | collective-permute-start | bytes 294920 | tf_op jit(solution)/shard_map/ppermute | solution.py:506
  32.2 30.7 %collective-permute-start.10 = (bf16[128,3072]{1,0:T(8,128)(2,1)S(1)}, bf16[128,3072]{1,0:T(8,128)(2,1)S(1)}, u32[]{:S(2)}, u32[]{:S(2)}) collective-permute-start(bf16[128,3072]{1,0:T(8,128)(2,1)S(1)} %copy-done.15), channel_id=1, source_target_pairs={{0,2},{1,3},{2,0},{3,1},{4,6},{5,7},{6,4},{7,5},{8,10},{9,11},{10,... | collective-permute-start | bytes 2359304 | tf_op jit(solution)/shard_map/ppermute | solution.py:511
  35.7 27.2 %collective-permute-start.11 = (bf16[80,3072]{1,0:T(8,128)(2,1)S(1)}, bf16[80,3072]{1,0:T(8,128)(2,1)S(1)}, u32[]{:S(2)}, u32[]{:S(2)}) collective-permute-start(bf16[80,3072]{1,0:T(8,128)(2,1)S(1)} %slice.148), channel_id=1, source_target_pairs={{0,2},{1,3},{2,0},{3,1},{4,6},{5,7},{6,4},{7,5},{8,10},{9,11},{10,... | collective-permute-start | bytes 1474568 | tf_op jit(solution)/shard_map/ppermute | solution.py:511
  35.8 27.1 %collective-permute-start.8 = (bf16[48,3072]{1,0:T(8,128)(2,1)}, bf16[48,3072]{1,0:T(8,128)(2,1)S(1)}, u32[]{:S(2)}, u32[]{:S(2)}) collective-permute-start(bf16[48,3072]{1,0:T(8,128)(2,1)} %collective-permute-done.1.refs_2_), channel_id=1, source_target_pairs={{0,4},{1,5},{2,6},{3,7},{4,0},{5,1},{6,2},{7,3},{8,12},{9,13},{10,... | collective-permute-start | bytes 884744 | tf_op jit(solution)/shard_map/ppermute | solution.py:511
  37.9 25.0 %collective-permute-start.7 = (bf16[48,3072]{1,0:T(8,128)(2,1)S(1)}, bf16[48,3072]{1,0:T(8,128)(2,1)S(1)}, u32[]{:S(2)}, u32[]{:S(2)}) collective-permute-start(bf16[48,3072]{1,0:T(8,128)(2,1)S(1)} %copy-done.23), channel_id=1, source_target_pairs={{0,8},{1,9},{2,10},{3,11},{4,12},{5,13},{6,14},{7,15},{8,0},{9,1},... | collective-permute-start | bytes 884744 | tf_op jit(solution)/shard_map/ppermute | solution.py:511
  40.3 22.6 %collective-permute-start.9 = (bf16[40,3072]{1,0:T(8,128)(2,1)S(1)}, bf16[40,3072]{1,0:T(8,128)(2,1)S(1)}, u32[]{:S(2)}, u32[]{:S(2)}) collective-permute-start(bf16[40,3072]{1,0:T(8,128)(2,1)S(1)} %shard_map.138), channel_id=1, source_target_pairs={{0,8},{1,9},{2,10},{3,11},{4,12},{5,13},{6,14},{7,15},{8,0},{9,1},... | collective-permute-start | bytes 737288 | tf_op jit(solution)/shard_map/ppermute | solution.py:506
  62.9 2.8 %collective-permute-start.13 = (bf16[128,3072]{1,0:T(8,128)(2,1)}, bf16[128,3072]{1,0:T(8,128)(2,1)S(1)}, u32[]{:S(2)}, u32[]{:S(2)}) collective-permute-start(bf16[128,3072]{1,0:T(8,128)(2,1)} %collective-permute-done.6.refs_8_), channel_id=1, source_target_pairs={{0,1},{1,0},{2,3},{3,2},{4,5},{5,4},{6,7},{7,6},{8,9},{9,8},{10,11... | collective-permute-start | bytes 2359304 | tf_op jit(solution)/shard_map/ppermute | solution.py:511
  63.0 10.9 %collective-permute-start.16 = (bf16[128,3072]{1,0:T(8,128)(2,1)S(1)}, bf16[128,3072]{1,0:T(8,128)(2,1)S(1)}, u32[]{:S(2)}, u32[]{:S(2)}) collective-permute-start(bf16[128,3072]{1,0:T(8,128)(2,1)S(1)} %collective-permute-done.10.refs_10_), channel_id=1, source_target_pairs={{0,1},{1,0},{2,3},{3,2},{4,5},{5,4},{6,7},{7,6},{8,9},{9,8},{10,11... | collective-permute-start | bytes 2359304 | tf_op jit(solution)/shard_map/ppermute | solution.py:511
  63.7 3.5 %collective-permute-start.14 = (bf16[96,3072]{1,0:T(8,128)(2,1)S(1)}, bf16[96,3072]{1,0:T(8,128)(2,1)S(1)}, u32[]{:S(2)}, u32[]{:S(2)}) collective-permute-start(bf16[96,3072]{1,0:T(8,128)(2,1)S(1)} %shard_map.139.refs_2_), channel_id=1, source_target_pairs={{0,1},{1,0},{2,3},{3,2},{4,5},{5,4},{6,7},{7,6},{8,9},{9,8},{10,11... | collective-permute-start | bytes 1769480 | tf_op jit(solution)/shard_map/ppermute | solution.py:506
  63.9 10.0 %collective-permute-start.15 = (bf16[48,3072]{1,0:T(8,128)(2,1)S(1)}, bf16[48,3072]{1,0:T(8,128)(2,1)S(1)}, u32[]{:S(2)}, u32[]{:S(2)}) collective-permute-start(bf16[48,3072]{1,0:T(8,128)(2,1)S(1)} %slice.149), channel_id=1, source_target_pairs={{0,16},{1,17},{2,18},{3,19},{4,20},{5,21},{6,22},{7,23},{8,24},{9,... | collective-permute-start | bytes 884744 | tf_op jit(solution)/shard_map/ppermute | solution.py:511
  64.5 9.4 %collective-permute-start.12 = (bf16[48,3072]{1,0:T(8,128)(2,1)S(1)}, bf16[48,3072]{1,0:T(8,128)(2,1)S(1)}, u32[]{:S(2)}, u32[]{:S(2)}) collective-permute-start(bf16[48,3072]{1,0:T(8,128)(2,1)S(1)} %collective-permute-done.7.refs_3_), channel_id=1, source_target_pairs={{0,4},{1,5},{2,6},{3,7},{4,0},{5,1},{6,2},{7,3},{8,12},{9,13},{10,... | collective-permute-start | bytes 884744 | tf_op jit(solution)/shard_map/ppermute | solution.py:511
  74.0 1.8 %collective-permute-start.17 = (bf16[4,384,128]{2,1,0:T(8,128)(2,1)S(1)}, bf16[4,384,128]{2,1,0:T(8,128)(2,1)S(1)}, u32[]{:S(2)}, u32[]{:S(2)}) collective-permute-start(bf16[4,384,128]{2,1,0:T(8,128)(2,1)S(1)} %get-tuple-element.110), channel_id=1, source_target_pairs={{0,1},{1,0},{2,3},{3,2},{4,5},{5,4},{6,7},{7,6},{8,9},{9,8},{10,11... | collective-permute-start | bytes 1179656 | tf_op jit(solution)/shard_map/ppermute | solution.py:511
  74.2 5.9 %collective-permute-start.21 = (bf16[64,3072]{1,0:T(8,128)(2,1)S(1)}, bf16[64,3072]{1,0:T(8,128)(2,1)S(1)}, u32[]{:S(2)}, u32[]{:S(2)}) collective-permute-start(bf16[64,3072]{1,0:T(8,128)(2,1)S(1)} %slice_bitcast_fusion.2), channel_id=1, source_target_pairs={{0,1},{1,0},{2,3},{3,2},{4,5},{5,4},{6,7},{7,6},{8,9},{9,8},{10,11... | collective-permute-start | bytes 1179656 | tf_op jit(solution)/shard_map/ppermute | solution.py:506
  74.6 3.4 %collective-permute-start.24 = (bf16[48,3072]{1,0:T(8,128)(2,1)S(1)}, bf16[48,3072]{1,0:T(8,128)(2,1)S(1)}, u32[]{:S(2)}, u32[]{:S(2)}) collective-permute-start(bf16[48,3072]{1,0:T(8,128)(2,1)S(1)} %collective-permute-done.15.refs_13_), channel_id=1, source_target_pairs={{0,1},{1,0},{2,3},{3,2},{4,5},{5,4},{6,7},{7,6},{8,9},{9,8},{10,11... | collective-permute-start | bytes 884744 | tf_op jit(solution)/shard_map/ppermute | solution.py:511
  76.5 6.4 %collective-permute-start.22 = (bf16[128,3072]{1,0:T(8,128)(2,1)S(1)}, bf16[128,3072]{1,0:T(8,128)(2,1)S(1)}, u32[]{:S(2)}, u32[]{:S(2)}) collective-permute-start(bf16[128,3072]{1,0:T(8,128)(2,1)S(1)} %copy-done.16), channel_id=1, source_target_pairs={{0,1},{1,0},{2,3},{3,2},{4,5},{5,4},{6,7},{7,6},{8,9},{9,8},{10,11... | collective-permute-start | bytes 2359304 | tf_op jit(solution)/shard_map/ppermute | solution.py:511
  76.6 11.1 %collective-permute-start.18 = (bf16[2,384,128]{2,1,0:T(8,128)(2,1)S(1)}, bf16[2,384,128]{2,1,0:T(8,128)(2,1)S(1)}, u32[]{:S(2)}, u32[]{:S(2)}) collective-permute-start(bf16[2,384,128]{2,1,0:T(8,128)(2,1)S(1)} %get-tuple-element.112), channel_id=1, source_target_pairs={{0,16},{1,17},{2,18},{3,19},{4,20},{5,21},{6,22},{7,23},{8,24},{9,... | collective-permute-start | bytes 589832 | tf_op jit(solution)/shard_map/ppermute | solution.py:511
  77.7 11.1 %collective-permute-start.19 = (bf16[2,384,128]{2,1,0:T(8,128)(2,1)S(1)}, bf16[2,384,128]{2,1,0:T(8,128)(2,1)S(1)}, u32[]{:S(2)}, u32[]{:S(2)}) collective-permute-start(bf16[2,384,128]{2,1,0:T(8,128)(2,1)S(1)} %get-tuple-element.113), channel_id=1, source_target_pairs={{0,2},{1,3},{2,0},{3,1},{4,6},{5,7},{6,4},{7,5},{8,10},{9,11},{10,... | collective-permute-start | bytes 589832 | tf_op jit(solution)/shard_map/ppermute | solution.py:511
  78.1 10.7 %collective-permute-start.20 = (bf16[2,384,128]{2,1,0:T(8,128)(2,1)S(1)}, bf16[2,384,128]{2,1,0:T(8,128)(2,1)S(1)}, u32[]{:S(2)}, u32[]{:S(2)}) collective-permute-start(bf16[2,384,128]{2,1,0:T(8,128)(2,1)S(1)} %get-tuple-element.114), channel_id=1, source_target_pairs={{0,18},{1,19},{2,16},{3,17},{4,22},{5,23},{6,20},{7,21},{8,26},{9,... | collective-permute-start | bytes 589832 | tf_op jit(solution)/shard_map/ppermute | solution.py:511
  80.2 1.9 %collective-permute-start.23 = (bf16[80,3072]{1,0:T(8,128)(2,1)S(1)}, bf16[80,3072]{1,0:T(8,128)(2,1)S(1)}, u32[]{:S(2)}, u32[]{:S(2)}) collective-permute-start(bf16[80,3072]{1,0:T(8,128)(2,1)S(1)} %collective-permute-done.11.refs_12_), channel_id=1, source_target_pairs={{0,1},{1,0},{2,3},{3,2},{4,5},{5,4},{6,7},{7,6},{8,9},{9,8},{10,11... | collective-permute-start | bytes 1474568 | tf_op jit(solution)/shard_map/ppermute | solution.py:511
  82.0 12.3 %collective-permute-start.26 = (bf16[64,3072]{1,0:T(8,128)(2,1)S(1)}, bf16[64,3072]{1,0:T(8,128)(2,1)S(1)}, u32[]{:S(2)}, u32[]{:S(2)}) collective-permute-start(bf16[64,3072]{1,0:T(8,128)(2,1)S(1)} %fusion.5), channel_id=1, source_target_pairs={{0,4},{1,5},{2,6},{3,7},{4,0},{5,1},{6,2},{7,3},{8,12},{9,13},{10,... | collective-permute-start | bytes 1179656 | tf_op jit(solution)/shard_map/ppermute | solution.py:506
  88.8 5.5 %collective-permute-start.25 = (bf16[4,384,128]{2,1,0:T(8,128)(2,1)S(1)}, bf16[4,384,128]{2,1,0:T(8,128)(2,1)S(1)}, u32[]{:S(2)}, u32[]{:S(2)}) collective-permute-start(bf16[4,384,128]{2,1,0:T(8,128)(2,1)S(1)} %get-tuple-element.126), channel_id=1, source_target_pairs={{0,1},{1,0},{2,3},{3,2},{4,5},{5,4},{6,7},{7,6},{8,9},{9,8},{10,11... | collective-permute-start | bytes 1179656 | tf_op jit(solution)/shard_map/ppermute | solution.py:511
  95.1 4.0 %collective-permute-start.29 = (bf16[4,128,1536]{2,1,0:T(8,128)(2,1)S(1)}, bf16[4,128,1536]{2,1,0:T(8,128)(2,1)S(1)}, u32[]{:S(2)}, u32[]{:S(2)}) collective-permute-start(bf16[4,128,1536]{2,1,0:T(8,128)(2,1)S(1)} %shard_map.146), channel_id=1, source_target_pairs={{0,1},{1,0},{2,3},{3,2},{4,5},{5,4},{6,7},{7,6},{8,9},{9,8},{10,11... | collective-permute-start | bytes 4718600 | tf_op jit(solution)/shard_map/ppermute | solution.py:511
  95.5 7.9 %collective-permute-start.27 = (bf16[4,128,1536]{2,1,0:T(8,128)(2,1)S(1)}, bf16[4,128,1536]{2,1,0:T(8,128)(2,1)S(1)}, u32[]{:S(2)}, u32[]{:S(2)}) collective-permute-start(bf16[4,128,1536]{2,1,0:T(8,128)(2,1)S(1)} %shard_map.143), channel_id=1, source_target_pairs={{0,1},{1,0},{2,3},{3,2},{4,5},{5,4},{6,7},{7,6},{8,9},{9,8},{10,11... | collective-permute-start | bytes 4718600 | tf_op jit(solution)/shard_map/ppermute | solution.py:511
  95.6 13.0 %collective-permute-start.31 = (bf16[2,384,128]{2,1,0:T(8,128)(2,1)S(1)}, bf16[2,384,128]{2,1,0:T(8,128)(2,1)S(1)}, u32[]{:S(2)}, u32[]{:S(2)}) collective-permute-start(bf16[2,384,128]{2,1,0:T(8,128)(2,1)S(1)} %get-tuple-element.128), channel_id=1, source_target_pairs={{0,16},{1,17},{2,18},{3,19},{4,20},{5,21},{6,22},{7,23},{8,24},{9,... | collective-permute-start | bytes 589832 | tf_op jit(solution)/shard_map/ppermute | solution.py:511
  96.5 12.0 %collective-permute-start.32 = (bf16[2,384,128]{2,1,0:T(8,128)(2,1)S(1)}, bf16[2,384,128]{2,1,0:T(8,128)(2,1)S(1)}, u32[]{:S(2)}, u32[]{:S(2)}) collective-permute-start(bf16[2,384,128]{2,1,0:T(8,128)(2,1)S(1)} %get-tuple-element.129), channel_id=1, source_target_pairs={{0,2},{1,3},{2,0},{3,1},{4,6},{5,7},{6,4},{7,5},{8,10},{9,11},{10,... | collective-permute-start | bytes 589832 | tf_op jit(solution)/shard_map/ppermute | solution.py:511
  97.3 11.9 %collective-permute-start.33 = (bf16[2,384,128]{2,1,0:T(8,128)(2,1)S(1)}, bf16[2,384,128]{2,1,0:T(8,128)(2,1)S(1)}, u32[]{:S(2)}, u32[]{:S(2)}) collective-permute-start(bf16[2,384,128]{2,1,0:T(8,128)(2,1)S(1)} %get-tuple-element.130), channel_id=1, source_target_pairs={{0,18},{1,19},{2,16},{3,17},{4,22},{5,23},{6,20},{7,21},{8,26},{9,... | collective-permute-start | bytes 589832 | tf_op jit(solution)/shard_map/ppermute | solution.py:511
  102.5 27.4 %collective-permute-start.30 = (bf16[2,128,1536]{2,1,0:T(8,128)(2,1)}, bf16[2,128,1536]{2,1,0:T(8,128)(2,1)}, u32[]{:S(2)}, u32[]{:S(2)}) collective-permute-start(bf16[2,128,1536]{2,1,0:T(8,128)(2,1)} %get-tuple-element.136), channel_id=1, source_target_pairs={{0,16},{1,17},{2,18},{3,19},{4,20},{5,21},{6,22},{7,23},{8,24},{9,... | collective-permute-start | bytes 2359304 | tf_op jit(solution)/shard_map/ppermute | solution.py:511
  106.9 23.0 %collective-permute-start.28 = (bf16[2,128,1536]{2,1,0:T(8,128)(2,1)}, bf16[2,128,1536]{2,1,0:T(8,128)(2,1)}, u32[]{:S(2)}, u32[]{:S(2)}) collective-permute-start(bf16[2,128,1536]{2,1,0:T(8,128)(2,1)} %get-tuple-element.134), channel_id=1, source_target_pairs={{0,2},{1,3},{2,0},{3,1},{4,6},{5,7},{6,4},{7,5},{8,10},{9,11},{10,... | collective-permute-start | bytes 2359304 | tf_op jit(solution)/shard_map/ppermute | solution.py:511
  109.9 20.0 %collective-permute-start.34 = (bf16[64,3072]{1,0:T(8,128)(2,1)}, bf16[64,3072]{1,0:T(8,128)(2,1)}, u32[]{:S(2)}, u32[]{:S(2)}) collective-permute-start(bf16[64,3072]{1,0:T(8,128)(2,1)} %convert_add_fusion.4), channel_id=1, source_target_pairs={{0,8},{1,9},{2,10},{3,11},{4,12},{5,13},{6,14},{7,15},{8,0},{9,1},... | collective-permute-start | bytes 1179656 | tf_op jit(solution)/shard_map/ppermute | solution.py:506
  129.9 2.6 %collective-permute-start.35 = (bf16[96,3072]{1,0:T(8,128)(2,1)}, bf16[96,3072]{1,0:T(8,128)(2,1)S(1)}, u32[]{:S(2)}, u32[]{:S(2)}) collective-permute-start(bf16[96,3072]{1,0:T(8,128)(2,1)} %get-tuple-element.151), channel_id=1, source_target_pairs={{1,0},{0,1},{3,2},{2,3},{5,4},{4,5},{7,6},{6,7},{9,8},{8,9},{11,10... | collective-permute-start | bytes 1769480 | tf_op jit(solution)/shard_map/ppermute | solution.py:506
  131.1 12.0 %collective-permute-start.42 = (bf16[64,3072]{1,0:T(8,128)(2,1)S(1)}, bf16[64,3072]{1,0:T(8,128)(2,1)S(1)}, u32[]{:S(2)}, u32[]{:S(2)}) collective-permute-start(bf16[64,3072]{1,0:T(8,128)(2,1)S(1)} %add_convert_fusion.3), channel_id=1, source_target_pairs={{0,2},{1,3},{2,0},{3,1},{4,6},{5,7},{6,4},{7,5},{8,10},{9,11},{10,... | collective-permute-start | bytes 1179656 | tf_op jit(solution)/shard_map/ppermute | solution.py:506
  132.8 13.6 %collective-permute-start.38 = (bf16[36,3072]{1,0:T(8,128)(2,1)S(1)}, bf16[36,3072]{1,0:T(8,128)(2,1)S(1)}, u32[]{:S(2)}, u32[]{:S(2)}) collective-permute-start(bf16[36,3072]{1,0:T(8,128)(2,1)S(1)} %pad_maximum_fusion), channel_id=1, source_target_pairs={{0,8},{1,9},{2,10},{3,11},{4,12},{5,13},{6,14},{7,15},{8,0},{9,1},... | collective-permute-start | bytes 663560 | tf_op jit(solution)/shard_map/ppermute | solution.py:506
  134.3 16.4 %collective-permute-start.36 = (bf16[128,1536]{1,0:T(8,128)(2,1)S(1)}, bf16[128,1536]{1,0:T(8,128)(2,1)S(1)}, u32[]{:S(2)}, u32[]{:S(2)}) collective-permute-start(bf16[128,1536]{1,0:T(8,128)(2,1)S(1)} %fusion.6), channel_id=1, source_target_pairs={{0,16},{1,17},{2,18},{3,19},{4,20},{5,21},{6,22},{7,23},{8,24},{9,... | collective-permute-start | bytes 1179656 | tf_op jit(solution)/shard_map/ppermute | solution.py:511
  136.8 14.3 %collective-permute-start.37 = (bf16[128,1536]{1,0:T(8,128)(2,1)S(1)}, bf16[128,1536]{1,0:T(8,128)(2,1)S(1)}, u32[]{:S(2)}, u32[]{:S(2)}) collective-permute-start(bf16[128,1536]{1,0:T(8,128)(2,1)S(1)} %fusion.7), channel_id=1, source_target_pairs={{0,2},{1,3},{2,0},{3,1},{4,6},{5,7},{6,4},{7,5},{8,10},{9,11},{10,... | collective-permute-start | bytes 1179656 | tf_op jit(solution)/shard_map/ppermute | solution.py:511
  137.8 18.1 %collective-permute-start.39 = (bf16[256,3072]{1,0:T(8,128)(2,1)S(1)}, bf16[256,3072]{1,0:T(8,128)(2,1)S(1)}, u32[]{:S(2)}, u32[]{:S(2)}) collective-permute-start(bf16[256,3072]{1,0:T(8,128)(2,1)S(1)} %copy-done.25), channel_id=1, source_target_pairs={{1,0},{0,1},{3,2},{2,3},{5,4},{4,5},{7,6},{6,7},{9,8},{8,9},{11,10... | collective-permute-start | bytes 4718600 | tf_op jit(solution)/shard_map/ppermute | solution.py:506
  146.6 7.5 %collective-permute-start.40 = (bf16[16,3072]{1,0:T(8,128)(2,1)S(1)}, bf16[16,3072]{1,0:T(8,128)(2,1)S(1)}, u32[]{:S(2)}, u32[]{:S(2)}) collective-permute-start(bf16[16,3072]{1,0:T(8,128)(2,1)S(1)} %pad_maximum_fusion.2), channel_id=1, source_target_pairs={{0,2},{1,3},{2,4},{3,5},{4,6},{5,7},{8,10},{9,11},{10,12},{11,13},... | collective-permute-start | bytes 294920 | tf_op jit(solution)/shard_map/ppermute | solution.py:506
  149.4 6.5 %collective-permute-start.41 = (bf16[16,3072]{1,0:T(8,128)(2,1)S(1)}, bf16[16,3072]{1,0:T(8,128)(2,1)S(1)}, u32[]{:S(2)}, u32[]{:S(2)}) collective-permute-start(bf16[16,3072]{1,0:T(8,128)(2,1)S(1)} %pad_maximum_fusion.1), channel_id=1, source_target_pairs={{2,0},{3,1},{4,2},{5,3},{6,4},{7,5},{10,8},{11,9},{12,10},{13,11},... | collective-permute-start | bytes 294920 | tf_op jit(solution)/shard_map/ppermute | solution.py:506
  151.1 1.7 %collective-permute-start.43 = (bf16[64,3072]{1,0:T(8,128)(2,1)S(1)}, bf16[64,3072]{1,0:T(8,128)(2,1)S(1)}, u32[]{:S(2)}, u32[]{:S(2)}) collective-permute-start(bf16[64,3072]{1,0:T(8,128)(2,1)S(1)} %add_convert_fusion.2), channel_id=1, source_target_pairs={{0,1},{1,0},{2,3},{3,2},{4,5},{5,4},{6,7},{7,6},{8,9},{9,8},{10,11... | collective-permute-start | bytes 1179656 | tf_op jit(solution)/shard_map/ppermute | solution.py:506
  (26 other events, 132.1 us)
